TPU v7x, 32 devices: a whole 2x2x4 slice. The times are simulated.
32 devices in a mesh: lvl: 2 (over x), row: 16 (over z, y, core).
Axes of the slice: x: 2, y: 2, z: 4, core: 2. Of those that a mesh axis runs over, the one named last changes fastest.
Arguments:
- rhs: float32 [2, 16, 3, 128, 128], P('lvl', 'row'), may hold values from -6 to 6
- op_tiles: float32 [2, 16, 3, 7, 128, 128], P('lvl', 'row'), may hold values from -1 to 4
- op_cols: int32 [2, 16, 3, 7], P('lvl', 'row'), may hold values from 0 to 8, as said below
- link_tiles: float32 [2, 16, 3, 2, 128, 128], P('lvl', 'row'), may hold values from -0.3125 to 0.3125
- level_links: int32 [2, 16, 3, 2], P('lvl', 'row'), may hold values from 0 to 1, as said below
Outputs:
- levels: float32 [2, 16, 3, 128, 128], P('lvl', 'row')
Inputs may be any that keep to these rules, and one draw needn't show every extreme that they name: `op_cols`: tile 0 of each block row has code 3 + s (the block itself). Fine blocks have 7 distinct codes; every other block names only codes s, 3 + s, 6 + s of its own slot s. `level_links`: entries of blocks that are not fine are 0.
All inputs are finite; a program needn't handle non-finite values.
Results may differ from a plain program's by a relative error of at most 0.00021.
Values sent between devices are 32-bit elements; how exact they have to be, the bound alone decides.
No kernel may reach another device: no remote copies, remote signals or barrier semaphores. Data moves between devices by JAX's collectives and lax.ppermute only.
A program may use at most 64 MiB of HBM per device.

v0:
```python
import jax
import jax.numpy as jnp
from jax import lax
from jax.sharding import PartitionSpec as P

CYCLES = 2


HIGH = lax.Precision.HIGHEST
COEF_ZERO = 0.9
COEF_ONE = -0.36
COEF_TWO = 0.05


def extended(block, sides, width):
    for axis, dim in sides:
        count = lax.axis_size(axis)
        forward = [(i, i + 1) for i in range(count - 1)]
        backward = [(target, source) for source, target in forward]
        low = lax.ppermute(
            lax.slice_in_dim(block, block.shape[dim] - width, None, axis=dim), axis, forward
        )
        high = lax.ppermute(lax.slice_in_dim(block, 0, width, axis=dim), axis, backward)
        block = jnp.concatenate([low, block, high], axis=dim)
    return block


def broadcast(block, axis, source):
    block = jnp.where(lax.axis_index(axis) == source, block, jnp.zeros_like(block))
    return lax.psum(block, axis)


def apply_operator(field, tiles, columns, keep):
    slots = field.shape[0]
    padded = extended(field[None], (("row", 0),), 1)
    candidates = padded.reshape((3 * slots,) + field.shape[1:])
    picked = candidates[columns]
    image = jnp.einsum("sjab,sjbn->san", tiles, picked, precision=HIGH)
    return image * keep[:, None, None]


def per_device(rhs, op_tiles, op_cols, link_tiles, level_links):
    n_lvl = lax.axis_size("lvl")
    fine_lvls = 5 * n_lvl // 8
    mid_lvls = max(n_lvl - fine_lvls - 1, 1)
    lvl_here = lax.axis_index("lvl")
    right = rhs[0, 0]
    tiles = op_tiles[0, 0]
    columns = op_cols[0, 0]
    links = link_tiles[0, 0]
    targets = level_links[0, 0]
    slots = right.shape[0]
    slot_ids = jnp.arange(slots)
    pair_ids = jnp.arange(2)
    is_fine = lvl_here < fine_lvls
    is_mid = (lvl_here >= fine_lvls) & (lvl_here < fine_lvls + mid_lvls)
    is_coarse = lvl_here == n_lvl - 1
    fine_keep = jnp.where(is_fine & (slot_ids >= 0), 1.0, 0.0).astype(jnp.float32)
    mid_keep = jnp.where(is_mid & ((slot_ids == 0) | (slot_ids == 2)), 1.0, 0.0).astype(jnp.float32)
    coarse_keep = jnp.where(is_coarse & (slot_ids == 1), 1.0, 0.0).astype(jnp.float32)
    all_keep = fine_keep + mid_keep + coarse_keep
    mid_flag = jnp.where(is_mid, 1.0, 0.0).astype(jnp.float32)
    place = (slot_ids[:, None] == 2 * pair_ids[None, :]).astype(jnp.float32) * mid_flag
    lvl_ids = jnp.arange(n_lvl)

    def lvl_table(target):
        by_lvl = (target[:, None] // 2 + fine_lvls == lvl_ids[None, :]).astype(jnp.float32)
        by_pair = (target[:, None] % 2 == pair_ids[None, :]).astype(jnp.float32)
        return by_lvl[:, :, None] * by_pair[:, None, :] * fine_keep[:, None, None]

    to_lvl = lvl_table(targets[:, 0])
    from_lvl = lvl_table(targets[:, 1])
    mid_restrict = jnp.stack([links[0, 0], links[2, 0]])
    mid_prolong = jnp.stack([links[0, 1], links[2, 1]])
    solution = jnp.zeros_like(right)
    mid_fix = jnp.zeros((2,) + right.shape[1:], jnp.float32)
    coarse_fix = jnp.zeros_like(right[0])
    for cycle in range(CYCLES):
        if cycle == 0:
            resid = right * fine_keep[:, None, None]
        else:
            resid = (right - apply_operator(solution, tiles, columns, all_keep)) * fine_keep[
                :, None, None
            ]
        terms = jnp.einsum("sab,sbn->san", links[:, 0], resid, precision=HIGH)
        dense = jnp.einsum("slm,san->lman", to_lvl, terms, precision=HIGH)
        mid_resid = lax.psum_scatter(dense, "lvl", scatter_dimension=0, tiled=True)[0] * mid_flag
        mid_part = jnp.einsum("mab,mbn->an", mid_restrict, mid_resid, precision=HIGH) * mid_flag
        fine_part = 0.5 * jnp.sum(terms * fine_keep[:, None, None], axis=0)
        coarse_resid = lax.psum(mid_part + fine_part, "lvl")
        level_resid = resid + jnp.einsum("sm,man->san", place, mid_resid, precision=HIGH)
        level_resid = level_resid + coarse_keep[:, None, None] * coarse_resid[None]
        first = apply_operator(level_resid, tiles, columns, all_keep)
        second = apply_operator(first, tiles, columns, all_keep)
        smooth = COEF_ZERO * level_resid + COEF_ONE * first + COEF_TWO * second
        coarse_fix = broadcast(smooth[1], "lvl", n_lvl - 1)
        mid_fix = jnp.stack([smooth[0], smooth[2]]) + jnp.einsum(
            "mab,bn->man", mid_prolong, coarse_fix, precision=HIGH
        )
        gathered = lax.all_gather(mid_fix[None], "lvl", axis=0, tiled=True)
        chosen = jnp.einsum("slm,lman->san", from_lvl, gathered, precision=HIGH)
        chosen = chosen + coarse_fix[None]
        fine_fix = smooth + jnp.einsum("sab,sbn->san", links[:, 1], chosen, precision=HIGH)
        solution = solution + fine_fix * fine_keep[:, None, None]
    levels = solution * fine_keep[:, None, None] + jnp.einsum(
        "sm,man->san", place, mid_fix, precision=HIGH
    )
    levels = levels + coarse_keep[:, None, None] * coarse_fix[None]
    return levels[None, None]


def solution(mesh):
    placed = (
        P("lvl", "row", None, None, None),
        P("lvl", "row", None, None, None, None),
        P("lvl", "row", None, None),
        P("lvl", "row", None, None, None, None),
        P("lvl", "row", None, None),
    )
    return jax.shard_map(
        per_device,
        mesh=mesh,
        in_specs=placed,
        out_specs=P("lvl", "row", None, None, None),
        check_vma=False,
    )
```

profile of v0, /device:TPU:0, one launch (start us, length us, event | category | flops | bytes accessed | tf_op | source)
XLA Modules:
  0.0 219.7 jit_solution(11737079947139868387)
XLA Ops:
  6.5 1.4 add_bitcast_fusion
  13.1 1.5 slice_bitcast_fusion.7
  14.7 12.0 %reduce-scatter.3.cloned.1.call-done = f32[1,2,128,128]{3,2,1,0:T(8,128)} async-done(((f32[2,2,128,128]{3,2,1,0:T(8,128)}), f32[1,2,128,128]{3,2,1,0:T(8,128)}) %reduce-scatter.3.cloned.1.call-update) | async-done | bytes 131088 | tf_op jit(solution)/shard_map/reduce_scatter | solution.py:87
  26.7 1.8 fusion.78
  30.4 19.4 %all-reduce.5.cloned.1.call-done = f32[128,128]{1,0:T(8,128)} async-done(((f32[128,128]{1,0:T(8,128)}), f32[128,128]{1,0:T(8,128)}) %all-reduce.5.cloned.1.call-update) | async-done | bytes 65552 | tf_op jit(solution)/shard_map/psum | solution.py:90
  52.2 3.0 %collective-permute-start = (f32[1,3,128,128]{2,3,1,0:T(8,128)S(1)}, f32[1,3,128,128]{2,3,1,0:T(8,128)S(1)}, u32[]{:S(2)}, u32[]{:S(2)}) collective-permute-start(f32[1,3,128,128]{2,3,1,0:T(8,128)S(1)} %fusion.139), channel_id=1, source_target_pairs={{0,1},{1,2},{2,3},{3,4},{4,5},{5,6},{6,7},{7,8},{8,9},{9,10},{10,1... | collective-permute-start | bytes 589832 | tf_op jit(solution)/shard_map/ppermute | solution.py:20
  57.0 1.6 fusion.73
  59.9 5.8 %collective-permute-start.2 = (f32[1,3,128,128]{2,3,1,0:T(8,128)S(1)}, f32[1,3,128,128]{2,3,1,0:T(8,128)S(1)}, u32[]{:S(2)}, u32[]{:S(2)}) collective-permute-start(f32[1,3,128,128]{2,3,1,0:T(8,128)S(1)} %bitcast.295), channel_id=1, source_target_pairs={{0,1},{1,2},{2,3},{3,4},{4,5},{5,6},{6,7},{7,8},{8,9},{9,10},{10,1... | collective-permute-start | bytes 589832 | tf_op jit(solution)/shard_map/ppermute | solution.py:20
  67.5 2.6 %fusion.70 = f32[3,128,128]{1,2,0:T(8,128)S(1)} fusion(f32[3,7,128,128]{2,3,1,0:T(8,128)S(1)} %bitcast.285, f32[1,1,3,7,128,128]{5,4,3,2,1,0:T(8,128)S(1)} %copy-done, f32[3,128,128]{2,1,0:T(8,128)} %copy-done.7, f32[3]{0:T(128)S(1)} %add_add_fusion, f32[128,128]{0,1:T(8,128)} %copy-done.15, f32[3]{0:T(128)S(1)} %and_select_fusion.3, ...), kind=kOutput, calls=%fused_computation.45 | convolution fusion | flops 528973824 | bytes 3604508 | tf_op jit(solution)/shard_map/sjab,sjbn->san/dot_general | solution.py:38
  71.5 25.8 %all-reduce.7.cloned.1.call-done = f32[128,128]{0,1:T(8,128)} async-done(((f32[128,128]{0,1:T(8,128)}), f32[128,128]{0,1:T(8,128)}) %all-reduce.7.cloned.1.call-update) | async-done | bytes 65552 | tf_op jit(solution)/shard_map/psum | solution.py:30
  98.6 5.6 %all-gather = f32[4,128,128]{2,1,0:T(8,128)S(1)} all-gather(f32[2,128,128]{2,1,0:T(8,128)S(1)} %copy.37), channel_id=2, replica_groups=mesh['lvl'=2,'row'=16] {'lvl'}, dimensions={0}, use_global_device_ids=true | all-gather | bytes 393216 | tf_op jit(solution)/shard_map/all_gather | solution.py:100
  105.9 1.3 collective-permute-start.5
  107.2 3.0 %collective-permute-start.4 = (f32[1,3,128,128]{2,3,1,0:T(8,128)S(1)}, f32[1,3,128,128]{2,3,1,0:T(8,128)S(1)}, u32[]{:S(2)}, u32[]{:S(2)}) collective-permute-start(f32[1,3,128,128]{2,3,1,0:T(8,128)S(1)} %bitcast.298), channel_id=1, source_target_pairs={{0,1},{1,2},{2,3},{3,4},{4,5},{5,6},{6,7},{7,8},{8,9},{9,10},{10,1... | collective-permute-start | bytes 589832 | tf_op jit(solution)/shard_map/ppermute | solution.py:20
  112.0 1.5 fusion.58
  114.3 1.4 fusion.80
  116.7 15.0 %reduce-scatter.5.cloned.1.call-done = f32[1,2,128,128]{3,2,1,0:T(8,128)} async-done(((f32[2,2,128,128]{3,2,1,0:T(8,128)}), f32[1,2,128,128]{3,2,1,0:T(8,128)}) %reduce-scatter.5.cloned.1.call-update) | async-done | bytes 131088 | tf_op jit(solution)/shard_map/reduce_scatter | solution.py:87
  131.8 1.8 fusion.79
  135.5 19.2 %all-reduce.9.cloned.1.call-done = f32[128,128]{1,0:T(8,128)} async-done(((f32[128,128]{1,0:T(8,128)}), f32[128,128]{1,0:T(8,128)}) %all-reduce.9.cloned.1.call-update) | async-done | bytes 65552 | tf_op jit(solution)/shard_map/psum | solution.py:90
  157.0 3.0 %collective-permute-start.6 = (f32[1,3,128,128]{2,3,1,0:T(8,128)S(1)}, f32[1,3,128,128]{2,3,1,0:T(8,128)S(1)}, u32[]{:S(2)}, u32[]{:S(2)}) collective-permute-start(f32[1,3,128,128]{2,3,1,0:T(8,128)S(1)} %fusion.138), channel_id=1, source_target_pairs={{0,1},{1,2},{2,3},{3,4},{4,5},{5,6},{6,7},{7,8},{8,9},{9,10},{10,1... | collective-permute-start | bytes 589832 | tf_op jit(solution)/shard_map/ppermute | solution.py:20
  161.8 1.6 fusion.46
  164.6 5.8 %collective-permute-start.8 = (f32[1,3,128,128]{2,3,1,0:T(8,128)S(1)}, f32[1,3,128,128]{2,3,1,0:T(8,128)S(1)}, u32[]{:S(2)}, u32[]{:S(2)}) collective-permute-start(f32[1,3,128,128]{2,3,1,0:T(8,128)S(1)} %bitcast.301), channel_id=1, source_target_pairs={{0,1},{1,2},{2,3},{3,4},{4,5},{5,6},{6,7},{7,8},{8,9},{9,10},{10,1... | collective-permute-start | bytes 589832 | tf_op jit(solution)/shard_map/ppermute | solution.py:20
  172.5 2.6 %fusion.43 = f32[3,128,128]{1,2,0:T(8,128)S(1)} fusion(f32[3,7,128,128]{2,3,1,0:T(8,128)S(1)} %bitcast.284, f32[1,1,3,7,128,128]{5,4,3,2,1,0:T(8,128)S(1)} %copy-done, f32[3,128,128]{2,1,0:T(8,128)} %copy-done.11, f32[3]{0:T(128)S(1)} %add_add_fusion, f32[128,128]{0,1:T(8,128)} %copy-done.16, f32[3]{0:T(128)S(1)} %and_select_fusion.3, ...), kind=kOutput, calls=%fused_computation.36 | convolution fusion | flops 528924672 | bytes 3604504 | tf_op jit(solution)/shard_map/sjab,sjbn->san/dot_general | solution.py:38
  175.9 26.5 %all-reduce.11.cloned.1.call-done = f32[128,128]{0,1:T(8,128)} async-done(((f32[128,128]{0,1:T(8,128)}), f32[128,128]{0,1:T(8,128)}) %all-reduce.11.cloned.1.call-update) | async-done | bytes 65552 | tf_op jit(solution)/shard_map/psum | solution.py:30
  204.7 5.6 %all-gather.1 = f32[4,128,128]{2,1,0:T(8,128)S(1)} all-gather(f32[2,128,128]{2,1,0:T(8,128)S(1)} %copy.46), channel_id=3, replica_groups=mesh['lvl'=2,'row'=16] {'lvl'}, dimensions={0}, use_global_device_ids=true | all-gather | bytes 393216 | tf_op jit(solution)/shard_map/all_gather | solution.py:100
  (154 shorter events, 36.2 us)
Async XLA Ops:
  6.5 50.4 %copy-start = (f32[1,1,3,7,128,128]{5,4,3,2,1,0:T(8,128)S(1)}, f32[1,1,3,7,128,128]{5,4,3,2,1,0:T(8,128)}, u32[]{:S(2)}) copy-start(f32[1,1,3,7,128,128]{5,4,3,2,1,0:T(8,128)} %param.6) | copy-start | bytes 4128772
  6.5 20.2 %reduce-scatter.3.cloned.1.call-start = ((), (), s32[]{:S(2)}) async-start(), calls=%async_computation.2 | async-start | bytes 393216 | tf_op jit(solution)/shard_map/reduce_scatter | solution.py:87
  12.2 37.6 %all-reduce.5.cloned.1.call-start = ((), (), s32[]{:S(2)}) async-start(), calls=%async_computation.3 | async-start | bytes 131072 | tf_op jit(solution)/shard_map/psum | solution.py:90
  12.3 38.6 %copy-start.30 = (s32[2]{0:T(128)}, s32[2]{0:T(128)S(1)}, u32[]{:S(2)}) copy-start(s32[2]{0:T(128)S(1)} %iota_multiply_fusion) | copy-start | bytes 28
  28.5 68.7 %all-reduce.7.cloned.1.call-start = ((), (), s32[]{:S(2)}) async-start(), calls=%async_computation.4 | async-start | bytes 131072 | tf_op jit(solution)/shard_map/psum | solution.py:30
  50.9 4.4 %collective-permute-start.1 = (f32[1,3,128,128]{2,3,1,0:T(8,128)S(1)}, f32[1,3,128,128]{2,3,1,0:T(8,128)S(1)}, u32[]{:S(2)}, u32[]{:S(2)}) collective-permute-start(f32[1,3,128,128]{2,3,1,0:T(8,128)S(1)} %fusion.139), channel_id=1, source_target_pairs={{1,0},{2,1},{3,2},{4,3},{5,4},{6,5},{7,6},{8,7},{9,8},{10,9},{11,1... | collective-permute-start | bytes 589832 | tf_op jit(solution)/shard_map/ppermute | solution.py:23
  52.2 4.1 %collective-permute-start = (f32[1,3,128,128]{2,3,1,0:T(8,128)S(1)}, f32[1,3,128,128]{2,3,1,0:T(8,128)S(1)}, u32[]{:S(2)}, u32[]{:S(2)}) collective-permute-start(f32[1,3,128,128]{2,3,1,0:T(8,128)S(1)} %fusion.139), channel_id=1, source_target_pairs={{0,1},{1,2},{2,3},{3,4},{4,5},{5,6},{6,7},{7,8},{8,9},{9,10},{10,1... | collective-permute-start | bytes 589832 | tf_op jit(solution)/shard_map/ppermute | solution.py:20
  58.6 7.8 %collective-permute-start.3 = (f32[1,3,128,128]{2,3,1,0:T(8,128)S(1)}, f32[1,3,128,128]{2,3,1,0:T(8,128)S(1)}, u32[]{:S(2)}, u32[]{:S(2)}) collective-permute-start(f32[1,3,128,128]{2,3,1,0:T(8,128)S(1)} %bitcast.294), channel_id=1, source_target_pairs={{1,0},{2,1},{3,2},{4,3},{5,4},{6,5},{7,6},{8,7},{9,8},{10,9},{11,1... | collective-permute-start | bytes 589832 | tf_op jit(solution)/shard_map/ppermute | solution.py:23
  59.9 6.9 %collective-permute-start.2 = (f32[1,3,128,128]{2,3,1,0:T(8,128)S(1)}, f32[1,3,128,128]{2,3,1,0:T(8,128)S(1)}, u32[]{:S(2)}, u32[]{:S(2)}) collective-permute-start(f32[1,3,128,128]{2,3,1,0:T(8,128)S(1)} %bitcast.295), channel_id=1, source_target_pairs={{0,1},{1,2},{2,3},{3,4},{4,5},{5,6},{6,7},{7,8},{8,9},{9,10},{10,1... | collective-permute-start | bytes 589832 | tf_op jit(solution)/shard_map/ppermute | solution.py:20
  70.1 35.3 %copy-start.2 = (f32[1,1,3,2,128,128]{5,4,2,3,1,0:T(8,128)S(1)}, f32[1,1,3,2,128,128]{5,4,2,3,1,0:T(8,128)}, u32[]{:S(2)}) copy-start(f32[1,1,3,2,128,128]{5,4,2,3,1,0:T(8,128)} %copy-done.1) | copy-start | bytes 1179652
  70.7 61.0 %reduce-scatter.5.cloned.1.call-start = ((), (), s32[]{:S(2)}) async-start(), calls=%async_computation.5 | async-start | bytes 393216 | tf_op jit(solution)/shard_map/reduce_scatter | solution.py:87
  71.5 32.8 %copy-start.26 = (f32[3,2]{0,1:T(2,128)}, f32[3,2]{0,1:T(2,128)S(1)}, u32[]{:S(2)}) copy-start(f32[3,2]{0,1:T(2,128)S(1)} %get-tuple-element.27) | copy-start | bytes 76
  71.5 32.8 %copy-start.28 = (f32[3,2]{0,1:T(2,128)}, f32[3,2]{0,1:T(2,128)S(1)}, u32[]{:S(2)}) copy-start(f32[3,2]{0,1:T(2,128)S(1)} %get-tuple-element.28) | copy-start | bytes 76
  105.9 4.4 %collective-permute-start.5 = (f32[1,3,128,128]{2,3,1,0:T(8,128)S(1)}, f32[1,3,128,128]{2,3,1,0:T(8,128)S(1)}, u32[]{:S(2)}, u32[]{:S(2)}) collective-permute-start(f32[1,3,128,128]{2,3,1,0:T(8,128)S(1)} %bitcast.297), channel_id=1, source_target_pairs={{1,0},{2,1},{3,2},{4,3},{5,4},{6,5},{7,6},{8,7},{9,8},{10,9},{11,1... | collective-permute-start | bytes 589832 | tf_op jit(solution)/shard_map/ppermute | solution.py:23
  107.2 4.1 %collective-permute-start.4 = (f32[1,3,128,128]{2,3,1,0:T(8,128)S(1)}, f32[1,3,128,128]{2,3,1,0:T(8,128)S(1)}, u32[]{:S(2)}, u32[]{:S(2)}) collective-permute-start(f32[1,3,128,128]{2,3,1,0:T(8,128)S(1)} %bitcast.298), channel_id=1, source_target_pairs={{0,1},{1,2},{2,3},{3,4},{4,5},{5,6},{6,7},{7,8},{8,9},{9,10},{10,1... | collective-permute-start | bytes 589832 | tf_op jit(solution)/shard_map/ppermute | solution.py:20
  113.5 42.0 %copy-start.5 = (f32[3,128,128]{1,2,0:T(8,128)}, f32[3,128,128]{1,2,0:T(8,128)S(1)}, u32[]{:S(2)}) copy-start(f32[3,128,128]{1,2,0:T(8,128)S(1)} %fusion.58) | copy-start | bytes 589828
  116.4 38.2 %all-reduce.9.cloned.1.call-start = ((), (), s32[]{:S(2)}) async-start(), calls=%async_computation.6 | async-start | bytes 131072 | tf_op jit(solution)/shard_map/psum | solution.py:90
  133.6 68.8 %all-reduce.11.cloned.1.call-start = ((), (), s32[]{:S(2)}) async-start(), calls=%async_computation.7 | async-start | bytes 131072 | tf_op jit(solution)/shard_map/psum | solution.py:30
  155.7 4.4 %collective-permute-start.7 = (f32[1,3,128,128]{2,3,1,0:T(8,128)S(1)}, f32[1,3,128,128]{2,3,1,0:T(8,128)S(1)}, u32[]{:S(2)}, u32[]{:S(2)}) collective-permute-start(f32[1,3,128,128]{2,3,1,0:T(8,128)S(1)} %fusion.138), channel_id=1, source_target_pairs={{1,0},{2,1},{3,2},{4,3},{5,4},{6,5},{7,6},{8,7},{9,8},{10,9},{11,1... | collective-permute-start | bytes 589832 | tf_op jit(solution)/shard_map/ppermute | solution.py:23
  157.0 4.1 %collective-permute-start.6 = (f32[1,3,128,128]{2,3,1,0:T(8,128)S(1)}, f32[1,3,128,128]{2,3,1,0:T(8,128)S(1)}, u32[]{:S(2)}, u32[]{:S(2)}) collective-permute-start(f32[1,3,128,128]{2,3,1,0:T(8,128)S(1)} %fusion.138), channel_id=1, source_target_pairs={{0,1},{1,2},{2,3},{3,4},{4,5},{5,6},{6,7},{7,8},{8,9},{9,10},{10,1... | collective-permute-start | bytes 589832 | tf_op jit(solution)/shard_map/ppermute | solution.py:20
  163.3 7.2 %collective-permute-start.9 = (f32[1,3,128,128]{2,3,1,0:T(8,128)S(1)}, f32[1,3,128,128]{2,3,1,0:T(8,128)S(1)}, u32[]{:S(2)}, u32[]{:S(2)}) collective-permute-start(f32[1,3,128,128]{2,3,1,0:T(8,128)S(1)} %bitcast.300), channel_id=1, source_target_pairs={{1,0},{2,1},{3,2},{4,3},{5,4},{6,5},{7,6},{8,7},{9,8},{10,9},{11,1... | collective-permute-start | bytes 589832 | tf_op jit(solution)/shard_map/ppermute | solution.py:23
  164.6 6.9 %collective-permute-start.8 = (f32[1,3,128,128]{2,3,1,0:T(8,128)S(1)}, f32[1,3,128,128]{2,3,1,0:T(8,128)S(1)}, u32[]{:S(2)}, u32[]{:S(2)}) collective-permute-start(f32[1,3,128,128]{2,3,1,0:T(8,128)S(1)} %bitcast.301), channel_id=1, source_target_pairs={{0,1},{1,2},{2,3},{3,4},{4,5},{5,6},{6,7},{7,8},{8,9},{9,10},{10,1... | collective-permute-start | bytes 589832 | tf_op jit(solution)/shard_map/ppermute | solution.py:20
  175.2 35.2 %copy-start.27 = (f32[3,2]{0,1:T(2,128)S(1)}, f32[3,2]{0,1:T(2,128)}, u32[]{:S(2)}) copy-start(f32[3,2]{0,1:T(2,128)} %copy-done.26) | copy-start | bytes 76
  175.2 35.2 %copy-start.29 = (f32[3,2]{0,1:T(2,128)S(1)}, f32[3,2]{0,1:T(2,128)}, u32[]{:S(2)}) copy-start(f32[3,2]{0,1:T(2,128)} %copy-done.28) | copy-start | bytes 76
  (27 other events, 359.0 us)
Sparse Core Ops, SparseCore 0:
  12.3 14.3 reduce-scatter.2
  29.0 20.7 all-reduce.4
  70.9 26.3 all-reduce.6
  116.5 15.1 reduce-scatter.4
  133.8 20.7 all-reduce.8
  176.0 26.3 all-reduce.10
where the time goes:
time: 221 us; the launch traced here: 220 us
  waiting for transfers between devices  123 us (56%)
  starting transfers between devices  27.7 us (13%)
  matrix products  24.2 us (11%)
  between operations  14.3 us (6%)
  local copies, waits for them, and re-layouts  13.4 us (6%)
  blocking collectives  11.3 us (5%)
  other arithmetic  6.2 us (3%)
    psum x2, waiting for transfers between devices, broadcast(): return lax.psum(block, axis)  52.3 us
    psum x2, waiting for transfers between devices, per_device(): coarse_resid = lax.psum(mid_part + fine_part, 'lvl')  38.6 us
    reduce_scatter x2, waiting for transfers between devices, per_device(): lax.psum_scatter(dense, 'lvl', scatter_dimension=0, tiled=True)[0]  27.1 us
    ppermute x5, starting transfers between devices, extended(): lax.ppermute(lax.slice_in_dim(block, block.shape[dim] - width, None, axis...  20.8 us
    all_gather x2, blocking collectives, per_device(): gathered = lax.all_gather(mid_fix[None], 'lvl', axis=0, tiled=True)  11.3 us
    dot_general x5, matrix products, apply_operator(): image = jnp.einsum('sjab,sjbn->san', tiles, picked, precision=HIGH)  9.85 us
    ppermute x5, starting transfers between devices, extended(): lax.ppermute(lax.slice_in_dim(block, 0, width, axis=dim), axis, backward)  6.46 us
    ppermute x5, waiting for transfers between devices, extended(): lax.ppermute(lax.slice_in_dim(block, block.shape[dim] - width, None, axis...  4.5 us
  transfers between devices with their start and end apart: 16, of which 11 were waited for; matrix products, arithmetic and copies ran while one was open for 3% of the time, Pallas kernels for 0%

commit v1 on v0

--- a/solution.py
+++ b/solution.py
@@ -1,6 +1,10 @@
+import functools
+
 import jax
 import jax.numpy as jnp
 from jax import lax
+from jax.experimental import pallas as pl
+from jax.experimental.pallas import tpu as pltpu
 from jax.sharding import PartitionSpec as P
 
 CYCLES = 2
@@ -10,6 +14,8 @@
 COEF_ZERO = 0.9
 COEF_ONE = -0.36
 COEF_TWO = 0.05
+F32 = jnp.float32
+BF16 = jnp.bfloat16
 
 
 def extended(block, sides, width):
@@ -109,6 +115,250 @@
     return levels[None, None]
 
 
+def split(value):
+    high = value.astype(BF16)
+    return high, (value - high.astype(F32)).astype(BF16)
+
+
+def split_rows(value):
+    return jnp.concatenate(split(value), axis=0)
+
+
+def split_columns(value):
+    return jnp.concatenate(split(value), axis=1)
+
+
+def product(left, right):
+    full = jnp.dot(left, right, preferred_element_type=F32)
+    rows, columns = full.shape[0] // 2, full.shape[1] // 2
+    small = full[rows:, :columns] + full[:rows, columns:] + full[rows:, columns:]
+    return full[:rows, :columns] + small
+
+
+def stacked(*blocks):
+    return jnp.concatenate(blocks, axis=0)
+
+
+def restrict_kernel(targets, rhs, links, mids, payload, restrict, prolong):
+    size = rhs.shape[-1]
+    slots = rhs.shape[0]
+
+    @pl.when(lax.axis_index("lvl") == 0)
+    def _():
+        payload[...] = rhs[...]
+        for s in range(slots):
+            for k in range(2):
+                down = jnp.where(targets[s, 0] == k, links[s, 0], 0.0)
+                high, low = split(down)
+                restrict[k * size:(k + 1) * size, s * size:(s + 1) * size] = high
+                restrict[(2 + k) * size:(3 + k) * size, s * size:(s + 1) * size] = low
+                up = jnp.where(targets[s, 1] == k, links[s, 1], 0.0)
+                high, low = split(up)
+                prolong[s * size:(s + 1) * size, k * size:(k + 1) * size] = high
+                prolong[(slots + s) * size:(slots + s + 1) * size, k * size:(k + 1) * size] = low
+        right = split_columns(rhs[...].reshape(slots * size, size))
+        mids[...] = product(restrict[...], right).reshape(mids.shape)
+
+    @pl.when(lax.axis_index("lvl") != 0)
+    def _():
+        payload[0] = links[0, 0]
+        payload[1] = links[2, 0]
+        payload[2] = jnp.zeros_like(payload[2])
+        mids[...] = jnp.zeros_like(mids)
+
+
+def operator_kernel(columns, tiles, matrix, gathered):
+    slots, count, size = tiles.shape[0], tiles.shape[1], tiles.shape[-1]
+    row = lax.axis_index("row")
+    odd = lax.rem(row, 2)
+    inner = (row > 0) & (row < lax.axis_size("row") - 1)
+    gathered[...] = jnp.zeros_like(gathered)
+    for s in range(slots):
+        for j in range(count):
+            code = columns[s, j]
+            step = code // slots
+            slot = code - slots * step
+            side = jnp.where(step == 1, 0, jnp.where(step == 2 * (1 - odd), 1, 2))
+            gathered[s, side * slots + slot] += tiles[s, j]
+    for s in range(slots):
+        for c in range(3 * slots):
+            block = gathered[s, c]
+            if c >= 2 * slots:
+                block = jnp.where(inner, block, 0.0)
+            high, low = split(block)
+            matrix[s * size:(s + 1) * size, c * size:(c + 1) * size] = high
+            matrix[(slots + s) * size:(slots + s + 1) * size, c * size:(c + 1) * size] = low
+
+
+def load(field, refs):
+    size = field.shape[0] // (len(refs) * refs[0].shape[0])
+    for g, ref in enumerate(refs):
+        for s in range(ref.shape[0]):
+            high, low = split(ref[s])
+            at = (g * ref.shape[0] + s) * size
+            field[at:at + size, :size] = high
+            field[at:at + size, size:] = low
+
+
+def first_kernel(matrix, own, core, cross, down_own, down_core, down_cross, mid_own, mid_core, mid_cross, level, first, field):
+    size = own.shape[-1]
+
+    @pl.when(lax.axis_index("lvl") == 0)
+    def _():
+        load(field, (own, core, cross))
+        level[...] = own[...]
+
+    @pl.when(lax.axis_index("lvl") != 0)
+    def _():
+        for g, (down, mid) in enumerate(((down_own, mid_own), (down_core, mid_core), (down_cross, mid_cross))):
+            left = split_rows(jnp.concatenate([down[0], down[1]], axis=1))
+            right = split_columns(stacked(mid[0], mid[1]))
+            coarse = product(left, right) + 0.5 * (mid[0] + mid[1])
+            for s, value in enumerate((mid[0], coarse, mid[1])):
+                high, low = split(value)
+                at = (3 * g + s) * size
+                field[at:at + size, :size] = high
+                field[at:at + size, size:] = low
+                if g == 0:
+                    level[s] = value
+
+    first[...] = product(matrix[...], field[...]).reshape(first.shape)
+
+
+def second_kernel(matrix, level, own, core, cross, links, smooth, fixes, field):
+    load(field, (own, core, cross))
+    second = product(matrix[...], field[...]).reshape(level.shape)
+    value = COEF_ZERO * level[...] + COEF_ONE * own[...] + COEF_TWO * second
+
+    @pl.when(lax.axis_index("lvl") == 0)
+    def _():
+        smooth[...] = value
+        fixes[...] = jnp.zeros_like(fixes)
+
+    @pl.when(lax.axis_index("lvl") != 0)
+    def _():
+        coarse = value[1]
+        up = product(split_rows(stacked(links[0, 1], links[2, 1])), split_columns(coarse))
+        size = coarse.shape[0]
+        low, high = value[0] + up[:size], value[2] + up[size:]
+        smooth[0] = low
+        smooth[1] = coarse
+        smooth[2] = high
+        fixes[0] = low + coarse
+        fixes[1] = high + coarse
+
+
+def solution_kernel(smooth, fixes, prolong, *rest):
+    result = rest[-1]
+
+    @pl.when(lax.axis_index("lvl") == 0)
+    def _():
+        right = split_columns(stacked(fixes[0], fixes[1]))
+        value = smooth[...] + product(prolong[...], right).reshape(smooth.shape)
+        if len(rest) == 2:
+            value = value + rest[0][...]
+        result[...] = value
+
+    @pl.when(lax.axis_index("lvl") != 0)
+    def _():
+        result[...] = smooth[...]
+
+
+def residual_kernel(matrix, own, core, cross, rhs, restrict, resid, mids, field):
+    @pl.when(lax.axis_index("lvl") == 0)
+    def _():
+        load(field, (own, core, cross))
+        value = rhs[...] - product(matrix[...], field[...]).reshape(rhs.shape)
+        resid[...] = value
+        right = split_columns(value.reshape(-1, value.shape[-1]))
+        mids[...] = product(restrict[...], right).reshape(mids.shape)
+
+    @pl.when(lax.axis_index("lvl") != 0)
+    def _():
+        resid[...] = jnp.zeros_like(resid)
+        mids[...] = jnp.zeros_like(mids)
+
+
+def call(kernel, outs, args, scalars=0, scratch=(), flops=0):
+    spaces = [pl.BlockSpec(memory_space=pltpu.SMEM)] * scalars
+    spaces += [pl.BlockSpec(memory_space=pltpu.VMEM)] * (len(args) - scalars)
+    size = sum(a.size * a.dtype.itemsize for a in args)
+    return pl.pallas_call(
+        kernel,
+        out_shape=[jax.ShapeDtypeStruct(shape, dtype) for shape, dtype in outs],
+        in_specs=spaces,
+        out_specs=[pl.BlockSpec(memory_space=pltpu.VMEM)] * len(outs),
+        scratch_shapes=[pltpu.VMEM(shape, dtype) for shape, dtype in scratch],
+        compiler_params=pltpu.CompilerParams(vmem_limit_bytes=24 * 1024 * 1024),
+        cost_estimate=pl.CostEstimate(flops=flops, bytes_accessed=size, transcendentals=0),
+    )(*args)
+
+
+def swaps(rows):
+    across = [0] + [r + 1 if r % 2 else r - 1 for r in range(1, rows - 1)] + [rows - 1]
+    core = [(l * rows + r, l * rows + (r ^ 1)) for l in range(2) for r in range(rows)]
+    cross = [(l * rows + r, l * rows + across[r]) for l in range(2) for r in range(1, rows - 1)]
+    cross += [(l * rows + r, (1 - l) * rows + r) for l in range(2) for r in (0, rows - 1)]
+    level = [(l * rows + r, (1 - l) * rows + r) for l in range(2) for r in range(rows)]
+    skew = [(r, rows + across[r]) for r in range(rows)] + [(rows + r, r) for r in range(rows)]
+    return tuple((lambda x, pairs=pairs: lax.ppermute(x, ("lvl", "row"), pairs)) for pairs in (core, cross, level, skew))
+
+
+def paired(rhs, op_tiles, op_cols, link_tiles, level_links):
+    core, cross, level, skew = swaps(lax.axis_size("row"))
+    right, tiles, columns = rhs[0, 0], op_tiles[0, 0], op_cols[0, 0]
+    links, targets = link_tiles[0, 0], level_links[0, 0]
+    slots, size, width = right.shape
+    blocks, pair = (right.shape, F32), ((2, size, width), F32)
+    big, field = slots * size, ((3 * slots * size, 2 * width), BF16)
+    mids, payload, restrict, prolong = call(
+        restrict_kernel,
+        [pair, blocks, ((4 * size, big), BF16), ((2 * big, 2 * size), BF16)],
+        [targets, right, links],
+        scalars=1,
+    )
+    down = None
+    result = None
+    matrix = None
+    for cycle in range(CYCLES):
+        if cycle > 0:
+            resid, mids = call(
+                residual_kernel,
+                [blocks, pair],
+                [matrix, result, core(result), cross(result), right, restrict],
+                scratch=[field],
+            )
+            payload = resid
+        mid_here, mid_cross = level(mids), skew(mids)
+        around = (payload, core(payload), cross(payload))
+        mid_core = core(mid_here)
+        if cycle == 0:
+            (matrix,) = call(
+                operator_kernel,
+                [((2 * big, 3 * big), BF16)],
+                [columns, tiles],
+                scalars=1,
+                scratch=[((slots, 3 * slots, size, size), F32)],
+            )
+            down = around
+        level_resid, first = call(
+            first_kernel,
+            [blocks, blocks],
+            [matrix, *around, *down, mid_here, mid_core, mid_cross],
+            scratch=[field],
+        )
+        smooth, fixes = call(
+            second_kernel,
+            [blocks, pair],
+            [matrix, level_resid, first, core(first), cross(first), links],
+            scratch=[field],
+        )
+        fixes = level(fixes)
+        args = [smooth, fixes, prolong] + ([] if cycle == 0 else [result])
+        (result,) = call(solution_kernel, [blocks], args)
+    return result[None, None]
+
+
 def solution(mesh):
     placed = (
         P("lvl", "row", None, None, None),
@@ -117,8 +367,9 @@
         P("lvl", "row", None, None, None, None),
         P("lvl", "row", None, None),
     )
+    pairs = mesh.shape["lvl"] == 2 and mesh.shape["row"] % 2 == 0
     return jax.shard_map(
-        per_device,
+        paired if pairs else per_device,
         mesh=mesh,
         in_specs=placed,
         out_specs=P("lvl", "row", None, None, None),

time: 221 us -> 59.8 us (0.27)
  waiting for transfers between devices: 123 us -> 26.5 us
  matrix products: 24.2 us -> 0 us
  between operations: 14.3 us -> 0.1 us
  blocking collectives: 11.3 us -> 0 us
  local copies, waits for them, and re-layouts: 13.4 us -> 4.72 us
  Pallas kernels: 0 us -> 7.64 us
  starting transfers between devices: 27.7 us -> 20.6 us
  other arithmetic: 6.2 us -> 0 us
    psum x4 -> x0, waiting for transfers between devices: 90.9 us -> none  [the longest x2 52.3 us: broadcast(): return lax.psum(block, axis)]
    reduce_scatter x2 -> x0, waiting for transfers between devices: 27.1 us -> none  [per_device(): lax.psum_scatter(dense, 'lvl', scatter_dimension=0, tiled=True)[0]]
    dot_general x20 -> x0, matrix products: 24.2 us -> none  [the longest x5 9.85 us: apply_operator(): image = jnp.einsum('sjab,sjbn->san', tiles, picked, precision=HIGH)]
    ppermute x10 -> x18, waiting for transfers between devices: 4.51 us -> 26.5 us  [swaps(): lax.ppermute(x, ('lvl', 'row'), pairs)]
    all_gather x2 -> x0, blocking collectives: 11.3 us -> none  [per_device(): gathered = lax.all_gather(mid_fix[None], 'lvl', axis=0, tiled=True)]
    pallas_call x0 -> x9, Pallas kernels: none -> 7.64 us  [call(): pl.pallas_call(kernel, out_shape=[jax.ShapeDtypeStruct(shape, dtype) for...]
    ppermute x10 -> x18, starting transfers between devices: 27.3 us -> 20.6 us  [swaps(): lax.ppermute(x, ('lvl', 'row'), pairs)]
    gather x5 -> x0, local copies, waits for them, and re-layouts: 3.18 us -> none  [apply_operator(): picked = candidates[columns]]
  transfers between devices with their start and end apart: 16 -> 18, of which waited for: 11 -> 9; matrix products, arithmetic and copies ran while one was open for 3% -> 1% of each run, Pallas kernels for 0% -> 2%
where the time goes in v1:
time: 59.8 us; the launch traced here: 59.5 us
  waiting for transfers between devices  26.5 us (44%)
  starting transfers between devices  20.6 us (34%)
  Pallas kernels  7.64 us (13%)
  local copies, waits for them, and re-layouts  4.72 us (8%)
    ppermute x18, waiting for transfers between devices, swaps(): lax.ppermute(x, ('lvl', 'row'), pairs)  26.5 us
    ppermute x18, starting transfers between devices, swaps(): lax.ppermute(x, ('lvl', 'row'), pairs)  20.6 us
    pallas_call x9, Pallas kernels, call(): pl.pallas_call(kernel, out_shape=[jax.ShapeDtypeStruct(shape, dtype) for...  7.64 us
    unnamed x11, local copies, waits for them, and re-layouts  3.95 us
  transfers between devices with their start and end apart: 18, of which 9 were waited for; matrix products, arithmetic and copies ran while one was open for 1% of the time, Pallas kernels for 2%

profile of v1, /device:TPU:0, one launch (start us, length us, event | category | flops | bytes accessed | tf_op | source)
XLA Modules:
  0.0 59.5 jit_solution(14853547971645965127)
XLA Ops:
  0.8 1.0 %copy-done = f32[1,1,3,2,128,128]{5,4,3,2,1,0:T(8,128)S(1)} copy-done((f32[1,1,3,2,128,128]{5,4,3,2,1,0:T(8,128)S(1)}, f32[1,1,3,2,128,128]{5,4,3,2,1,0:T(8,128)}, u32[]{:S(2)}) %copy-start) | copy-done | bytes 393240
  2.7 1.0 %shard_map.56 = (f32[2,128,128]{2,1,0:T(8,128)S(1)}, f32[3,128,128]{2,1,0:T(8,128)S(1)}, bf16[512,384]{1,0:T(8,128)(2,1)S(1)}, bf16[768,256]{1,0:T(8,128)(2,1)S(1)}) custom-call(s32[3,2]{1,0:T(4,128)S(1)} %copy.6.targets, f32[3,128,128]{2,1,0:T(8,128)S(1)} %bitcast.12, f32[3,2,128,128]{3,2,1,0:T(8,128)S(1)} %bitcast.8), custom_call_target="tpu_custom_call" | custom-call | bytes 589848 | tf_op jit(solution)/shard_map/pallas_call | solution.py:286
  3.7 2.6 %collective-permute-start.2 = (f32[2,128,128]{2,1,0:T(8,128)S(1)}, f32[2,128,128]{2,1,0:T(8,128)S(1)}, u32[]{:S(2)}, u32[]{:S(2)}) collective-permute-start(f32[2,128,128]{2,1,0:T(8,128)S(1)} %get-tuple-element.20), channel_id=1, source_target_pairs={{0,16},{1,17},{2,18},{3,19},{4,20},{5,21},{6,22},{7,23},{8,24},{9,... | collective-permute-start | bytes 393224 | tf_op jit(solution)/shard_map/ppermute | solution.py:304
  6.4 1.6 %collective-permute-start = (f32[3,128,128]{2,1,0:T(8,128)S(1)}, f32[3,128,128]{2,1,0:T(8,128)S(1)}, u32[]{:S(2)}, u32[]{:S(2)}) collective-permute-start(f32[3,128,128]{2,1,0:T(8,128)S(1)} %get-tuple-element.19.own.down_own), channel_id=1, source_target_pairs={{0,1},{1,0},{2,3},{3,2},{4,5},{5,4},{6,7},{7,6},{8,9},{9,8},{10,11... | collective-permute-start | bytes 589832 | tf_op jit(solution)/shard_map/ppermute | solution.py:304
  8.8 1.0 %collective-permute-done.2.mid_own = f32[2,128,128]{2,1,0:T(8,128)S(1)} collective-permute-done((f32[2,128,128]{2,1,0:T(8,128)S(1)}, f32[2,128,128]{2,1,0:T(8,128)S(1)}, u32[]{:S(2)}, u32[]{:S(2)}) %collective-permute-start.2) | collective-permute-done | bytes 131104 | tf_op jit(solution)/shard_map/ppermute | solution.py:304
  10.6 1.3 %copy-done.2 = f32[1,1,3,7,128,128]{5,4,3,2,1,0:T(8,128)S(1)} copy-done((f32[1,1,3,7,128,128]{5,4,3,2,1,0:T(8,128)S(1)}, f32[1,1,3,7,128,128]{5,4,3,2,1,0:T(8,128)}, u32[]{:S(2)}) %copy-start.2) | copy-done | bytes 1376280
  11.9 1.2 %shard_map.55.matrix = bf16[768,1152]{1,0:T(8,128)(2,1)S(1)} custom-call(s32[3,7]{1,0:T(4,128)S(1)} %bitcast.14, f32[3,7,128,128]{3,2,1,0:T(8,128)S(1)} %bitcast.11), custom_call_target="tpu_custom_call" | custom-call | bytes 1376340 | tf_op jit(solution)/shard_map/pallas_call | solution.py:286
  13.1 2.3 %collective-permute-done.4.mid_cross = f32[2,128,128]{2,1,0:T(8,128)S(1)} collective-permute-done((f32[2,128,128]{2,1,0:T(8,128)S(1)}, f32[2,128,128]{2,1,0:T(8,128)S(1)}, u32[]{:S(2)}, u32[]{:S(2)}) %collective-permute-start.4) | collective-permute-done | bytes 131104 | tf_op jit(solution)/shard_map/ppermute | solution.py:304
  16.2 2.8 %collective-permute-start.6 = (f32[3,128,128]{2,1,0:T(8,128)S(1)}, f32[3,128,128]{2,1,0:T(8,128)S(1)}, u32[]{:S(2)}, u32[]{:S(2)}) collective-permute-start(f32[3,128,128]{2,1,0:T(8,128)S(1)} %get-tuple-element.22.own), channel_id=1, source_target_pairs={{1,2},{2,1},{3,4},{4,3},{5,6},{6,5},{7,8},{8,7},{9,10},{10,9},{11,... | collective-permute-start | bytes 589832 | tf_op jit(solution)/shard_map/ppermute | solution.py:304
  19.0 3.6 %collective-permute-done.6.cross = f32[3,128,128]{2,1,0:T(8,128)S(1)} collective-permute-done((f32[3,128,128]{2,1,0:T(8,128)S(1)}, f32[3,128,128]{2,1,0:T(8,128)S(1)}, u32[]{:S(2)}, u32[]{:S(2)}) %collective-permute-start.6) | collective-permute-done | bytes 196640 | tf_op jit(solution)/shard_map/ppermute | solution.py:304
  23.4 2.3 %collective-permute-start.7 = (f32[2,128,128]{2,1,0:T(8,128)S(1)}, f32[2,128,128]{2,1,0:T(8,128)S(1)}, u32[]{:S(2)}, u32[]{:S(2)}) collective-permute-start(f32[2,128,128]{2,1,0:T(8,128)S(1)} %get-tuple-element.24), channel_id=1, source_target_pairs={{0,16},{1,17},{2,18},{3,19},{4,20},{5,21},{6,22},{7,23},{8,24},{9,... | collective-permute-start | bytes 393224 | tf_op jit(solution)/shard_map/ppermute | solution.py:304
  25.7 2.9 %collective-permute-done.7.fixes = f32[2,128,128]{2,1,0:T(8,128)S(1)} collective-permute-done((f32[2,128,128]{2,1,0:T(8,128)S(1)}, f32[2,128,128]{2,1,0:T(8,128)S(1)}, u32[]{:S(2)}, u32[]{:S(2)}) %collective-permute-start.7) | collective-permute-done | bytes 131104 | tf_op jit(solution)/shard_map/ppermute | solution.py:304
  28.9 1.8 %collective-permute-start.9 = (f32[3,128,128]{2,1,0:T(8,128)S(1)}, f32[3,128,128]{2,1,0:T(8,128)S(1)}, u32[]{:S(2)}, u32[]{:S(2)}) collective-permute-start(f32[3,128,128]{2,1,0:T(8,128)S(1)} %shard_map.59.own.rest_0_), channel_id=1, source_target_pairs={{1,2},{2,1},{3,4},{4,3},{5,6},{6,5},{7,8},{8,7},{9,10},{10,9},{11,... | collective-permute-start | bytes 589832 | tf_op jit(solution)/shard_map/ppermute | solution.py:304
  30.7 3.9 %collective-permute-done.9.cross = f32[3,128,128]{2,1,0:T(8,128)S(1)} collective-permute-done((f32[3,128,128]{2,1,0:T(8,128)S(1)}, f32[3,128,128]{2,1,0:T(8,128)S(1)}, u32[]{:S(2)}, u32[]{:S(2)}) %collective-permute-start.9) | collective-permute-done | bytes 196640 | tf_op jit(solution)/shard_map/ppermute | solution.py:304
  34.6 1.2 %shard_map.60 = (f32[3,128,128]{2,1,0:T(8,128)S(1)}, f32[2,128,128]{2,1,0:T(8,128)S(1)}) custom-call(bf16[768,1152]{1,0:T(8,128)(2,1)S(1)} %shard_map.55.matrix, f32[3,128,128]{2,1,0:T(8,128)S(1)} %shard_map.59.own.rest_0_, f32[3,128,128]{2,1,0:T(8,128)S(1)} %collective-permute-done.8.core, f32[3,128,128]{2,1,0:T(8,128)S(1)} %collective-permute-done.9.cross, ...), custom_call_target="tpu_custom_call" | custom-call | bytes 2949120 | tf_op jit(solution)/shard_map/pallas_call | solution.py:286
  36.5 1.5 %collective-permute-start.11 = (f32[3,128,128]{2,1,0:T(8,128)S(1)}, f32[3,128,128]{2,1,0:T(8,128)S(1)}, u32[]{:S(2)}, u32[]{:S(2)}) collective-permute-start(f32[3,128,128]{2,1,0:T(8,128)S(1)} %get-tuple-element.27.own), channel_id=1, source_target_pairs={{1,2},{2,1},{3,4},{4,3},{5,6},{6,5},{7,8},{8,7},{9,10},{10,9},{11,... | collective-permute-start | bytes 589832 | tf_op jit(solution)/shard_map/ppermute | solution.py:304
  38.6 1.1 %collective-permute-start.14 = (f32[2,128,128]{2,1,0:T(8,128)S(1)}, f32[2,128,128]{2,1,0:T(8,128)S(1)}, u32[]{:S(2)}, u32[]{:S(2)}) collective-permute-start(f32[2,128,128]{2,1,0:T(8,128)S(1)} %get-tuple-element.28), channel_id=1, source_target_pairs={{0,16},{1,18},{2,17},{3,20},{4,19},{5,22},{6,21},{7,24},{8,23},{9,... | collective-permute-start | bytes 393224 | tf_op jit(solution)/shard_map/ppermute | solution.py:304
  39.7 1.3 %collective-permute-done.12.mid_own = f32[2,128,128]{2,1,0:T(8,128)S(1)} collective-permute-done((f32[2,128,128]{2,1,0:T(8,128)S(1)}, f32[2,128,128]{2,1,0:T(8,128)S(1)}, u32[]{:S(2)}, u32[]{:S(2)}) %collective-permute-start.12) | collective-permute-done | bytes 131104 | tf_op jit(solution)/shard_map/ppermute | solution.py:304
  41.0 4.9 %collective-permute-done.14.mid_cross = f32[2,128,128]{2,1,0:T(8,128)S(1)} collective-permute-done((f32[2,128,128]{2,1,0:T(8,128)S(1)}, f32[2,128,128]{2,1,0:T(8,128)S(1)}, u32[]{:S(2)}, u32[]{:S(2)}) %collective-permute-start.14) | collective-permute-done | bytes 131104 | tf_op jit(solution)/shard_map/ppermute | solution.py:304
  46.7 2.3 %collective-permute-start.16 = (f32[3,128,128]{2,1,0:T(8,128)S(1)}, f32[3,128,128]{2,1,0:T(8,128)S(1)}, u32[]{:S(2)}, u32[]{:S(2)}) collective-permute-start(f32[3,128,128]{2,1,0:T(8,128)S(1)} %get-tuple-element.30.own), channel_id=1, source_target_pairs={{1,2},{2,1},{3,4},{4,3},{5,6},{6,5},{7,8},{8,7},{9,10},{10,9},{11,... | collective-permute-start | bytes 589832 | tf_op jit(solution)/shard_map/ppermute | solution.py:304
  48.9 3.6 %collective-permute-done.16.cross = f32[3,128,128]{2,1,0:T(8,128)S(1)} collective-permute-done((f32[3,128,128]{2,1,0:T(8,128)S(1)}, f32[3,128,128]{2,1,0:T(8,128)S(1)}, u32[]{:S(2)}, u32[]{:S(2)}) %collective-permute-start.16) | collective-permute-done | bytes 196640 | tf_op jit(solution)/shard_map/ppermute | solution.py:304
  53.3 2.3 %collective-permute-start.17 = (f32[2,128,128]{2,1,0:T(8,128)S(1)}, f32[2,128,128]{2,1,0:T(8,128)S(1)}, u32[]{:S(2)}, u32[]{:S(2)}) collective-permute-start(f32[2,128,128]{2,1,0:T(8,128)S(1)} %get-tuple-element.32), channel_id=1, source_target_pairs={{0,16},{1,17},{2,18},{3,19},{4,20},{5,21},{6,22},{7,23},{8,24},{9,... | collective-permute-start | bytes 393224 | tf_op jit(solution)/shard_map/ppermute | solution.py:304
  55.6 2.9 %collective-permute-done.17.fixes = f32[2,128,128]{2,1,0:T(8,128)S(1)} collective-permute-done((f32[2,128,128]{2,1,0:T(8,128)S(1)}, f32[2,128,128]{2,1,0:T(8,128)S(1)}, u32[]{:S(2)}, u32[]{:S(2)}) %collective-permute-start.17) | collective-permute-done | bytes 131104 | tf_op jit(solution)/shard_map/ppermute | solution.py:304
  58.6 0.9 %shard_map.63 = f32[3,128,128]{2,1,0:T(8,128)} custom-call(f32[3,128,128]{2,1,0:T(8,128)S(1)} %get-tuple-element.31.smooth, f32[2,128,128]{2,1,0:T(8,128)S(1)} %collective-permute-done.17.fixes, bf16[768,256]{1,0:T(8,128)(2,1)S(1)} %get-tuple-element.25.prolong, f32[3,128,128]{2,1,0:T(8,128)S(1)} %shard_map.59.own.rest_0_), custom_call_target="tpu_custom_call" | custom-call | bytes 917504 | tf_op jit(solution)/shard_map/pallas_call | solution.py:286
  (33 shorter events, 8.1 us)
Async XLA Ops:
  0.8 1.0 %copy-start = (f32[1,1,3,2,128,128]{5,4,3,2,1,0:T(8,128)S(1)}, f32[1,1,3,2,128,128]{5,4,3,2,1,0:T(8,128)}, u32[]{:S(2)}) copy-start(f32[1,1,3,2,128,128]{5,4,3,2,1,0:T(8,128)} %param.8) | copy-start | bytes 1179652
  1.8 0.9 %copy-start.3 = (f32[1,1,3,128,128]{4,3,2,1,0:T(8,128)S(1)}, f32[1,1,3,128,128]{4,3,2,1,0:T(8,128)}, u32[]{:S(2)}) copy-start(f32[1,1,3,128,128]{4,3,2,1,0:T(8,128)} %param.5) | copy-start | bytes 589828
  3.7 6.1 %collective-permute-start.2 = (f32[2,128,128]{2,1,0:T(8,128)S(1)}, f32[2,128,128]{2,1,0:T(8,128)S(1)}, u32[]{:S(2)}, u32[]{:S(2)}) collective-permute-start(f32[2,128,128]{2,1,0:T(8,128)S(1)} %get-tuple-element.20), channel_id=1, source_target_pairs={{0,16},{1,17},{2,18},{3,19},{4,20},{5,21},{6,22},{7,23},{8,24},{9,... | collective-permute-start | bytes 393224 | tf_op jit(solution)/shard_map/ppermute | solution.py:304
  6.3 9.1 %collective-permute-start.1 = (f32[3,128,128]{2,1,0:T(8,128)S(1)}, f32[3,128,128]{2,1,0:T(8,128)S(1)}, u32[]{:S(2)}, u32[]{:S(2)}) collective-permute-start(f32[3,128,128]{2,1,0:T(8,128)S(1)} %get-tuple-element.19.own.down_own), channel_id=1, source_target_pairs={{1,2},{2,1},{3,4},{4,3},{5,6},{6,5},{7,8},{8,7},{9,10},{10,9},{11,... | collective-permute-start | bytes 589832 | tf_op jit(solution)/shard_map/ppermute | solution.py:304
  6.4 9.0 %collective-permute-start = (f32[3,128,128]{2,1,0:T(8,128)S(1)}, f32[3,128,128]{2,1,0:T(8,128)S(1)}, u32[]{:S(2)}, u32[]{:S(2)}) collective-permute-start(f32[3,128,128]{2,1,0:T(8,128)S(1)} %get-tuple-element.19.own.down_own), channel_id=1, source_target_pairs={{0,1},{1,0},{2,3},{3,2},{4,5},{5,4},{6,7},{7,6},{8,9},{9,8},{10,11... | collective-permute-start | bytes 589832 | tf_op jit(solution)/shard_map/ppermute | solution.py:304
  7.9 7.4 %collective-permute-start.4 = (f32[2,128,128]{2,1,0:T(8,128)S(1)}, f32[2,128,128]{2,1,0:T(8,128)S(1)}, u32[]{:S(2)}, u32[]{:S(2)}) collective-permute-start(f32[2,128,128]{2,1,0:T(8,128)S(1)} %get-tuple-element.20), channel_id=1, source_target_pairs={{0,16},{1,18},{2,17},{3,20},{4,19},{5,22},{6,21},{7,24},{8,23},{9,... | collective-permute-start | bytes 393224 | tf_op jit(solution)/shard_map/ppermute | solution.py:304
  9.8 5.6 %collective-permute-start.3 = (f32[2,128,128]{2,1,0:T(8,128)S(1)}, f32[2,128,128]{2,1,0:T(8,128)S(1)}, u32[]{:S(2)}, u32[]{:S(2)}) collective-permute-start(f32[2,128,128]{2,1,0:T(8,128)S(1)} %collective-permute-done.2.mid_own), channel_id=1, source_target_pairs={{0,1},{1,0},{2,3},{3,2},{4,5},{5,4},{6,7},{7,6},{8,9},{9,8},{10,11... | collective-permute-start | bytes 393224 | tf_op jit(solution)/shard_map/ppermute | solution.py:304
  10.6 1.3 %copy-start.2 = (f32[1,1,3,7,128,128]{5,4,3,2,1,0:T(8,128)S(1)}, f32[1,1,3,7,128,128]{5,4,3,2,1,0:T(8,128)}, u32[]{:S(2)}) copy-start(f32[1,1,3,7,128,128]{5,4,3,2,1,0:T(8,128)} %param.6) | copy-start | bytes 4128772
  13.1 9.5 %copy-start.1 = (f32[1,1,3,2,128,128]{5,4,3,2,1,0:T(8,128)S(1)}, f32[1,1,3,2,128,128]{5,4,3,2,1,0:T(8,128)}, u32[]{:S(2)}) copy-start(f32[1,1,3,2,128,128]{5,4,3,2,1,0:T(8,128)} %param.8) | copy-start | bytes 1179652
  16.2 6.4 %collective-permute-start.6 = (f32[3,128,128]{2,1,0:T(8,128)S(1)}, f32[3,128,128]{2,1,0:T(8,128)S(1)}, u32[]{:S(2)}, u32[]{:S(2)}) collective-permute-start(f32[3,128,128]{2,1,0:T(8,128)S(1)} %get-tuple-element.22.own), channel_id=1, source_target_pairs={{1,2},{2,1},{3,4},{4,3},{5,6},{6,5},{7,8},{8,7},{9,10},{10,9},{11,... | collective-permute-start | bytes 589832 | tf_op jit(solution)/shard_map/ppermute | solution.py:304
  19.0 3.7 %collective-permute-start.5 = (f32[3,128,128]{2,1,0:T(8,128)S(1)}, f32[3,128,128]{2,1,0:T(8,128)S(1)}, u32[]{:S(2)}, u32[]{:S(2)}) collective-permute-start(f32[3,128,128]{2,1,0:T(8,128)S(1)} %get-tuple-element.22.own), channel_id=1, source_target_pairs={{0,1},{1,0},{2,3},{3,2},{4,5},{5,4},{6,7},{7,6},{8,9},{9,8},{10,11... | collective-permute-start | bytes 589832 | tf_op jit(solution)/shard_map/ppermute | solution.py:304
  22.6 12.0 %copy-start.4 = (f32[1,1,3,128,128]{4,3,2,1,0:T(8,128)S(1)}, f32[1,1,3,128,128]{4,3,2,1,0:T(8,128)}, u32[]{:S(2)}) copy-start(f32[1,1,3,128,128]{4,3,2,1,0:T(8,128)} %param.5) | copy-start | bytes 589828
  23.4 5.2 %collective-permute-start.7 = (f32[2,128,128]{2,1,0:T(8,128)S(1)}, f32[2,128,128]{2,1,0:T(8,128)S(1)}, u32[]{:S(2)}, u32[]{:S(2)}) collective-permute-start(f32[2,128,128]{2,1,0:T(8,128)S(1)} %get-tuple-element.24), channel_id=1, source_target_pairs={{0,16},{1,17},{2,18},{3,19},{4,20},{5,21},{6,22},{7,23},{8,24},{9,... | collective-permute-start | bytes 393224 | tf_op jit(solution)/shard_map/ppermute | solution.py:304
  28.9 5.7 %collective-permute-start.9 = (f32[3,128,128]{2,1,0:T(8,128)S(1)}, f32[3,128,128]{2,1,0:T(8,128)S(1)}, u32[]{:S(2)}, u32[]{:S(2)}) collective-permute-start(f32[3,128,128]{2,1,0:T(8,128)S(1)} %shard_map.59.own.rest_0_), channel_id=1, source_target_pairs={{1,2},{2,1},{3,4},{4,3},{5,6},{6,5},{7,8},{8,7},{9,10},{10,9},{11,... | collective-permute-start | bytes 589832 | tf_op jit(solution)/shard_map/ppermute | solution.py:304
  30.7 3.9 %collective-permute-start.8 = (f32[3,128,128]{2,1,0:T(8,128)S(1)}, f32[3,128,128]{2,1,0:T(8,128)S(1)}, u32[]{:S(2)}, u32[]{:S(2)}) collective-permute-start(f32[3,128,128]{2,1,0:T(8,128)S(1)} %shard_map.59.own.rest_0_), channel_id=1, source_target_pairs={{0,1},{1,0},{2,3},{3,2},{4,5},{5,4},{6,7},{7,6},{8,9},{9,8},{10,11... | collective-permute-start | bytes 589832 | tf_op jit(solution)/shard_map/ppermute | solution.py:304
  35.8 5.1 %collective-permute-start.12 = (f32[2,128,128]{2,1,0:T(8,128)S(1)}, f32[2,128,128]{2,1,0:T(8,128)S(1)}, u32[]{:S(2)}, u32[]{:S(2)}) collective-permute-start(f32[2,128,128]{2,1,0:T(8,128)S(1)} %get-tuple-element.28), channel_id=1, source_target_pairs={{0,16},{1,17},{2,18},{3,19},{4,20},{5,21},{6,22},{7,23},{8,24},{9,... | collective-permute-start | bytes 393224 | tf_op jit(solution)/shard_map/ppermute | solution.py:304
  36.5 9.4 %collective-permute-start.11 = (f32[3,128,128]{2,1,0:T(8,128)S(1)}, f32[3,128,128]{2,1,0:T(8,128)S(1)}, u32[]{:S(2)}, u32[]{:S(2)}) collective-permute-start(f32[3,128,128]{2,1,0:T(8,128)S(1)} %get-tuple-element.27.own), channel_id=1, source_target_pairs={{1,2},{2,1},{3,4},{4,3},{5,6},{6,5},{7,8},{8,7},{9,10},{10,9},{11,... | collective-permute-start | bytes 589832 | tf_op jit(solution)/shard_map/ppermute | solution.py:304
  37.9 7.9 %collective-permute-start.10 = (f32[3,128,128]{2,1,0:T(8,128)S(1)}, f32[3,128,128]{2,1,0:T(8,128)S(1)}, u32[]{:S(2)}, u32[]{:S(2)}) collective-permute-start(f32[3,128,128]{2,1,0:T(8,128)S(1)} %get-tuple-element.27.own), channel_id=1, source_target_pairs={{0,1},{1,0},{2,3},{3,2},{4,5},{5,4},{6,7},{7,6},{8,9},{9,8},{10,11... | collective-permute-start | bytes 589832 | tf_op jit(solution)/shard_map/ppermute | solution.py:304
  38.6 7.3 %collective-permute-start.14 = (f32[2,128,128]{2,1,0:T(8,128)S(1)}, f32[2,128,128]{2,1,0:T(8,128)S(1)}, u32[]{:S(2)}, u32[]{:S(2)}) collective-permute-start(f32[2,128,128]{2,1,0:T(8,128)S(1)} %get-tuple-element.28), channel_id=1, source_target_pairs={{0,16},{1,18},{2,17},{3,20},{4,19},{5,22},{6,21},{7,24},{8,23},{9,... | collective-permute-start | bytes 393224 | tf_op jit(solution)/shard_map/ppermute | solution.py:304
  41.0 4.9 %collective-permute-start.13 = (f32[2,128,128]{2,1,0:T(8,128)S(1)}, f32[2,128,128]{2,1,0:T(8,128)S(1)}, u32[]{:S(2)}, u32[]{:S(2)}) collective-permute-start(f32[2,128,128]{2,1,0:T(8,128)S(1)} %collective-permute-done.12.mid_own), channel_id=1, source_target_pairs={{0,1},{1,0},{2,3},{3,2},{4,5},{5,4},{6,7},{7,6},{8,9},{9,8},{10,11... | collective-permute-start | bytes 393224 | tf_op jit(solution)/shard_map/ppermute | solution.py:304
  46.7 5.9 %collective-permute-start.16 = (f32[3,128,128]{2,1,0:T(8,128)S(1)}, f32[3,128,128]{2,1,0:T(8,128)S(1)}, u32[]{:S(2)}, u32[]{:S(2)}) collective-permute-start(f32[3,128,128]{2,1,0:T(8,128)S(1)} %get-tuple-element.30.own), channel_id=1, source_target_pairs={{1,2},{2,1},{3,4},{4,3},{5,6},{6,5},{7,8},{8,7},{9,10},{10,9},{11,... | collective-permute-start | bytes 589832 | tf_op jit(solution)/shard_map/ppermute | solution.py:304
  48.9 3.7 %collective-permute-start.15 = (f32[3,128,128]{2,1,0:T(8,128)S(1)}, f32[3,128,128]{2,1,0:T(8,128)S(1)}, u32[]{:S(2)}, u32[]{:S(2)}) collective-permute-start(f32[3,128,128]{2,1,0:T(8,128)S(1)} %get-tuple-element.30.own), channel_id=1, source_target_pairs={{0,1},{1,0},{2,3},{3,2},{4,5},{5,4},{6,7},{7,6},{8,9},{9,8},{10,11... | collective-permute-start | bytes 589832 | tf_op jit(solution)/shard_map/ppermute | solution.py:304
  53.3 5.2 %collective-permute-start.17 = (f32[2,128,128]{2,1,0:T(8,128)S(1)}, f32[2,128,128]{2,1,0:T(8,128)S(1)}, u32[]{:S(2)}, u32[]{:S(2)}) collective-permute-start(f32[2,128,128]{2,1,0:T(8,128)S(1)} %get-tuple-element.32), channel_id=1, source_target_pairs={{0,16},{1,17},{2,18},{3,19},{4,20},{5,21},{6,22},{7,23},{8,24},{9,... | collective-permute-start | bytes 393224 | tf_op jit(solution)/shard_map/ppermute | solution.py:304

commit v2 on v1

--- a/solution.py
+++ b/solution.py
@@ -139,48 +139,62 @@
     return jnp.concatenate(blocks, axis=0)
 
 
-def restrict_kernel(targets, rhs, links, mids, payload, restrict, prolong):
-    size = rhs.shape[-1]
-    slots = rhs.shape[0]
+def restrict_kernel(targets_in, rhs_in, links_in, mids, payload, restrict, targets, links, sems):
+    size = payload.shape[-1]
+    slots = payload.shape[0]
+    fetch_targets = pltpu.make_async_copy(targets_in.at[0, 0], targets, sems.at[0])
+    fetch_links = pltpu.make_async_copy(links_in, links, sems.at[1])
+    fetch_rhs = pltpu.make_async_copy(rhs_in, payload, sems.at[2])
+    fetch_targets.start()
+    fetch_links.start()
 
     @pl.when(lax.axis_index("lvl") == 0)
     def _():
-        payload[...] = rhs[...]
+        fetch_rhs.start()
+        fetch_targets.wait()
+        fetch_links.wait()
         for s in range(slots):
             for k in range(2):
-                down = jnp.where(targets[s, 0] == k, links[s, 0], 0.0)
+                down = jnp.where(targets[0, s] == k, links[s, 0], 0.0)
                 high, low = split(down)
                 restrict[k * size:(k + 1) * size, s * size:(s + 1) * size] = high
                 restrict[(2 + k) * size:(3 + k) * size, s * size:(s + 1) * size] = low
-                up = jnp.where(targets[s, 1] == k, links[s, 1], 0.0)
-                high, low = split(up)
-                prolong[s * size:(s + 1) * size, k * size:(k + 1) * size] = high
-                prolong[(slots + s) * size:(slots + s + 1) * size, k * size:(k + 1) * size] = low
-        right = split_columns(rhs[...].reshape(slots * size, size))
+        fetch_rhs.wait()
+        right = split_columns(payload[...].reshape(slots * size, size))
         mids[...] = product(restrict[...], right).reshape(mids.shape)
 
     @pl.when(lax.axis_index("lvl") != 0)
     def _():
+        fetch_targets.wait()
+        fetch_links.wait()
         payload[0] = links[0, 0]
         payload[1] = links[2, 0]
         payload[2] = jnp.zeros_like(payload[2])
         mids[...] = jnp.zeros_like(mids)
 
 
-def operator_kernel(columns, tiles, matrix, gathered):
+def operator_kernel(columns_in, targets_in, links_in, tiles_in, matrix, prolong, columns, targets, links, tiles, gathered, sems):
     slots, count, size = tiles.shape[0], tiles.shape[1], tiles.shape[-1]
+    fetch_columns = pltpu.make_async_copy(columns_in.at[0], columns, sems.at[0])
+    fetch_targets = pltpu.make_async_copy(targets_in.at[0, 0], targets, sems.at[1])
+    fetch_links = pltpu.make_async_copy(links_in, links, sems.at[2])
+    fetch_tiles = [pltpu.make_async_copy(tiles_in.at[s], tiles.at[s], sems.at[3 + s]) for s in range(slots)]
+    for fetch in (fetch_columns, fetch_targets, *fetch_tiles, fetch_links):
+        fetch.start()
     row = lax.axis_index("row")
     odd = lax.rem(row, 2)
     inner = (row > 0) & (row < lax.axis_size("row") - 1)
     gathered[...] = jnp.zeros_like(gathered)
+    fetch_columns.wait()
+    fetch_targets.wait()
     for s in range(slots):
+        fetch_tiles[s].wait()
         for j in range(count):
-            code = columns[s, j]
+            code = columns[s, 0, j]
             step = code // slots
             slot = code - slots * step
             side = jnp.where(step == 1, 0, jnp.where(step == 2 * (1 - odd), 1, 2))
             gathered[s, side * slots + slot] += tiles[s, j]
-    for s in range(slots):
         for c in range(3 * slots):
             block = gathered[s, c]
             if c >= 2 * slots:
@@ -188,46 +202,60 @@
             high, low = split(block)
             matrix[s * size:(s + 1) * size, c * size:(c + 1) * size] = high
             matrix[(slots + s) * size:(slots + s + 1) * size, c * size:(c + 1) * size] = low
-
-
-def load(field, refs):
-    size = field.shape[0] // (len(refs) * refs[0].shape[0])
-    for g, ref in enumerate(refs):
-        for s in range(ref.shape[0]):
-            high, low = split(ref[s])
-            at = (g * ref.shape[0] + s) * size
-            field[at:at + size, :size] = high
-            field[at:at + size, size:] = low
+    fetch_links.wait()
+    for s in range(slots):
+        for k in range(2):
+            up = jnp.where(targets[1, s] == k, links[s, 1], 0.0)
+            high, low = split(up)
+            prolong[s * size:(s + 1) * size, k * size:(k + 1) * size] = high
+            prolong[(slots + s) * size:(slots + s + 1) * size, k * size:(k + 1) * size] = low
+
+
+def joined(blocks):
+    return split_columns(stacked(*blocks))
+
+
+def blocks_of(*refs):
+    return [ref[s] for ref in refs for s in range(ref.shape[0])]
+
+
+def near(matrix, field):
+    columns = 2 * (matrix.shape[1] // 3)
+    return product(matrix[:, :columns], field)
+
+
+def far(matrix, field):
+    columns = 2 * (matrix.shape[1] // 3)
+    return product(matrix[:, columns:], field)
+
+
+def level_blocks(down, mid):
+    left = split_rows(jnp.concatenate([down[0], down[1]], axis=1))
+    coarse = product(left, joined((mid[0], mid[1]))) + 0.5 * (mid[0] + mid[1])
+    return [mid[0], coarse, mid[1]]
 
 
 def first_kernel(matrix, own, core, cross, down_own, down_core, down_cross, mid_own, mid_core, mid_cross, level, first, field):
-    size = own.shape[-1]
-
     @pl.when(lax.axis_index("lvl") == 0)
     def _():
-        load(field, (own, core, cross))
+        field[...] = joined(blocks_of(own, core, cross))
         level[...] = own[...]
 
     @pl.when(lax.axis_index("lvl") != 0)
     def _():
-        for g, (down, mid) in enumerate(((down_own, mid_own), (down_core, mid_core), (down_cross, mid_cross))):
-            left = split_rows(jnp.concatenate([down[0], down[1]], axis=1))
-            right = split_columns(stacked(mid[0], mid[1]))
-            coarse = product(left, right) + 0.5 * (mid[0] + mid[1])
-            for s, value in enumerate((mid[0], coarse, mid[1])):
-                high, low = split(value)
-                at = (3 * g + s) * size
-                field[at:at + size, :size] = high
-                field[at:at + size, size:] = low
-                if g == 0:
-                    level[s] = value
+        here = level_blocks(down_own, mid_own)
+        field[...] = joined(here + level_blocks(down_core, mid_core) + level_blocks(down_cross, mid_cross))
+        level[...] = stacked(*here).reshape(level.shape)
 
     first[...] = product(matrix[...], field[...]).reshape(first.shape)
 
 
-def second_kernel(matrix, level, own, core, cross, links, smooth, fixes, field):
-    load(field, (own, core, cross))
-    second = product(matrix[...], field[...]).reshape(level.shape)
+def near_kernel(matrix, own, core, core_last, part):
+    part[...] = near(matrix, joined(blocks_of(own, core, core_last))).reshape(part.shape)
+
+
+def second_kernel(matrix, level, own, part, cross, links, smooth, fixes):
+    second = part[...] + far(matrix, joined(blocks_of(cross))).reshape(part.shape)
     value = COEF_ZERO * level[...] + COEF_ONE * own[...] + COEF_TWO * second
 
     @pl.when(lax.axis_index("lvl") == 0)
@@ -253,8 +281,7 @@
 
     @pl.when(lax.axis_index("lvl") == 0)
     def _():
-        right = split_columns(stacked(fixes[0], fixes[1]))
-        value = smooth[...] + product(prolong[...], right).reshape(smooth.shape)
+        value = smooth[...] + product(prolong[...], joined((fixes[0], fixes[1]))).reshape(smooth.shape)
         if len(rest) == 2:
             value = value + rest[0][...]
         result[...] = value
@@ -264,14 +291,12 @@
         result[...] = smooth[...]
 
 
-def residual_kernel(matrix, own, core, cross, rhs, restrict, resid, mids, field):
+def residual_kernel(matrix, part, cross, rhs, restrict, resid, mids):
     @pl.when(lax.axis_index("lvl") == 0)
     def _():
-        load(field, (own, core, cross))
-        value = rhs[...] - product(matrix[...], field[...]).reshape(rhs.shape)
+        value = rhs[...] - (part[...] + far(matrix, joined(blocks_of(cross))).reshape(rhs.shape))
         resid[...] = value
-        right = split_columns(value.reshape(-1, value.shape[-1]))
-        mids[...] = product(restrict[...], right).reshape(mids.shape)
+        mids[...] = product(restrict[...], joined([value[s] for s in range(value.shape[0])])).reshape(mids.shape)
 
     @pl.when(lax.axis_index("lvl") != 0)
     def _():
@@ -279,18 +304,19 @@
         mids[...] = jnp.zeros_like(mids)
 
 
-def call(kernel, outs, args, scalars=0, scratch=(), flops=0):
-    spaces = [pl.BlockSpec(memory_space=pltpu.SMEM)] * scalars
-    spaces += [pl.BlockSpec(memory_space=pltpu.VMEM)] * (len(args) - scalars)
-    size = sum(a.size * a.dtype.itemsize for a in args)
+def call(kernel, outs, args, anywhere=0, scratch=(), aliases={}):
+    args = [pltpu.with_memory_space_constraint(a, pltpu.HBM) for a in args[:anywhere]] + list(args[anywhere:])
+    spaces = [pl.BlockSpec(memory_space=pltpu.HBM)] * anywhere
+    spaces += [pl.BlockSpec(memory_space=pltpu.VMEM)] * (len(args) - anywhere)
     return pl.pallas_call(
         kernel,
         out_shape=[jax.ShapeDtypeStruct(shape, dtype) for shape, dtype in outs],
         in_specs=spaces,
         out_specs=[pl.BlockSpec(memory_space=pltpu.VMEM)] * len(outs),
-        scratch_shapes=[pltpu.VMEM(shape, dtype) for shape, dtype in scratch],
+        scratch_shapes=scratch,
+        input_output_aliases=aliases,
         compiler_params=pltpu.CompilerParams(vmem_limit_bytes=24 * 1024 * 1024),
-        cost_estimate=pl.CostEstimate(flops=flops, bytes_accessed=size, transcendentals=0),
+        cost_estimate=pl.CostEstimate(flops=0, bytes_accessed=0, transcendentals=0),
     )(*args)
 
 
@@ -299,60 +325,66 @@
     core = [(l * rows + r, l * rows + (r ^ 1)) for l in range(2) for r in range(rows)]
     cross = [(l * rows + r, l * rows + across[r]) for l in range(2) for r in range(1, rows - 1)]
     cross += [(l * rows + r, (1 - l) * rows + r) for l in range(2) for r in (0, rows - 1)]
+    fine = [(r, across[r]) for r in range(1, rows - 1)] + [(rows + r, rows + (r ^ 1)) for r in range(2, rows - 2)]
+    for end, beside in ((0, 1), (rows - 1, rows - 2)):
+        fine += [(end, rows + end), (rows + end, rows + beside), (rows + beside, end)]
     level = [(l * rows + r, (1 - l) * rows + r) for l in range(2) for r in range(rows)]
     skew = [(r, rows + across[r]) for r in range(rows)] + [(rows + r, r) for r in range(rows)]
-    return tuple((lambda x, pairs=pairs: lax.ppermute(x, ("lvl", "row"), pairs)) for pairs in (core, cross, level, skew))
+    return tuple((lambda x, pairs=pairs: lax.ppermute(x, ("lvl", "row"), pairs)) for pairs in (core, cross, fine, level, skew))
 
 
 def paired(rhs, op_tiles, op_cols, link_tiles, level_links):
-    core, cross, level, skew = swaps(lax.axis_size("row"))
-    right, tiles, columns = rhs[0, 0], op_tiles[0, 0], op_cols[0, 0]
-    links, targets = link_tiles[0, 0], level_links[0, 0]
+    core, cross, fine, level, skew = swaps(lax.axis_size("row"))
+    right, tiles, links = rhs[0, 0], op_tiles[0, 0], link_tiles[0, 0]
     slots, size, width = right.shape
     blocks, pair = (right.shape, F32), ((2, size, width), F32)
-    big, field = slots * size, ((3 * slots * size, 2 * width), BF16)
-    mids, payload, restrict, prolong = call(
+    big = slots * size
+    codes, goals = jnp.swapaxes(op_cols, 1, 2), jnp.swapaxes(level_links, 2, 3)
+    mids, payload, restrict = call(
         restrict_kernel,
-        [pair, blocks, ((4 * size, big), BF16), ((2 * big, 2 * size), BF16)],
-        [targets, right, links],
-        scalars=1,
+        [pair, blocks, ((4 * size, big), BF16)],
+        [goals, right, links],
+        anywhere=3,
+        scratch=[
+            pltpu.SMEM(goals.shape[2:], goals.dtype),
+            pltpu.VMEM(links.shape, links.dtype),
+            pltpu.SemaphoreType.DMA((3,)),
+        ],
     )
-    down = None
-    result = None
-    matrix = None
+    down = result = matrix = prolong = None
     for cycle in range(CYCLES):
         if cycle > 0:
-            resid, mids = call(
-                residual_kernel,
-                [blocks, pair],
-                [matrix, result, core(result), cross(result), right, restrict],
-                scratch=[field],
-            )
-            payload = resid
+            result_cross = cross(result)
+            (part,) = call(near_kernel, [blocks], [matrix, result, core(result[:-1]), core(result[-1:])])
+            payload, mids = call(residual_kernel, [blocks, pair], [matrix, part, result_cross, right, restrict])
         mid_here, mid_cross = level(mids), skew(mids)
-        around = (payload, core(payload), cross(payload))
+        around = (payload, core(payload), cross(payload) if cycle == 0 else fine(payload))
         mid_core = core(mid_here)
         if cycle == 0:
-            (matrix,) = call(
+            matrix, prolong = call(
                 operator_kernel,
-                [((2 * big, 3 * big), BF16)],
-                [columns, tiles],
-                scalars=1,
-                scratch=[((slots, 3 * slots, size, size), F32)],
+                [((2 * big, 3 * big), BF16), ((2 * big, 2 * size), BF16)],
+                [codes, goals, links, tiles],
+                anywhere=4,
+                scratch=[
+                    pltpu.SMEM(codes.shape[1:], codes.dtype),
+                    pltpu.SMEM(goals.shape[2:], goals.dtype),
+                    pltpu.VMEM(links.shape, links.dtype),
+                    pltpu.VMEM(tiles.shape, tiles.dtype),
+                    pltpu.VMEM((slots, 3 * slots, size, size), F32),
+                    pltpu.SemaphoreType.DMA((3 + slots,)),
+                ],
             )
             down = around
         level_resid, first = call(
             first_kernel,
             [blocks, blocks],
             [matrix, *around, *down, mid_here, mid_core, mid_cross],
-            scratch=[field],
+            scratch=[pltpu.VMEM((3 * big, 2 * width), BF16)],
         )
-        smooth, fixes = call(
-            second_kernel,
-            [blocks, pair],
-            [matrix, level_resid, first, core(first), cross(first), links],
-            scratch=[field],
-        )
+        first_cross = cross(first)
+        (part,) = call(near_kernel, [blocks], [matrix, first, core(first[:-1]), core(first[-1:])])
+        smooth, fixes = call(second_kernel, [blocks, pair], [matrix, level_resid, first, part, first_cross, links])
         fixes = level(fixes)
         args = [smooth, fixes, prolong] + ([] if cycle == 0 else [result])
         (result,) = call(solution_kernel, [blocks], args)

time: 59.8 us -> 56.6 us (0.946)
  local copies, waits for them, and re-layouts: 4.72 us -> 0.06 us
  starting transfers between devices: 20.6 us -> 22 us
  Pallas kernels: 7.64 us -> 8.92 us
  waiting for transfers between devices: 26.5 us -> 25.3 us
    unnamed x11 -> x4, local copies, waits for them, and re-layouts: 3.95 us -> 0.01 us
    ppermute x18 -> x21, starting transfers between devices: 20.6 us -> 22 us  [swaps(): lax.ppermute(x, ('lvl', 'row'), pairs)]
    pallas_call x9 -> x12, Pallas kernels: 7.64 us -> 8.92 us  [call(): pl.pallas_call(kernel, out_shape=[jax.ShapeDtypeStruct(shape, dtype) for...]
    ppermute x18 -> x21, waiting for transfers between devices: 26.5 us -> 25.3 us  [swaps(): lax.ppermute(x, ('lvl', 'row'), pairs)]
    squeeze x1 -> x0, local copies, waits for them, and re-layouts: 0.76 us -> none  [paired(): links, targets = (link_tiles[0, 0], level_links[0, 0])]
  transfers between devices with their start and end apart: 18 -> 21, of which waited for: 9 -> 12; matrix products, arithmetic and copies ran while one was open for 1% -> 0% of each run, Pallas kernels for 2% -> 6%
where the time goes in v2:
time: 56.6 us; the launch traced here: 56.5 us
  waiting for transfers between devices  25.3 us (45%)
  starting transfers between devices  22 us (39%)
  Pallas kernels  8.92 us (16%)
    ppermute x21, waiting for transfers between devices, swaps(): lax.ppermute(x, ('lvl', 'row'), pairs)  25.3 us
    ppermute x21, starting transfers between devices, swaps(): lax.ppermute(x, ('lvl', 'row'), pairs)  22 us
    pallas_call x12, Pallas kernels, call(): pl.pallas_call(kernel, out_shape=[jax.ShapeDtypeStruct(shape, dtype) for...  8.92 us
  transfers between devices with their start and end apart: 21, of which 12 were waited for; matrix products, arithmetic and copies ran while one was open for 0% of the time, Pallas kernels for 6%

profile of v2, /device:TPU:0, one launch (start us, length us, event | category | flops | bytes accessed | tf_op | source)
XLA Modules:
  0.0 56.5 jit_solution(17249536726674538340)
XLA Ops:
  0.0 1.4 %shard_map.56 = (f32[2,128,128]{2,1,0:T(8,128)S(1)}, f32[3,128,128]{2,1,0:T(8,128)S(1)}, bf16[512,384]{1,0:T(8,128)(2,1)S(1)}) custom-call(s32[1,1,2,3]{3,2,1,0:T(2,128)} %bitcast.13, f32[3,128,128]{2,1,0:T(8,128)} %bitcast.10, f32[3,2,128,128]{3,2,1,0:T(8,128)} %bitcast.6), custom_call_target="tpu_custom_call" | custom-call | tf_op jit(solution)/shard_map/pallas_call | solution.py:311
  1.4 2.7 %collective-permute-start.2 = (f32[2,128,128]{2,1,0:T(8,128)S(1)}, f32[2,128,128]{2,1,0:T(8,128)S(1)}, u32[]{:S(2)}, u32[]{:S(2)}) collective-permute-start(f32[2,128,128]{2,1,0:T(8,128)S(1)} %get-tuple-element.22), channel_id=1, source_target_pairs={{0,16},{1,17},{2,18},{3,19},{4,20},{5,21},{6,22},{7,23},{8,24},{9,... | collective-permute-start | bytes 393224 | tf_op jit(solution)/shard_map/ppermute | solution.py:333
  4.1 1.6 %collective-permute-start = (f32[3,128,128]{2,1,0:T(8,128)S(1)}, f32[3,128,128]{2,1,0:T(8,128)S(1)}, u32[]{:S(2)}, u32[]{:S(2)}) collective-permute-start(f32[3,128,128]{2,1,0:T(8,128)S(1)} %get-tuple-element.21.own.down_own), channel_id=1, source_target_pairs={{0,1},{1,0},{2,3},{3,2},{4,5},{5,4},{6,7},{7,6},{8,9},{9,8},{10,11... | collective-permute-start | bytes 589832 | tf_op jit(solution)/shard_map/ppermute | solution.py:333
  6.6 1.0 %collective-permute-done.2.mid_own = f32[2,128,128]{2,1,0:T(8,128)S(1)} collective-permute-done((f32[2,128,128]{2,1,0:T(8,128)S(1)}, f32[2,128,128]{2,1,0:T(8,128)S(1)}, u32[]{:S(2)}, u32[]{:S(2)}) %collective-permute-start.2) | collective-permute-done | bytes 131104 | tf_op jit(solution)/shard_map/ppermute | solution.py:333
  7.7 1.7 %shard_map.55 = (bf16[768,1152]{1,0:T(8,128)(2,1)S(1)}, bf16[768,256]{1,0:T(8,128)(2,1)S(1)}) custom-call(s32[1,3,1,7]{3,2,1,0:T(1,128)} %bitcast.15, s32[1,1,2,3]{3,2,1,0:T(2,128)} %bitcast.14, f32[3,2,128,128]{3,2,1,0:T(8,128)} %bitcast.7, f32[3,7,128,128]{3,2,1,0:T(8,128)} %bitcast.12), custom_call_target="tpu_custom_call" | custom-call | tf_op jit(solution)/shard_map/pallas_call | solution.py:311
  9.3 3.8 %collective-permute-done.4.mid_cross = f32[2,128,128]{2,1,0:T(8,128)S(1)} collective-permute-done((f32[2,128,128]{2,1,0:T(8,128)S(1)}, f32[2,128,128]{2,1,0:T(8,128)S(1)}, u32[]{:S(2)}, u32[]{:S(2)}) %collective-permute-start.4) | collective-permute-done | bytes 131104 | tf_op jit(solution)/shard_map/ppermute | solution.py:333
  13.9 2.8 %collective-permute-start.7 = (f32[3,128,128]{2,1,0:T(8,128)S(1)}, f32[3,128,128]{2,1,0:T(8,128)S(1)}, u32[]{:S(2)}, u32[]{:S(2)}) collective-permute-start(f32[3,128,128]{2,1,0:T(8,128)S(1)} %get-tuple-element.24.own), channel_id=1, source_target_pairs={{1,2},{2,1},{3,4},{4,3},{5,6},{6,5},{7,8},{8,7},{9,10},{10,9},{11,... | collective-permute-start | bytes 589832 | tf_op jit(solution)/shard_map/ppermute | solution.py:333
  17.3 0.9 %collective-permute-done.6.core_last = f32[1,128,128]{2,1,0:T(8,128)S(1)} collective-permute-done((f32[1,128,128]{2,1,0:T(8,128)S(1)}, f32[1,128,128]{2,1,0:T(8,128)S(1)}, u32[]{:S(2)}, u32[]{:S(2)}) %collective-permute-start.6) | collective-permute-done | bytes 65568 | tf_op jit(solution)/shard_map/ppermute | solution.py:333
  18.7 1.6 %collective-permute-done.7.cross = f32[3,128,128]{2,1,0:T(8,128)S(1)} collective-permute-done((f32[3,128,128]{2,1,0:T(8,128)S(1)}, f32[3,128,128]{2,1,0:T(8,128)S(1)}, u32[]{:S(2)}, u32[]{:S(2)}) %collective-permute-start.7) | collective-permute-done | bytes 196640 | tf_op jit(solution)/shard_map/ppermute | solution.py:333
  20.7 2.3 %collective-permute-start.8 = (f32[2,128,128]{2,1,0:T(8,128)S(1)}, f32[2,128,128]{2,1,0:T(8,128)S(1)}, u32[]{:S(2)}, u32[]{:S(2)}) collective-permute-start(f32[2,128,128]{2,1,0:T(8,128)S(1)} %get-tuple-element.26), channel_id=1, source_target_pairs={{0,16},{1,17},{2,18},{3,19},{4,20},{5,21},{6,22},{7,23},{8,24},{9,... | collective-permute-start | bytes 393224 | tf_op jit(solution)/shard_map/ppermute | solution.py:333
  23.0 2.9 %collective-permute-done.8.fixes = f32[2,128,128]{2,1,0:T(8,128)S(1)} collective-permute-done((f32[2,128,128]{2,1,0:T(8,128)S(1)}, f32[2,128,128]{2,1,0:T(8,128)S(1)}, u32[]{:S(2)}, u32[]{:S(2)}) %collective-permute-start.8) | collective-permute-done | bytes 131104 | tf_op jit(solution)/shard_map/ppermute | solution.py:333
  26.3 1.8 %collective-permute-start.11 = (f32[3,128,128]{2,1,0:T(8,128)S(1)}, f32[3,128,128]{2,1,0:T(8,128)S(1)}, u32[]{:S(2)}, u32[]{:S(2)}) collective-permute-start(f32[3,128,128]{2,1,0:T(8,128)S(1)} %shard_map.60.own.rest_0_), channel_id=1, source_target_pairs={{1,2},{2,1},{3,4},{4,3},{5,6},{6,5},{7,8},{8,7},{9,10},{10,9},{11,... | collective-permute-start | bytes 589832 | tf_op jit(solution)/shard_map/ppermute | solution.py:333
  28.7 0.9 %collective-permute-done.10.core_last = f32[1,128,128]{2,1,0:T(8,128)S(1)} collective-permute-done((f32[1,128,128]{2,1,0:T(8,128)S(1)}, f32[1,128,128]{2,1,0:T(8,128)S(1)}, u32[]{:S(2)}, u32[]{:S(2)}) %collective-permute-start.10) | collective-permute-done | bytes 65568 | tf_op jit(solution)/shard_map/ppermute | solution.py:333
  30.1 1.9 %collective-permute-done.11.cross = f32[3,128,128]{2,1,0:T(8,128)S(1)} collective-permute-done((f32[3,128,128]{2,1,0:T(8,128)S(1)}, f32[3,128,128]{2,1,0:T(8,128)S(1)}, u32[]{:S(2)}, u32[]{:S(2)}) %collective-permute-start.11) | collective-permute-done | bytes 196640 | tf_op jit(solution)/shard_map/ppermute | solution.py:333
  32.9 0.9 %collective-permute-start.14 = (f32[2,128,128]{2,1,0:T(8,128)S(1)}, f32[2,128,128]{2,1,0:T(8,128)S(1)}, u32[]{:S(2)}, u32[]{:S(2)}) collective-permute-start(f32[2,128,128]{2,1,0:T(8,128)S(1)} %get-tuple-element.30), channel_id=1, source_target_pairs={{0,16},{1,17},{2,18},{3,19},{4,20},{5,21},{6,22},{7,23},{8,24},{9,... | collective-permute-start | bytes 393224 | tf_op jit(solution)/shard_map/ppermute | solution.py:333
  33.8 1.1 %collective-permute-start.13 = (f32[3,128,128]{2,1,0:T(8,128)S(1)}, f32[3,128,128]{2,1,0:T(8,128)S(1)}, u32[]{:S(2)}, u32[]{:S(2)}) collective-permute-start(f32[3,128,128]{2,1,0:T(8,128)S(1)} %get-tuple-element.29.own), channel_id=1, source_target_pairs={{1,2},{2,1},{3,4},{4,3},{5,6},{6,5},{7,8},{8,7},{9,10},{10,9},{11,... | collective-permute-start | bytes 589832 | tf_op jit(solution)/shard_map/ppermute | solution.py:333
  35.0 0.9 %collective-permute-start.12 = (f32[3,128,128]{2,1,0:T(8,128)S(1)}, f32[3,128,128]{2,1,0:T(8,128)S(1)}, u32[]{:S(2)}, u32[]{:S(2)}) collective-permute-start(f32[3,128,128]{2,1,0:T(8,128)S(1)} %get-tuple-element.29.own), channel_id=1, source_target_pairs={{0,1},{1,0},{2,3},{3,2},{4,5},{5,4},{6,7},{7,6},{8,9},{9,8},{10,11... | collective-permute-start | bytes 589832 | tf_op jit(solution)/shard_map/ppermute | solution.py:333
  36.0 3.0 %collective-permute-done.14.mid_own = f32[2,128,128]{2,1,0:T(8,128)S(1)} collective-permute-done((f32[2,128,128]{2,1,0:T(8,128)S(1)}, f32[2,128,128]{2,1,0:T(8,128)S(1)}, u32[]{:S(2)}, u32[]{:S(2)}) %collective-permute-start.14) | collective-permute-done | bytes 131104 | tf_op jit(solution)/shard_map/ppermute | solution.py:333
  39.0 3.7 %collective-permute-done.16.mid_cross = f32[2,128,128]{2,1,0:T(8,128)S(1)} collective-permute-done((f32[2,128,128]{2,1,0:T(8,128)S(1)}, f32[2,128,128]{2,1,0:T(8,128)S(1)}, u32[]{:S(2)}, u32[]{:S(2)}) %collective-permute-start.16) | collective-permute-done | bytes 131104 | tf_op jit(solution)/shard_map/ppermute | solution.py:333
  43.5 2.8 %collective-permute-start.19 = (f32[3,128,128]{2,1,0:T(8,128)S(1)}, f32[3,128,128]{2,1,0:T(8,128)S(1)}, u32[]{:S(2)}, u32[]{:S(2)}) collective-permute-start(f32[3,128,128]{2,1,0:T(8,128)S(1)} %get-tuple-element.32.own), channel_id=1, source_target_pairs={{1,2},{2,1},{3,4},{4,3},{5,6},{6,5},{7,8},{8,7},{9,10},{10,9},{11,... | collective-permute-start | bytes 589832 | tf_op jit(solution)/shard_map/ppermute | solution.py:333
  48.3 1.6 %collective-permute-done.19.cross = f32[3,128,128]{2,1,0:T(8,128)S(1)} collective-permute-done((f32[3,128,128]{2,1,0:T(8,128)S(1)}, f32[3,128,128]{2,1,0:T(8,128)S(1)}, u32[]{:S(2)}, u32[]{:S(2)}) %collective-permute-start.19) | collective-permute-done | bytes 196640 | tf_op jit(solution)/shard_map/ppermute | solution.py:333
  50.3 2.3 %collective-permute-start.20 = (f32[2,128,128]{2,1,0:T(8,128)S(1)}, f32[2,128,128]{2,1,0:T(8,128)S(1)}, u32[]{:S(2)}, u32[]{:S(2)}) collective-permute-start(f32[2,128,128]{2,1,0:T(8,128)S(1)} %get-tuple-element.34), channel_id=1, source_target_pairs={{0,16},{1,17},{2,18},{3,19},{4,20},{5,21},{6,22},{7,23},{8,24},{9,... | collective-permute-start | bytes 393224 | tf_op jit(solution)/shard_map/ppermute | solution.py:333
  52.6 2.9 %collective-permute-done.20.fixes = f32[2,128,128]{2,1,0:T(8,128)S(1)} collective-permute-done((f32[2,128,128]{2,1,0:T(8,128)S(1)}, f32[2,128,128]{2,1,0:T(8,128)S(1)}, u32[]{:S(2)}, u32[]{:S(2)}) %collective-permute-start.20) | collective-permute-done | bytes 131104 | tf_op jit(solution)/shard_map/ppermute | solution.py:333
  55.5 1.0 %shard_map.66 = f32[3,128,128]{2,1,0:T(8,128)} custom-call(f32[3,128,128]{2,1,0:T(8,128)S(1)} %get-tuple-element.33.smooth, f32[2,128,128]{2,1,0:T(8,128)S(1)} %collective-permute-done.20.fixes, bf16[768,256]{1,0:T(8,128)(2,1)S(1)} %get-tuple-element.27.prolong, f32[3,128,128]{2,1,0:T(8,128)S(1)} %shard_map.60.own.rest_0_), custom_call_target="tpu_custom_call" | custom-call | tf_op jit(solution)/shard_map/pallas_call | solution.py:311
  (40 shorter events, 8.7 us)
Async XLA Ops:
  1.4 6.1 %collective-permute-start.2 = (f32[2,128,128]{2,1,0:T(8,128)S(1)}, f32[2,128,128]{2,1,0:T(8,128)S(1)}, u32[]{:S(2)}, u32[]{:S(2)}) collective-permute-start(f32[2,128,128]{2,1,0:T(8,128)S(1)} %get-tuple-element.22), channel_id=1, source_target_pairs={{0,16},{1,17},{2,18},{3,19},{4,20},{5,21},{6,22},{7,23},{8,24},{9,... | collective-permute-start | bytes 393224 | tf_op jit(solution)/shard_map/ppermute | solution.py:333
  4.1 9.1 %collective-permute-start.1 = (f32[3,128,128]{2,1,0:T(8,128)S(1)}, f32[3,128,128]{2,1,0:T(8,128)S(1)}, u32[]{:S(2)}, u32[]{:S(2)}) collective-permute-start(f32[3,128,128]{2,1,0:T(8,128)S(1)} %get-tuple-element.21.own.down_own), channel_id=1, source_target_pairs={{1,2},{2,1},{3,4},{4,3},{5,6},{6,5},{7,8},{8,7},{9,10},{10,9},{11,... | collective-permute-start | bytes 589832 | tf_op jit(solution)/shard_map/ppermute | solution.py:333
  4.1 9.0 %collective-permute-start = (f32[3,128,128]{2,1,0:T(8,128)S(1)}, f32[3,128,128]{2,1,0:T(8,128)S(1)}, u32[]{:S(2)}, u32[]{:S(2)}) collective-permute-start(f32[3,128,128]{2,1,0:T(8,128)S(1)} %get-tuple-element.21.own.down_own), channel_id=1, source_target_pairs={{0,1},{1,0},{2,3},{3,2},{4,5},{5,4},{6,7},{7,6},{8,9},{9,8},{10,11... | collective-permute-start | bytes 589832 | tf_op jit(solution)/shard_map/ppermute | solution.py:333
  5.7 7.4 %collective-permute-start.4 = (f32[2,128,128]{2,1,0:T(8,128)S(1)}, f32[2,128,128]{2,1,0:T(8,128)S(1)}, u32[]{:S(2)}, u32[]{:S(2)}) collective-permute-start(f32[2,128,128]{2,1,0:T(8,128)S(1)} %get-tuple-element.22), channel_id=1, source_target_pairs={{0,16},{1,18},{2,17},{3,20},{4,19},{5,22},{6,21},{7,24},{8,23},{9,... | collective-permute-start | bytes 393224 | tf_op jit(solution)/shard_map/ppermute | solution.py:333
  7.6 5.6 %collective-permute-start.3 = (f32[2,128,128]{2,1,0:T(8,128)S(1)}, f32[2,128,128]{2,1,0:T(8,128)S(1)}, u32[]{:S(2)}, u32[]{:S(2)}) collective-permute-start(f32[2,128,128]{2,1,0:T(8,128)S(1)} %collective-permute-done.2.mid_own), channel_id=1, source_target_pairs={{0,1},{1,0},{2,3},{3,2},{4,5},{5,4},{6,7},{7,6},{8,9},{9,8},{10,11... | collective-permute-start | bytes 393224 | tf_op jit(solution)/shard_map/ppermute | solution.py:333
  13.9 6.4 %copy-start = (f32[1,1,3,2,128,128]{5,4,3,2,1,0:T(8,128)S(1)}, f32[1,1,3,2,128,128]{5,4,3,2,1,0:T(8,128)}, u32[]{:S(2)}) copy-start(f32[1,1,3,2,128,128]{5,4,3,2,1,0:T(8,128)} %param.8) | copy-start | bytes 1179652
  13.9 6.4 %collective-permute-start.7 = (f32[3,128,128]{2,1,0:T(8,128)S(1)}, f32[3,128,128]{2,1,0:T(8,128)S(1)}, u32[]{:S(2)}, u32[]{:S(2)}) collective-permute-start(f32[3,128,128]{2,1,0:T(8,128)S(1)} %get-tuple-element.24.own), channel_id=1, source_target_pairs={{1,2},{2,1},{3,4},{4,3},{5,6},{6,5},{7,8},{8,7},{9,10},{10,9},{11,... | collective-permute-start | bytes 589832 | tf_op jit(solution)/shard_map/ppermute | solution.py:333
  16.7 1.5 %collective-permute-start.5 = (f32[2,128,128]{2,1,0:T(8,128)S(1)}, f32[2,128,128]{2,1,0:T(8,128)S(1)}, u32[]{:S(2)}, u32[]{:S(2)}) collective-permute-start(f32[2,128,128]{2,1,0:T(8,128)S(1)} %slice.18), channel_id=1, source_target_pairs={{0,1},{1,0},{2,3},{3,2},{4,5},{5,4},{6,7},{7,6},{8,9},{9,8},{10,11... | collective-permute-start | bytes 393224 | tf_op jit(solution)/shard_map/ppermute | solution.py:333
  16.8 1.4 %collective-permute-start.6 = (f32[1,128,128]{2,1,0:T(8,128)S(1)}, f32[1,128,128]{2,1,0:T(8,128)S(1)}, u32[]{:S(2)}, u32[]{:S(2)}) collective-permute-start(f32[1,128,128]{2,1,0:T(8,128)S(1)} %slice.19), channel_id=1, source_target_pairs={{0,1},{1,0},{2,3},{3,2},{4,5},{5,4},{6,7},{7,6},{8,9},{9,8},{10,11... | collective-permute-start | bytes 196616 | tf_op jit(solution)/shard_map/ppermute | solution.py:333
  20.7 5.2 %collective-permute-start.8 = (f32[2,128,128]{2,1,0:T(8,128)S(1)}, f32[2,128,128]{2,1,0:T(8,128)S(1)}, u32[]{:S(2)}, u32[]{:S(2)}) collective-permute-start(f32[2,128,128]{2,1,0:T(8,128)S(1)} %get-tuple-element.26), channel_id=1, source_target_pairs={{0,16},{1,17},{2,18},{3,19},{4,20},{5,21},{6,22},{7,23},{8,24},{9,... | collective-permute-start | bytes 393224 | tf_op jit(solution)/shard_map/ppermute | solution.py:333
  26.0 6.0 %copy-start.1 = (f32[1,1,3,128,128]{4,3,2,1,0:T(8,128)S(1)}, f32[1,1,3,128,128]{4,3,2,1,0:T(8,128)}, u32[]{:S(2)}) copy-start(f32[1,1,3,128,128]{4,3,2,1,0:T(8,128)} %param.5) | copy-start | bytes 589828
  26.3 5.7 %collective-permute-start.11 = (f32[3,128,128]{2,1,0:T(8,128)S(1)}, f32[3,128,128]{2,1,0:T(8,128)S(1)}, u32[]{:S(2)}, u32[]{:S(2)}) collective-permute-start(f32[3,128,128]{2,1,0:T(8,128)S(1)} %shard_map.60.own.rest_0_), channel_id=1, source_target_pairs={{1,2},{2,1},{3,4},{4,3},{5,6},{6,5},{7,8},{8,7},{9,10},{10,9},{11,... | collective-permute-start | bytes 589832 | tf_op jit(solution)/shard_map/ppermute | solution.py:333
  28.1 1.5 %collective-permute-start.9 = (f32[2,128,128]{2,1,0:T(8,128)S(1)}, f32[2,128,128]{2,1,0:T(8,128)S(1)}, u32[]{:S(2)}, u32[]{:S(2)}) collective-permute-start(f32[2,128,128]{2,1,0:T(8,128)S(1)} %slice.24), channel_id=1, source_target_pairs={{0,1},{1,0},{2,3},{3,2},{4,5},{5,4},{6,7},{7,6},{8,9},{9,8},{10,11... | collective-permute-start | bytes 393224 | tf_op jit(solution)/shard_map/ppermute | solution.py:333
  28.2 1.4 %collective-permute-start.10 = (f32[1,128,128]{2,1,0:T(8,128)S(1)}, f32[1,128,128]{2,1,0:T(8,128)S(1)}, u32[]{:S(2)}, u32[]{:S(2)}) collective-permute-start(f32[1,128,128]{2,1,0:T(8,128)S(1)} %slice.25), channel_id=1, source_target_pairs={{0,1},{1,0},{2,3},{3,2},{4,5},{5,4},{6,7},{7,6},{8,9},{9,8},{10,11... | collective-permute-start | bytes 196616 | tf_op jit(solution)/shard_map/ppermute | solution.py:333
  32.9 6.1 %collective-permute-start.14 = (f32[2,128,128]{2,1,0:T(8,128)S(1)}, f32[2,128,128]{2,1,0:T(8,128)S(1)}, u32[]{:S(2)}, u32[]{:S(2)}) collective-permute-start(f32[2,128,128]{2,1,0:T(8,128)S(1)} %get-tuple-element.30), channel_id=1, source_target_pairs={{0,16},{1,17},{2,18},{3,19},{4,20},{5,21},{6,22},{7,23},{8,24},{9,... | collective-permute-start | bytes 393224 | tf_op jit(solution)/shard_map/ppermute | solution.py:333
  33.8 8.9 %collective-permute-start.13 = (f32[3,128,128]{2,1,0:T(8,128)S(1)}, f32[3,128,128]{2,1,0:T(8,128)S(1)}, u32[]{:S(2)}, u32[]{:S(2)}) collective-permute-start(f32[3,128,128]{2,1,0:T(8,128)S(1)} %get-tuple-element.29.own), channel_id=1, source_target_pairs={{1,2},{2,1},{3,4},{4,3},{5,6},{6,5},{7,8},{8,7},{9,10},{10,9},{11,... | collective-permute-start | bytes 589832 | tf_op jit(solution)/shard_map/ppermute | solution.py:333
  35.0 7.7 %collective-permute-start.12 = (f32[3,128,128]{2,1,0:T(8,128)S(1)}, f32[3,128,128]{2,1,0:T(8,128)S(1)}, u32[]{:S(2)}, u32[]{:S(2)}) collective-permute-start(f32[3,128,128]{2,1,0:T(8,128)S(1)} %get-tuple-element.29.own), channel_id=1, source_target_pairs={{0,1},{1,0},{2,3},{3,2},{4,5},{5,4},{6,7},{7,6},{8,9},{9,8},{10,11... | collective-permute-start | bytes 589832 | tf_op jit(solution)/shard_map/ppermute | solution.py:333
  35.9 6.8 %collective-permute-start.16 = (f32[2,128,128]{2,1,0:T(8,128)S(1)}, f32[2,128,128]{2,1,0:T(8,128)S(1)}, u32[]{:S(2)}, u32[]{:S(2)}) collective-permute-start(f32[2,128,128]{2,1,0:T(8,128)S(1)} %get-tuple-element.30), channel_id=1, source_target_pairs={{0,16},{1,18},{2,17},{3,20},{4,19},{5,22},{6,21},{7,24},{8,23},{9,... | collective-permute-start | bytes 393224 | tf_op jit(solution)/shard_map/ppermute | solution.py:333
  39.0 3.7 %collective-permute-start.15 = (f32[2,128,128]{2,1,0:T(8,128)S(1)}, f32[2,128,128]{2,1,0:T(8,128)S(1)}, u32[]{:S(2)}, u32[]{:S(2)}) collective-permute-start(f32[2,128,128]{2,1,0:T(8,128)S(1)} %collective-permute-done.14.mid_own), channel_id=1, source_target_pairs={{0,1},{1,0},{2,3},{3,2},{4,5},{5,4},{6,7},{7,6},{8,9},{9,8},{10,11... | collective-permute-start | bytes 393224 | tf_op jit(solution)/shard_map/ppermute | solution.py:333
  43.5 6.4 %collective-permute-start.19 = (f32[3,128,128]{2,1,0:T(8,128)S(1)}, f32[3,128,128]{2,1,0:T(8,128)S(1)}, u32[]{:S(2)}, u32[]{:S(2)}) collective-permute-start(f32[3,128,128]{2,1,0:T(8,128)S(1)} %get-tuple-element.32.own), channel_id=1, source_target_pairs={{1,2},{2,1},{3,4},{4,3},{5,6},{6,5},{7,8},{8,7},{9,10},{10,9},{11,... | collective-permute-start | bytes 589832 | tf_op jit(solution)/shard_map/ppermute | solution.py:333
  46.3 1.5 %collective-permute-start.17 = (f32[2,128,128]{2,1,0:T(8,128)S(1)}, f32[2,128,128]{2,1,0:T(8,128)S(1)}, u32[]{:S(2)}, u32[]{:S(2)}) collective-permute-start(f32[2,128,128]{2,1,0:T(8,128)S(1)} %slice.22), channel_id=1, source_target_pairs={{0,1},{1,0},{2,3},{3,2},{4,5},{5,4},{6,7},{7,6},{8,9},{9,8},{10,11... | collective-permute-start | bytes 393224 | tf_op jit(solution)/shard_map/ppermute | solution.py:333
  46.4 1.4 %collective-permute-start.18 = (f32[1,128,128]{2,1,0:T(8,128)S(1)}, f32[1,128,128]{2,1,0:T(8,128)S(1)}, u32[]{:S(2)}, u32[]{:S(2)}) collective-permute-start(f32[1,128,128]{2,1,0:T(8,128)S(1)} %slice.23), channel_id=1, source_target_pairs={{0,1},{1,0},{2,3},{3,2},{4,5},{5,4},{6,7},{7,6},{8,9},{9,8},{10,11... | collective-permute-start | bytes 196616 | tf_op jit(solution)/shard_map/ppermute | solution.py:333
  50.3 5.2 %collective-permute-start.20 = (f32[2,128,128]{2,1,0:T(8,128)S(1)}, f32[2,128,128]{2,1,0:T(8,128)S(1)}, u32[]{:S(2)}, u32[]{:S(2)}) collective-permute-start(f32[2,128,128]{2,1,0:T(8,128)S(1)} %get-tuple-element.34), channel_id=1, source_target_pairs={{0,16},{1,17},{2,18},{3,19},{4,20},{5,21},{6,22},{7,23},{8,24},{9,... | collective-permute-start | bytes 393224 | tf_op jit(solution)/shard_map/ppermute | solution.py:333

commit v3 on v2

--- a/solution.py
+++ b/solution.py
@@ -139,7 +139,13 @@
     return jnp.concatenate(blocks, axis=0)
 
 
-def restrict_kernel(targets_in, rhs_in, links_in, mids, payload, restrict, targets, links, sems):
+def store_mids(value, mids, skewed):
+    mids[...] = value.reshape(mids.shape)
+    skewed[:value.shape[0], :] = value
+    skewed[value.shape[0]:, :] = jnp.zeros_like(skewed[value.shape[0]:, :])
+
+
+def restrict_kernel(targets_in, rhs_in, links_in, mids, skewed, payload, restrict, targets, links, sems):
     size = payload.shape[-1]
     slots = payload.shape[0]
     fetch_targets = pltpu.make_async_copy(targets_in.at[0, 0], targets, sems.at[0])
@@ -161,7 +167,7 @@
                 restrict[(2 + k) * size:(3 + k) * size, s * size:(s + 1) * size] = low
         fetch_rhs.wait()
         right = split_columns(payload[...].reshape(slots * size, size))
-        mids[...] = product(restrict[...], right).reshape(mids.shape)
+        store_mids(product(restrict[...], right), mids, skewed)
 
     @pl.when(lax.axis_index("lvl") != 0)
     def _():
@@ -171,6 +177,7 @@
         payload[1] = links[2, 0]
         payload[2] = jnp.zeros_like(payload[2])
         mids[...] = jnp.zeros_like(mids)
+        skewed[...] = jnp.zeros_like(skewed)
 
 
 def operator_kernel(columns_in, targets_in, links_in, tiles_in, matrix, prolong, columns, targets, links, tiles, gathered, sems):
@@ -235,19 +242,32 @@
     return [mid[0], coarse, mid[1]]
 
 
-def first_kernel(matrix, own, core, cross, down_own, down_core, down_cross, mid_own, mid_core, mid_cross, level, first, field):
-    @pl.when(lax.axis_index("lvl") == 0)
-    def _():
-        field[...] = joined(blocks_of(own, core, cross))
+def first_near_kernel(matrix, own, core, core_last, down_own, down_core, mid_own, mid_core, mid_core_last, level, part, field):
+    @pl.when(lax.axis_index("lvl") == 0)
+    def _():
+        field[...] = joined(blocks_of(own, core, core_last))
         level[...] = own[...]
 
     @pl.when(lax.axis_index("lvl") != 0)
     def _():
-        here = level_blocks(down_own, mid_own)
-        field[...] = joined(here + level_blocks(down_core, mid_core) + level_blocks(down_cross, mid_cross))
+        here = level_blocks(down_own, blocks_of(mid_own))
+        field[...] = joined(here + level_blocks(down_core, blocks_of(mid_core, mid_core_last)))
         level[...] = stacked(*here).reshape(level.shape)
 
-    first[...] = product(matrix[...], field[...]).reshape(first.shape)
+    part[...] = near(matrix, field[...]).reshape(part.shape)
+
+
+def first_far_kernel(matrix, part, cross, down_cross, skewed, first, field):
+    @pl.when(lax.axis_index("lvl") == 0)
+    def _():
+        field[...] = joined(blocks_of(cross))
+
+    @pl.when(lax.axis_index("lvl") != 0)
+    def _():
+        size = cross.shape[-1]
+        field[...] = joined(level_blocks(down_cross, (skewed[:size, :], skewed[size:2 * size, :])))
+
+    first[...] = part[...] + far(matrix, field[...]).reshape(first.shape)
 
 
 def near_kernel(matrix, own, core, core_last, part):
@@ -291,17 +311,18 @@
         result[...] = smooth[...]
 
 
-def residual_kernel(matrix, part, cross, rhs, restrict, resid, mids):
+def residual_kernel(matrix, part, cross, rhs, restrict, resid, mids, skewed):
     @pl.when(lax.axis_index("lvl") == 0)
     def _():
         value = rhs[...] - (part[...] + far(matrix, joined(blocks_of(cross))).reshape(rhs.shape))
         resid[...] = value
-        mids[...] = product(restrict[...], joined([value[s] for s in range(value.shape[0])])).reshape(mids.shape)
+        store_mids(product(restrict[...], joined([value[s] for s in range(value.shape[0])])), mids, skewed)
 
     @pl.when(lax.axis_index("lvl") != 0)
     def _():
         resid[...] = jnp.zeros_like(resid)
         mids[...] = jnp.zeros_like(mids)
+        skewed[...] = jnp.zeros_like(skewed)
 
 
 def call(kernel, outs, args, anywhere=0, scratch=(), aliases={}):
@@ -329,7 +350,10 @@
     for end, beside in ((0, 1), (rows - 1, rows - 2)):
         fine += [(end, rows + end), (rows + end, rows + beside), (rows + beside, end)]
     level = [(l * rows + r, (1 - l) * rows + r) for l in range(2) for r in range(rows)]
-    skew = [(r, rows + across[r]) for r in range(rows)] + [(rows + r, r) for r in range(rows)]
+    skew = [(r, rows + across[r]) for r in range(1, rows - 1)]
+    skew += [(rows + r, r) for r in range(rows) if r not in (1, rows - 2)]
+    for end, beside in ((0, 1), (rows - 1, rows - 2)):
+        skew += [(end, beside), (rows + beside, rows + end)]
     return tuple((lambda x, pairs=pairs: lax.ppermute(x, ("lvl", "row"), pairs)) for pairs in (core, cross, fine, level, skew))
 
 
@@ -340,9 +364,10 @@
     blocks, pair = (right.shape, F32), ((2, size, width), F32)
     big = slots * size
     codes, goals = jnp.swapaxes(op_cols, 1, 2), jnp.swapaxes(level_links, 2, 3)
-    mids, payload, restrict = call(
+    long = ((2 * size + 8, width), F32)
+    mids, skewed, payload, restrict = call(
         restrict_kernel,
-        [pair, blocks, ((4 * size, big), BF16)],
+        [pair, long, blocks, ((4 * size, big), BF16)],
         [goals, right, links],
         anywhere=3,
         scratch=[
@@ -356,10 +381,10 @@
         if cycle > 0:
             result_cross = cross(result)
             (part,) = call(near_kernel, [blocks], [matrix, result, core(result[:-1]), core(result[-1:])])
-            payload, mids = call(residual_kernel, [blocks, pair], [matrix, part, result_cross, right, restrict])
-        mid_here, mid_cross = level(mids), skew(mids)
-        around = (payload, core(payload), cross(payload) if cycle == 0 else fine(payload))
-        mid_core = core(mid_here)
+            payload, mids, skewed = call(residual_kernel, [blocks, pair, long], [matrix, part, result_cross, right, restrict])
+        mid_here, mid_cross = level(mids), skew(skewed)
+        around = (payload, core(payload[:-1]), core(payload[-1:]), cross(payload) if cycle == 0 else fine(payload))
+        mid_core = core(mid_here[:1]), core(mid_here[1:])
         if cycle == 0:
             matrix, prolong = call(
                 operator_kernel,
@@ -375,12 +400,18 @@
                     pltpu.SemaphoreType.DMA((3 + slots,)),
                 ],
             )
-            down = around
-        level_resid, first = call(
-            first_kernel,
+            down = around[0], around[1], around[3]
+        level_resid, part = call(
+            first_near_kernel,
             [blocks, blocks],
-            [matrix, *around, *down, mid_here, mid_core, mid_cross],
-            scratch=[pltpu.VMEM((3 * big, 2 * width), BF16)],
+            [matrix, *around[:3], *down[:2], mid_here, *mid_core],
+            scratch=[pltpu.VMEM((2 * big, 2 * width), BF16)],
+        )
+        (first,) = call(
+            first_far_kernel,
+            [blocks],
+            [matrix, part, around[3], down[2], mid_cross],
+            scratch=[pltpu.VMEM((big, 2 * width), BF16)],
         )
         first_cross = cross(first)
         (part,) = call(near_kernel, [blocks], [matrix, first, core(first[:-1]), core(first[-1:])])

time: 56.6 us -> 54.5 us (0.963)
  waiting for transfers between devices: 25.3 us -> 21.6 us
  starting transfers between devices: 22 us -> 23 us
    ppermute x21 -> x25, waiting for transfers between devices: 25.3 us -> 21.6 us  [swaps(): lax.ppermute(x, ('lvl', 'row'), pairs)]
    ppermute x21 -> x25, starting transfers between devices: 22 us -> 23 us  [swaps(): lax.ppermute(x, ('lvl', 'row'), pairs)]
    pallas_call x12 -> x14, Pallas kernels: 8.92 us -> 9.23 us  [call(): pl.pallas_call(kernel, out_shape=[jax.ShapeDtypeStruct(shape, dtype) for...]
  transfers between devices with their start and end apart: 21 -> 25, of which waited for: 12 -> 13; matrix products, arithmetic and copies ran while one was open for 0% -> 0% of each run, Pallas kernels for 6% -> 8%
where the time goes in v3:
time: 54.5 us; the launch traced here: 54.1 us
  starting transfers between devices  23 us (42%)
  waiting for transfers between devices  21.6 us (40%)
  Pallas kernels  9.23 us (17%)
    ppermute x25, starting transfers between devices, swaps(): lax.ppermute(x, ('lvl', 'row'), pairs)  23 us
    ppermute x25, waiting for transfers between devices, swaps(): lax.ppermute(x, ('lvl', 'row'), pairs)  21.6 us
    pallas_call x14, Pallas kernels, call(): pl.pallas_call(kernel, out_shape=[jax.ShapeDtypeStruct(shape, dtype) for...  9.23 us
  transfers between devices with their start and end apart: 25, of which 13 were waited for; matrix products, arithmetic and copies ran while one was open for 0% of the time, Pallas kernels for 8%

profile of v3, /device:TPU:0, one launch (start us, length us, event | category | flops | bytes accessed | tf_op | source)
XLA Modules:
  0.0 54.1 jit_solution(8283869188490535873)
XLA Ops:
  0.0 1.4 %shard_map.56 = (f32[2,128,128]{2,1,0:T(8,128)S(1)}, f32[264,128]{1,0:T(8,128)S(1)}, f32[3,128,128]{2,1,0:T(8,128)S(1)}, bf16[512,384]{1,0:T(8,128)(2,1)S(1)}) custom-call(s32[1,1,2,3]{3,2,1,0:T(2,128)} %bitcast.13, f32[3,128,128]{2,1,0:T(8,128)} %bitcast.10, f32[3,2,128,128]{3,2,1,0:T(8,128)} %bitcast.6), custom_call_target="tpu_custom_call" | custom-call | tf_op jit(solution)/shard_map/pallas_call | solution.py:332
  1.4 2.7 %collective-permute-start.2 = (f32[2,128,128]{2,1,0:T(8,128)S(1)}, f32[2,128,128]{2,1,0:T(8,128)S(1)}, u32[]{:S(2)}, u32[]{:S(2)}) collective-permute-start(f32[2,128,128]{2,1,0:T(8,128)S(1)} %get-tuple-element.24), channel_id=1, source_target_pairs={{0,16},{1,17},{2,18},{3,19},{4,20},{5,21},{6,22},{7,23},{8,24},{9,... | collective-permute-start | bytes 393224 | tf_op jit(solution)/shard_map/ppermute | solution.py:357
  4.1 1.6 %collective-permute-start.1 = (f32[1,128,128]{2,1,0:T(8,128)S(1)}, f32[1,128,128]{2,1,0:T(8,128)S(1)}, u32[]{:S(2)}, u32[]{:S(2)}) collective-permute-start(f32[1,128,128]{2,1,0:T(8,128)S(1)} %slice.43), channel_id=1, source_target_pairs={{0,1},{1,0},{2,3},{3,2},{4,5},{5,4},{6,7},{7,6},{8,9},{9,8},{10,11... | collective-permute-start | bytes 196616 | tf_op jit(solution)/shard_map/ppermute | solution.py:357
  6.3 1.3 %collective-permute-done.2.mid_own = f32[2,128,128]{2,1,0:T(8,128)S(1)} collective-permute-done((f32[2,128,128]{2,1,0:T(8,128)S(1)}, f32[2,128,128]{2,1,0:T(8,128)S(1)}, u32[]{:S(2)}, u32[]{:S(2)}) %collective-permute-start.2) | collective-permute-done | bytes 131104 | tf_op jit(solution)/shard_map/ppermute | solution.py:357
  8.2 1.7 %shard_map.55 = (bf16[768,1152]{1,0:T(8,128)(2,1)S(1)}, bf16[768,256]{1,0:T(8,128)(2,1)S(1)}) custom-call(s32[1,3,1,7]{3,2,1,0:T(1,128)} %bitcast.15, s32[1,1,2,3]{3,2,1,0:T(2,128)} %bitcast.14, f32[3,2,128,128]{3,2,1,0:T(8,128)} %bitcast.7, f32[3,7,128,128]{3,2,1,0:T(8,128)} %bitcast.12), custom_call_target="tpu_custom_call" | custom-call | tf_op jit(solution)/shard_map/pallas_call | solution.py:332
  11.6 1.4 %collective-permute-start.9 = (f32[3,128,128]{2,1,0:T(8,128)S(1)}, f32[3,128,128]{2,1,0:T(8,128)S(1)}, u32[]{:S(2)}, u32[]{:S(2)}) collective-permute-start(f32[3,128,128]{2,1,0:T(8,128)S(1)} %shard_map.58.own), channel_id=1, source_target_pairs={{1,2},{2,1},{3,4},{4,3},{5,6},{6,5},{7,8},{8,7},{9,10},{10,9},{11,... | collective-permute-start | bytes 589832 | tf_op jit(solution)/shard_map/ppermute | solution.py:357
  13.0 0.9 %collective-permute-start.7 = (f32[2,128,128]{2,1,0:T(8,128)S(1)}, f32[2,128,128]{2,1,0:T(8,128)S(1)}, u32[]{:S(2)}, u32[]{:S(2)}) collective-permute-start(f32[2,128,128]{2,1,0:T(8,128)S(1)} %slice.58), channel_id=1, source_target_pairs={{0,1},{1,0},{2,3},{3,2},{4,5},{5,4},{6,7},{7,6},{8,9},{9,8},{10,11... | collective-permute-start | bytes 393224 | tf_op jit(solution)/shard_map/ppermute | solution.py:357
  14.1 1.2 %collective-permute-done.8.core_last = f32[1,128,128]{2,1,0:T(8,128)S(1)} collective-permute-done((f32[1,128,128]{2,1,0:T(8,128)S(1)}, f32[1,128,128]{2,1,0:T(8,128)S(1)}, u32[]{:S(2)}, u32[]{:S(2)}) %collective-permute-start.8) | collective-permute-done | bytes 65568 | tf_op jit(solution)/shard_map/ppermute | solution.py:357
  15.7 1.6 %collective-permute-done.9.cross = f32[3,128,128]{2,1,0:T(8,128)S(1)} collective-permute-done((f32[3,128,128]{2,1,0:T(8,128)S(1)}, f32[3,128,128]{2,1,0:T(8,128)S(1)}, u32[]{:S(2)}, u32[]{:S(2)}) %collective-permute-start.9) | collective-permute-done | bytes 196640 | tf_op jit(solution)/shard_map/ppermute | solution.py:357
  17.7 2.1 %collective-permute-start.10 = (f32[2,128,128]{2,1,0:T(8,128)S(1)}, f32[2,128,128]{2,1,0:T(8,128)S(1)}, u32[]{:S(2)}, u32[]{:S(2)}) collective-permute-start(f32[2,128,128]{2,1,0:T(8,128)S(1)} %get-tuple-element.29), channel_id=1, source_target_pairs={{0,16},{1,17},{2,18},{3,19},{4,20},{5,21},{6,22},{7,23},{8,24},{9,... | collective-permute-start | bytes 393224 | tf_op jit(solution)/shard_map/ppermute | solution.py:357
  19.8 2.9 %collective-permute-done.10.fixes = f32[2,128,128]{2,1,0:T(8,128)S(1)} collective-permute-done((f32[2,128,128]{2,1,0:T(8,128)S(1)}, f32[2,128,128]{2,1,0:T(8,128)S(1)}, u32[]{:S(2)}, u32[]{:S(2)}) %collective-permute-start.10) | collective-permute-done | bytes 131104 | tf_op jit(solution)/shard_map/ppermute | solution.py:357
  23.0 1.8 %collective-permute-start.13 = (f32[3,128,128]{2,1,0:T(8,128)S(1)}, f32[3,128,128]{2,1,0:T(8,128)S(1)}, u32[]{:S(2)}, u32[]{:S(2)}) collective-permute-start(f32[3,128,128]{2,1,0:T(8,128)S(1)} %shard_map.61.own.rest_0_), channel_id=1, source_target_pairs={{1,2},{2,1},{3,4},{4,3},{5,6},{6,5},{7,8},{8,7},{9,10},{10,9},{11,... | collective-permute-start | bytes 589832 | tf_op jit(solution)/shard_map/ppermute | solution.py:357
  24.9 3.3 %collective-permute-start.11 = (f32[2,128,128]{2,1,0:T(8,128)S(1)}, f32[2,128,128]{2,1,0:T(8,128)S(1)}, u32[]{:S(2)}, u32[]{:S(2)}) collective-permute-start(f32[2,128,128]{2,1,0:T(8,128)S(1)} %slice.60), channel_id=1, source_target_pairs={{0,1},{1,0},{2,3},{3,2},{4,5},{5,4},{6,7},{7,6},{8,9},{9,8},{10,11... | collective-permute-start | bytes 393224 | tf_op jit(solution)/shard_map/ppermute | solution.py:357
  28.2 1.2 %collective-permute-done.12.core_last = f32[1,128,128]{2,1,0:T(8,128)S(1)} collective-permute-done((f32[1,128,128]{2,1,0:T(8,128)S(1)}, f32[1,128,128]{2,1,0:T(8,128)S(1)}, u32[]{:S(2)}, u32[]{:S(2)}) %collective-permute-start.12) | collective-permute-done | bytes 65568 | tf_op jit(solution)/shard_map/ppermute | solution.py:357
  30.8 1.0 %collective-permute-start.16 = (f32[2,128,128]{2,1,0:T(8,128)S(1)}, f32[2,128,128]{2,1,0:T(8,128)S(1)}, u32[]{:S(2)}, u32[]{:S(2)}) collective-permute-start(f32[2,128,128]{2,1,0:T(8,128)S(1)} %get-tuple-element.33), channel_id=1, source_target_pairs={{0,16},{1,17},{2,18},{3,19},{4,20},{5,21},{6,22},{7,23},{8,24},{9,... | collective-permute-start | bytes 393224 | tf_op jit(solution)/shard_map/ppermute | solution.py:357
  31.8 1.2 %collective-permute-start.19 = (f32[3,128,128]{2,1,0:T(8,128)S(1)}, f32[3,128,128]{2,1,0:T(8,128)S(1)}, u32[]{:S(2)}, u32[]{:S(2)}) collective-permute-start(f32[3,128,128]{2,1,0:T(8,128)S(1)} %get-tuple-element.32.own), channel_id=1, source_target_pairs={{1,2},{2,1},{3,4},{4,3},{5,6},{6,5},{7,8},{8,7},{9,10},{10,9},{11,... | collective-permute-start | bytes 589832 | tf_op jit(solution)/shard_map/ppermute | solution.py:357
  33.0 2.3 %collective-permute-start.15 = (f32[1,128,128]{2,1,0:T(8,128)S(1)}, f32[1,128,128]{2,1,0:T(8,128)S(1)}, u32[]{:S(2)}, u32[]{:S(2)}) collective-permute-start(f32[1,128,128]{2,1,0:T(8,128)S(1)} %slice.51), channel_id=1, source_target_pairs={{0,1},{1,0},{2,3},{3,2},{4,5},{5,4},{6,7},{7,6},{8,9},{9,8},{10,11... | collective-permute-start | bytes 196616 | tf_op jit(solution)/shard_map/ppermute | solution.py:357
  35.8 1.0 %collective-permute-done.16.mid_own = f32[2,128,128]{2,1,0:T(8,128)S(1)} collective-permute-done((f32[2,128,128]{2,1,0:T(8,128)S(1)}, f32[2,128,128]{2,1,0:T(8,128)S(1)}, u32[]{:S(2)}, u32[]{:S(2)}) %collective-permute-start.16) | collective-permute-done | bytes 131104 | tf_op jit(solution)/shard_map/ppermute | solution.py:357
  39.0 1.9 %collective-permute-done.20.skewed = f32[264,128]{1,0:T(8,128)S(1)} collective-permute-done((f32[264,128]{1,0:T(8,128)S(1)}, f32[264,128]{1,0:T(8,128)S(1)}, u32[]{:S(2)}, u32[]{:S(2)}) %collective-permute-start.20) | collective-permute-done | bytes 135200 | tf_op jit(solution)/shard_map/ppermute | solution.py:357
  41.6 1.3 %collective-permute-start.21 = (f32[2,128,128]{2,1,0:T(8,128)S(1)}, f32[2,128,128]{2,1,0:T(8,128)S(1)}, u32[]{:S(2)}, u32[]{:S(2)}) collective-permute-start(f32[2,128,128]{2,1,0:T(8,128)S(1)} %slice.64), channel_id=1, source_target_pairs={{0,1},{1,0},{2,3},{3,2},{4,5},{5,4},{6,7},{7,6},{8,9},{9,8},{10,11... | collective-permute-start | bytes 393224 | tf_op jit(solution)/shard_map/ppermute | solution.py:357
  43.0 1.2 %collective-permute-done.22.core_last = f32[1,128,128]{2,1,0:T(8,128)S(1)} collective-permute-done((f32[1,128,128]{2,1,0:T(8,128)S(1)}, f32[1,128,128]{2,1,0:T(8,128)S(1)}, u32[]{:S(2)}, u32[]{:S(2)}) %collective-permute-start.22) | collective-permute-done | bytes 65568 | tf_op jit(solution)/shard_map/ppermute | solution.py:357
  44.7 2.3 %collective-permute-done.23.cross = f32[3,128,128]{2,1,0:T(8,128)S(1)} collective-permute-done((f32[3,128,128]{2,1,0:T(8,128)S(1)}, f32[3,128,128]{2,1,0:T(8,128)S(1)}, u32[]{:S(2)}, u32[]{:S(2)}) %collective-permute-start.23) | collective-permute-done | bytes 196640 | tf_op jit(solution)/shard_map/ppermute | solution.py:357
  47.9 5.3 %collective-permute-done.24.fixes = f32[2,128,128]{2,1,0:T(8,128)S(1)} collective-permute-done((f32[2,128,128]{2,1,0:T(8,128)S(1)}, f32[2,128,128]{2,1,0:T(8,128)S(1)}, u32[]{:S(2)}, u32[]{:S(2)}) %collective-permute-start.24) | collective-permute-done | bytes 131104 | tf_op jit(solution)/shard_map/ppermute | solution.py:357
  53.2 0.9 %shard_map.68 = f32[3,128,128]{2,1,0:T(8,128)} custom-call(f32[3,128,128]{2,1,0:T(8,128)S(1)} %get-tuple-element.37.smooth, f32[2,128,128]{2,1,0:T(8,128)S(1)} %collective-permute-done.24.fixes, bf16[768,256]{1,0:T(8,128)(2,1)S(1)} %get-tuple-element.30.prolong, f32[3,128,128]{2,1,0:T(8,128)S(1)} %shard_map.61.own.rest_0_), custom_call_target="tpu_custom_call" | custom-call | tf_op jit(solution)/shard_map/pallas_call | solution.py:332
  (56 shorter events, 10.6 us)
Async XLA Ops:
  1.4 6.2 %collective-permute-start.2 = (f32[2,128,128]{2,1,0:T(8,128)S(1)}, f32[2,128,128]{2,1,0:T(8,128)S(1)}, u32[]{:S(2)}, u32[]{:S(2)}) collective-permute-start(f32[2,128,128]{2,1,0:T(8,128)S(1)} %get-tuple-element.24), channel_id=1, source_target_pairs={{0,16},{1,17},{2,18},{3,19},{4,20},{5,21},{6,22},{7,23},{8,24},{9,... | collective-permute-start | bytes 393224 | tf_op jit(solution)/shard_map/ppermute | solution.py:357
  4.1 7.1 %collective-permute-start.5 = (f32[3,128,128]{2,1,0:T(8,128)S(1)}, f32[3,128,128]{2,1,0:T(8,128)S(1)}, u32[]{:S(2)}, u32[]{:S(2)}) collective-permute-start(f32[3,128,128]{2,1,0:T(8,128)S(1)} %get-tuple-element.23.own.down_own), channel_id=1, source_target_pairs={{1,2},{2,1},{3,4},{4,3},{5,6},{6,5},{7,8},{8,7},{9,10},{10,9},{11,... | collective-permute-start | bytes 589832 | tf_op jit(solution)/shard_map/ppermute | solution.py:357
  4.1 3.7 %collective-permute-start.1 = (f32[1,128,128]{2,1,0:T(8,128)S(1)}, f32[1,128,128]{2,1,0:T(8,128)S(1)}, u32[]{:S(2)}, u32[]{:S(2)}) collective-permute-start(f32[1,128,128]{2,1,0:T(8,128)S(1)} %slice.43), channel_id=1, source_target_pairs={{0,1},{1,0},{2,3},{3,2},{4,5},{5,4},{6,7},{7,6},{8,9},{9,8},{10,11... | collective-permute-start | bytes 196616 | tf_op jit(solution)/shard_map/ppermute | solution.py:357
  5.7 4.1 %collective-permute-start = (f32[2,128,128]{2,1,0:T(8,128)S(1)}, f32[2,128,128]{2,1,0:T(8,128)S(1)}, u32[]{:S(2)}, u32[]{:S(2)}) collective-permute-start(f32[2,128,128]{2,1,0:T(8,128)S(1)} %slice.42), channel_id=1, source_target_pairs={{0,1},{1,0},{2,3},{3,2},{4,5},{5,4},{6,7},{7,6},{8,9},{9,8},{10,11... | collective-permute-start | bytes 393224 | tf_op jit(solution)/shard_map/ppermute | solution.py:357
  5.8 5.4 %collective-permute-start.6 = (f32[264,128]{1,0:T(8,128)S(1)}, f32[264,128]{1,0:T(8,128)S(1)}, u32[]{:S(2)}, u32[]{:S(2)}) collective-permute-start(f32[264,128]{1,0:T(8,128)S(1)} %get-tuple-element.27), channel_id=1, source_target_pairs={{1,18},{2,17},{3,20},{4,19},{5,22},{6,21},{7,24},{8,23},{9,26},{10... | collective-permute-start | bytes 405512 | tf_op jit(solution)/shard_map/ppermute | solution.py:357
  7.6 2.3 %collective-permute-start.4 = (f32[1,128,128]{2,1,0:T(8,128)S(1)}, f32[1,128,128]{2,1,0:T(8,128)S(1)}, u32[]{:S(2)}, u32[]{:S(2)}) collective-permute-start(f32[1,128,128]{2,1,0:T(8,128)S(1)} %get-tuple-element.41), channel_id=1, source_target_pairs={{0,1},{1,0},{2,3},{3,2},{4,5},{5,4},{6,7},{7,6},{8,9},{9,8},{10,11... | collective-permute-start | bytes 196616 | tf_op jit(solution)/shard_map/ppermute | solution.py:357
  7.9 2.0 %collective-permute-start.3 = (f32[1,128,128]{2,1,0:T(8,128)S(1)}, f32[1,128,128]{2,1,0:T(8,128)S(1)}, u32[]{:S(2)}, u32[]{:S(2)}) collective-permute-start(f32[1,128,128]{2,1,0:T(8,128)S(1)} %get-tuple-element.42), channel_id=1, source_target_pairs={{0,1},{1,0},{2,3},{3,2},{4,5},{5,4},{6,7},{7,6},{8,9},{9,8},{10,11... | collective-permute-start | bytes 196616 | tf_op jit(solution)/shard_map/ppermute | solution.py:357
  11.6 5.7 %collective-permute-start.9 = (f32[3,128,128]{2,1,0:T(8,128)S(1)}, f32[3,128,128]{2,1,0:T(8,128)S(1)}, u32[]{:S(2)}, u32[]{:S(2)}) collective-permute-start(f32[3,128,128]{2,1,0:T(8,128)S(1)} %shard_map.58.own), channel_id=1, source_target_pairs={{1,2},{2,1},{3,4},{4,3},{5,6},{6,5},{7,8},{8,7},{9,10},{10,9},{11,... | collective-permute-start | bytes 589832 | tf_op jit(solution)/shard_map/ppermute | solution.py:357
  13.0 2.2 %collective-permute-start.7 = (f32[2,128,128]{2,1,0:T(8,128)S(1)}, f32[2,128,128]{2,1,0:T(8,128)S(1)}, u32[]{:S(2)}, u32[]{:S(2)}) collective-permute-start(f32[2,128,128]{2,1,0:T(8,128)S(1)} %slice.58), channel_id=1, source_target_pairs={{0,1},{1,0},{2,3},{3,2},{4,5},{5,4},{6,7},{7,6},{8,9},{9,8},{10,11... | collective-permute-start | bytes 393224 | tf_op jit(solution)/shard_map/ppermute | solution.py:357
  14.0 1.3 %collective-permute-start.8 = (f32[1,128,128]{2,1,0:T(8,128)S(1)}, f32[1,128,128]{2,1,0:T(8,128)S(1)}, u32[]{:S(2)}, u32[]{:S(2)}) collective-permute-start(f32[1,128,128]{2,1,0:T(8,128)S(1)} %slice.59), channel_id=1, source_target_pairs={{0,1},{1,0},{2,3},{3,2},{4,5},{5,4},{6,7},{7,6},{8,9},{9,8},{10,11... | collective-permute-start | bytes 196616 | tf_op jit(solution)/shard_map/ppermute | solution.py:357
  17.7 5.1 %collective-permute-start.10 = (f32[2,128,128]{2,1,0:T(8,128)S(1)}, f32[2,128,128]{2,1,0:T(8,128)S(1)}, u32[]{:S(2)}, u32[]{:S(2)}) collective-permute-start(f32[2,128,128]{2,1,0:T(8,128)S(1)} %get-tuple-element.29), channel_id=1, source_target_pairs={{0,16},{1,17},{2,18},{3,19},{4,20},{5,21},{6,22},{7,23},{8,24},{9,... | collective-permute-start | bytes 393224 | tf_op jit(solution)/shard_map/ppermute | solution.py:357
  23.0 6.8 %collective-permute-start.13 = (f32[3,128,128]{2,1,0:T(8,128)S(1)}, f32[3,128,128]{2,1,0:T(8,128)S(1)}, u32[]{:S(2)}, u32[]{:S(2)}) collective-permute-start(f32[3,128,128]{2,1,0:T(8,128)S(1)} %shard_map.61.own.rest_0_), channel_id=1, source_target_pairs={{1,2},{2,1},{3,4},{4,3},{5,6},{6,5},{7,8},{8,7},{9,10},{10,9},{11,... | collective-permute-start | bytes 589832 | tf_op jit(solution)/shard_map/ppermute | solution.py:357
  24.9 4.5 %collective-permute-start.11 = (f32[2,128,128]{2,1,0:T(8,128)S(1)}, f32[2,128,128]{2,1,0:T(8,128)S(1)}, u32[]{:S(2)}, u32[]{:S(2)}) collective-permute-start(f32[2,128,128]{2,1,0:T(8,128)S(1)} %slice.60), channel_id=1, source_target_pairs={{0,1},{1,0},{2,3},{3,2},{4,5},{5,4},{6,7},{7,6},{8,9},{9,8},{10,11... | collective-permute-start | bytes 393224 | tf_op jit(solution)/shard_map/ppermute | solution.py:357
  28.2 1.3 %collective-permute-start.12 = (f32[1,128,128]{2,1,0:T(8,128)S(1)}, f32[1,128,128]{2,1,0:T(8,128)S(1)}, u32[]{:S(2)}, u32[]{:S(2)}) collective-permute-start(f32[1,128,128]{2,1,0:T(8,128)S(1)} %slice.61), channel_id=1, source_target_pairs={{0,1},{1,0},{2,3},{3,2},{4,5},{5,4},{6,7},{7,6},{8,9},{9,8},{10,11... | collective-permute-start | bytes 196616 | tf_op jit(solution)/shard_map/ppermute | solution.py:357
  30.8 6.0 %collective-permute-start.16 = (f32[2,128,128]{2,1,0:T(8,128)S(1)}, f32[2,128,128]{2,1,0:T(8,128)S(1)}, u32[]{:S(2)}, u32[]{:S(2)}) collective-permute-start(f32[2,128,128]{2,1,0:T(8,128)S(1)} %get-tuple-element.33), channel_id=1, source_target_pairs={{0,16},{1,17},{2,18},{3,19},{4,20},{5,21},{6,22},{7,23},{8,24},{9,... | collective-permute-start | bytes 393224 | tf_op jit(solution)/shard_map/ppermute | solution.py:357
  31.8 9.0 %collective-permute-start.19 = (f32[3,128,128]{2,1,0:T(8,128)S(1)}, f32[3,128,128]{2,1,0:T(8,128)S(1)}, u32[]{:S(2)}, u32[]{:S(2)}) collective-permute-start(f32[3,128,128]{2,1,0:T(8,128)S(1)} %get-tuple-element.32.own), channel_id=1, source_target_pairs={{1,2},{2,1},{3,4},{4,3},{5,6},{6,5},{7,8},{8,7},{9,10},{10,9},{11,... | collective-permute-start | bytes 589832 | tf_op jit(solution)/shard_map/ppermute | solution.py:357
  33.0 4.2 %collective-permute-start.15 = (f32[1,128,128]{2,1,0:T(8,128)S(1)}, f32[1,128,128]{2,1,0:T(8,128)S(1)}, u32[]{:S(2)}, u32[]{:S(2)}) collective-permute-start(f32[1,128,128]{2,1,0:T(8,128)S(1)} %slice.51), channel_id=1, source_target_pairs={{0,1},{1,0},{2,3},{3,2},{4,5},{5,4},{6,7},{7,6},{8,9},{9,8},{10,11... | collective-permute-start | bytes 196616 | tf_op jit(solution)/shard_map/ppermute | solution.py:357
  35.3 2.1 %collective-permute-start.14 = (f32[2,128,128]{2,1,0:T(8,128)S(1)}, f32[2,128,128]{2,1,0:T(8,128)S(1)}, u32[]{:S(2)}, u32[]{:S(2)}) collective-permute-start(f32[2,128,128]{2,1,0:T(8,128)S(1)} %slice.50), channel_id=1, source_target_pairs={{0,1},{1,0},{2,3},{3,2},{4,5},{5,4},{6,7},{7,6},{8,9},{9,8},{10,11... | collective-permute-start | bytes 393224 | tf_op jit(solution)/shard_map/ppermute | solution.py:357
  35.3 5.5 %collective-permute-start.20 = (f32[264,128]{1,0:T(8,128)S(1)}, f32[264,128]{1,0:T(8,128)S(1)}, u32[]{:S(2)}, u32[]{:S(2)}) collective-permute-start(f32[264,128]{1,0:T(8,128)S(1)} %get-tuple-element.36), channel_id=1, source_target_pairs={{1,18},{2,17},{3,20},{4,19},{5,22},{6,21},{7,24},{8,23},{9,26},{10... | collective-permute-start | bytes 405512 | tf_op jit(solution)/shard_map/ppermute | solution.py:357
  36.8 1.3 %collective-permute-start.18 = (f32[1,128,128]{2,1,0:T(8,128)S(1)}, f32[1,128,128]{2,1,0:T(8,128)S(1)}, u32[]{:S(2)}, u32[]{:S(2)}) collective-permute-start(f32[1,128,128]{2,1,0:T(8,128)S(1)} %get-tuple-element.39), channel_id=1, source_target_pairs={{0,1},{1,0},{2,3},{3,2},{4,5},{5,4},{6,7},{7,6},{8,9},{9,8},{10,11... | collective-permute-start | bytes 196616 | tf_op jit(solution)/shard_map/ppermute | solution.py:357
  37.2 1.3 %collective-permute-start.17 = (f32[1,128,128]{2,1,0:T(8,128)S(1)}, f32[1,128,128]{2,1,0:T(8,128)S(1)}, u32[]{:S(2)}, u32[]{:S(2)}) collective-permute-start(f32[1,128,128]{2,1,0:T(8,128)S(1)} %get-tuple-element.40), channel_id=1, source_target_pairs={{0,1},{1,0},{2,3},{3,2},{4,5},{5,4},{6,7},{7,6},{8,9},{9,8},{10,11... | collective-permute-start | bytes 196616 | tf_op jit(solution)/shard_map/ppermute | solution.py:357
  41.2 5.7 %collective-permute-start.23 = (f32[3,128,128]{2,1,0:T(8,128)S(1)}, f32[3,128,128]{2,1,0:T(8,128)S(1)}, u32[]{:S(2)}, u32[]{:S(2)}) collective-permute-start(f32[3,128,128]{2,1,0:T(8,128)S(1)} %shard_map.65.own), channel_id=1, source_target_pairs={{1,2},{2,1},{3,4},{4,3},{5,6},{6,5},{7,8},{8,7},{9,10},{10,9},{11,... | collective-permute-start | bytes 589832 | tf_op jit(solution)/shard_map/ppermute | solution.py:357
  41.6 2.6 %collective-permute-start.21 = (f32[2,128,128]{2,1,0:T(8,128)S(1)}, f32[2,128,128]{2,1,0:T(8,128)S(1)}, u32[]{:S(2)}, u32[]{:S(2)}) collective-permute-start(f32[2,128,128]{2,1,0:T(8,128)S(1)} %slice.64), channel_id=1, source_target_pairs={{0,1},{1,0},{2,3},{3,2},{4,5},{5,4},{6,7},{7,6},{8,9},{9,8},{10,11... | collective-permute-start | bytes 393224 | tf_op jit(solution)/shard_map/ppermute | solution.py:357
  47.3 5.9 %collective-permute-start.24 = (f32[2,128,128]{2,1,0:T(8,128)S(1)}, f32[2,128,128]{2,1,0:T(8,128)S(1)}, u32[]{:S(2)}, u32[]{:S(2)}) collective-permute-start(f32[2,128,128]{2,1,0:T(8,128)S(1)} %get-tuple-element.38), channel_id=1, source_target_pairs={{0,16},{1,17},{2,18},{3,19},{4,20},{5,21},{6,22},{7,23},{8,24},{9,... | collective-permute-start | bytes 393224 | tf_op jit(solution)/shard_map/ppermute | solution.py:357
  (3 other events, 14.1 us)

commit v4 on v3

--- a/solution.py
+++ b/solution.py
@@ -145,7 +145,7 @@
     skewed[value.shape[0]:, :] = jnp.zeros_like(skewed[value.shape[0]:, :])
 
 
-def restrict_kernel(targets_in, rhs_in, links_in, mids, skewed, payload, restrict, targets, links, sems):
+def restrict_kernel(targets_in, rhs_in, links_in, mids, skewed, payload, wide, restrict, targets, links, sems):
     size = payload.shape[-1]
     slots = payload.shape[0]
     fetch_targets = pltpu.make_async_copy(targets_in.at[0, 0], targets, sems.at[0])
@@ -168,6 +168,7 @@
         fetch_rhs.wait()
         right = split_columns(payload[...].reshape(slots * size, size))
         store_mids(product(restrict[...], right), mids, skewed)
+        wide[...] = jnp.zeros_like(wide)
 
     @pl.when(lax.axis_index("lvl") != 0)
     def _():
@@ -176,6 +177,8 @@
         payload[0] = links[0, 0]
         payload[1] = links[2, 0]
         payload[2] = jnp.zeros_like(payload[2])
+        wide[:2 * size, :] = stacked(links[0, 0], links[2, 0])
+        wide[2 * size:, :] = jnp.zeros_like(wide[2 * size:, :])
         mids[...] = jnp.zeros_like(mids)
         skewed[...] = jnp.zeros_like(skewed)
 
@@ -210,12 +213,19 @@
             matrix[s * size:(s + 1) * size, c * size:(c + 1) * size] = high
             matrix[(slots + s) * size:(slots + s + 1) * size, c * size:(c + 1) * size] = low
     fetch_links.wait()
-    for s in range(slots):
-        for k in range(2):
-            up = jnp.where(targets[1, s] == k, links[s, 1], 0.0)
-            high, low = split(up)
-            prolong[s * size:(s + 1) * size, k * size:(k + 1) * size] = high
-            prolong[(slots + s) * size:(slots + s + 1) * size, k * size:(k + 1) * size] = low
+
+    @pl.when(lax.axis_index("lvl") == 0)
+    def _():
+        for s in range(slots):
+            for k in range(2):
+                up = jnp.where(targets[1, s] == k, links[s, 1], 0.0)
+                high, low = split(up)
+                prolong[s * size:(s + 1) * size, k * size:(k + 1) * size] = high
+                prolong[(slots + s) * size:(slots + s + 1) * size, k * size:(k + 1) * size] = low
+
+    @pl.when(lax.axis_index("lvl") != 0)
+    def _():
+        prolong[:4 * size, :size] = split_rows(stacked(links[0, 1], links[2, 1]))
 
 
 def joined(blocks):
@@ -224,6 +234,19 @@
 
 def blocks_of(*refs):
     return [ref[s] for ref in refs for s in range(ref.shape[0])]
+
+
+def own_slots(matrix, sides, groups):
+    size = groups[0][0].shape[0]
+    slots = len(groups[0])
+    parts = []
+    for s in range(slots):
+        columns = [slice((side * slots + s) * size, (side * slots + s + 1) * size) for side in sides]
+        high = [matrix[s * size:(s + 1) * size, c] for c in columns]
+        low = [matrix[(slots + s) * size:(slots + s + 1) * size, c] for c in columns]
+        left = stacked(jnp.concatenate(high, axis=1), jnp.concatenate(low, axis=1))
+        parts.append(product(left, joined([group[s] for group in groups])))
+    return stacked(*parts).reshape(slots, size, -1)
 
 
 def near(matrix, field):
@@ -242,52 +265,90 @@
     return [mid[0], coarse, mid[1]]
 
 
-def first_near_kernel(matrix, own, core, core_last, down_own, down_core, mid_own, mid_core, mid_core_last, level, part, field):
-    @pl.when(lax.axis_index("lvl") == 0)
-    def _():
-        field[...] = joined(blocks_of(own, core, core_last))
+def rows_of(ref):
+    size = ref.shape[-1]
+    return [ref[k * size:(k + 1) * size, :] for k in range(2)]
+
+
+def first_fine_kernel(matrix, own, core, core_last, part):
+    @pl.when(lax.axis_index("lvl") == 0)
+    def _():
+        part[...] = near(matrix, joined(blocks_of(own, core, core_last))).reshape(part.shape)
+
+
+def first_near_kernel(fine_part, matrix, own, down_own, down_core, mid_own, mid_core, mid_core_last, part, level):
+    @pl.when(lax.axis_index("lvl") == 0)
+    def _():
         level[...] = own[...]
 
     @pl.when(lax.axis_index("lvl") != 0)
     def _():
         here = level_blocks(down_own, blocks_of(mid_own))
-        field[...] = joined(here + level_blocks(down_core, blocks_of(mid_core, mid_core_last)))
+        beside = level_blocks(down_core, blocks_of(mid_core, mid_core_last))
         level[...] = stacked(*here).reshape(level.shape)
-
-    part[...] = near(matrix, field[...]).reshape(part.shape)
-
-
-def first_far_kernel(matrix, part, cross, down_cross, skewed, first, field):
-    @pl.when(lax.axis_index("lvl") == 0)
-    def _():
-        field[...] = joined(blocks_of(cross))
-
-    @pl.when(lax.axis_index("lvl") != 0)
-    def _():
-        size = cross.shape[-1]
-        field[...] = joined(level_blocks(down_cross, (skewed[:size, :], skewed[size:2 * size, :])))
-
-    first[...] = part[...] + far(matrix, field[...]).reshape(first.shape)
+        part[...] = own_slots(matrix, (0, 1), (here, beside))
+
+
+def start_near_kernel(matrix, own, down_own, down_core, mid_own, mid_core, part, level):
+    @pl.when(lax.axis_index("lvl") == 0)
+    def _():
+        level[...] = own[...]
+        part[...] = near(matrix, joined(blocks_of(own, down_core))).reshape(part.shape)
+
+    @pl.when(lax.axis_index("lvl") != 0)
+    def _():
+        here = level_blocks(down_own, blocks_of(mid_own))
+        beside = level_blocks(down_core, blocks_of(mid_core))
+        level[...] = stacked(*here).reshape(level.shape)
+        part[...] = own_slots(matrix, (0, 1), (here, beside))
+
+
+def start_far_kernel(matrix, part, cross, down_cross, skewed, first):
+    @pl.when(lax.axis_index("lvl") == 0)
+    def _():
+        first[...] = part[...] + far(matrix, joined(blocks_of(cross))).reshape(first.shape)
+
+    @pl.when(lax.axis_index("lvl") != 0)
+    def _():
+        beside = level_blocks(rows_of(down_cross), rows_of(skewed))
+        first[...] = part[...] + own_slots(matrix, (2,), (beside,))
+
+
+def first_far_kernel(matrix, part, cross, down_cross, skewed, first):
+    @pl.when(lax.axis_index("lvl") == 0)
+    def _():
+        first[...] = part[...] + far(matrix, joined(blocks_of(cross))).reshape(first.shape)
+
+    @pl.when(lax.axis_index("lvl") != 0)
+    def _():
+        beside = level_blocks(rows_of(down_cross), rows_of(skewed))
+        first[...] = part[...] + own_slots(matrix, (2,), (beside,))
 
 
 def near_kernel(matrix, own, core, core_last, part):
-    part[...] = near(matrix, joined(blocks_of(own, core, core_last))).reshape(part.shape)
-
-
-def second_kernel(matrix, level, own, part, cross, links, smooth, fixes):
-    second = part[...] + far(matrix, joined(blocks_of(cross))).reshape(part.shape)
-    value = COEF_ZERO * level[...] + COEF_ONE * own[...] + COEF_TWO * second
-
-    @pl.when(lax.axis_index("lvl") == 0)
-    def _():
-        smooth[...] = value
+    @pl.when(lax.axis_index("lvl") == 0)
+    def _():
+        part[...] = near(matrix, joined(blocks_of(own, core, core_last))).reshape(part.shape)
+
+    @pl.when(lax.axis_index("lvl") != 0)
+    def _():
+        part[...] = own_slots(matrix, (0, 1), (blocks_of(own), blocks_of(core, core_last)))
+
+
+def second_kernel(matrix, level, own, part, cross, prolong, smooth, fixes):
+    @pl.when(lax.axis_index("lvl") == 0)
+    def _():
+        second = part[...] + far(matrix, joined(blocks_of(cross))).reshape(part.shape)
+        smooth[...] = COEF_ZERO * level[...] + COEF_ONE * own[...] + COEF_TWO * second
         fixes[...] = jnp.zeros_like(fixes)
 
     @pl.when(lax.axis_index("lvl") != 0)
     def _():
+        second = part[...] + own_slots(matrix, (2,), (blocks_of(cross),))
+        value = COEF_ZERO * level[...] + COEF_ONE * own[...] + COEF_TWO * second
         coarse = value[1]
-        up = product(split_rows(stacked(links[0, 1], links[2, 1])), split_columns(coarse))
         size = coarse.shape[0]
+        up = product(prolong[:4 * size, :size], split_columns(coarse))
         low, high = value[0] + up[:size], value[2] + up[size:]
         smooth[0] = low
         smooth[1] = coarse
@@ -311,12 +372,34 @@
         result[...] = smooth[...]
 
 
-def residual_kernel(matrix, part, cross, rhs, restrict, resid, mids, skewed):
-    @pl.when(lax.axis_index("lvl") == 0)
-    def _():
-        value = rhs[...] - (part[...] + far(matrix, joined(blocks_of(cross))).reshape(rhs.shape))
-        resid[...] = value
-        store_mids(product(restrict[...], joined([value[s] for s in range(value.shape[0])])), mids, skewed)
+def tall_kernel(matrix, restrict, tall):
+    big, wide = matrix.shape[0] // 2, restrict.shape[0] // 2
+
+    @pl.when(lax.axis_index("lvl") == 0)
+    def _():
+        tall[:big, :] = matrix[:big, :]
+        tall[big + wide:2 * big + wide, :] = matrix[big:, :]
+        for c in range(0, matrix.shape[1], big):
+            right = jnp.concatenate([matrix[:big, c:c + big], matrix[big:, c:c + big]], axis=1)
+            high, low = split(product(restrict[...], right))
+            tall[big:big + wide, c:c + big] = high
+            tall[2 * big + wide:, c:c + big] = low
+
+
+def residual_near_kernel(tall, own, core, core_last, part):
+    @pl.when(lax.axis_index("lvl") == 0)
+    def _():
+        part[...] = near(tall, joined(blocks_of(own, core, core_last)))
+
+
+def residual_far_kernel(tall, part, cross, rhs, before, resid, mids, skewed):
+    big, size = rhs.shape[0] * rhs.shape[1], rhs.shape[1]
+
+    @pl.when(lax.axis_index("lvl") == 0)
+    def _():
+        value = part[...] + far(tall, joined(blocks_of(cross)))
+        store_mids(before[...].reshape(2 * size, -1) - value[big:], mids, skewed)
+        resid[...] = rhs[...] - value[:big].reshape(rhs.shape)
 
     @pl.when(lax.axis_index("lvl") != 0)
     def _():
@@ -346,28 +429,33 @@
     core = [(l * rows + r, l * rows + (r ^ 1)) for l in range(2) for r in range(rows)]
     cross = [(l * rows + r, l * rows + across[r]) for l in range(2) for r in range(1, rows - 1)]
     cross += [(l * rows + r, (1 - l) * rows + r) for l in range(2) for r in (0, rows - 1)]
-    fine = [(r, across[r]) for r in range(1, rows - 1)] + [(rows + r, rows + (r ^ 1)) for r in range(2, rows - 2)]
+    fine = [(r, across[r]) for r in range(1, rows - 1)] + [(0, rows - 1), (rows - 1, 0)]
+    fine += [(rows + r, rows + (r ^ 1)) for r in range(rows)]
+    short = [(r, across[r]) for r in range(1, rows - 1)] + [(rows + r, rows + (r ^ 1)) for r in range(2, rows - 2)]
     for end, beside in ((0, 1), (rows - 1, rows - 2)):
-        fine += [(end, rows + end), (rows + end, rows + beside), (rows + beside, end)]
+        short += [(end, rows + end), (rows + end, rows + beside), (rows + beside, end)]
+    other = [(r, r ^ 1) for r in range(2, rows - 2)] + [(rows + r, rows + across[r]) for r in range(1, rows - 1)]
+    for end, beside in ((0, 1), (rows - 1, rows - 2)):
+        other += [(rows + end, end), (end, beside), (beside, rows + end)]
     level = [(l * rows + r, (1 - l) * rows + r) for l in range(2) for r in range(rows)]
     skew = [(r, rows + across[r]) for r in range(1, rows - 1)]
     skew += [(rows + r, r) for r in range(rows) if r not in (1, rows - 2)]
     for end, beside in ((0, 1), (rows - 1, rows - 2)):
         skew += [(end, beside), (rows + beside, rows + end)]
-    return tuple((lambda x, pairs=pairs: lax.ppermute(x, ("lvl", "row"), pairs)) for pairs in (core, cross, fine, level, skew))
+    return tuple((lambda x, pairs=pairs: lax.ppermute(x, ("lvl", "row"), pairs)) for pairs in (core, cross, fine, short, other, level, skew))
 
 
 def paired(rhs, op_tiles, op_cols, link_tiles, level_links):
-    core, cross, fine, level, skew = swaps(lax.axis_size("row"))
+    core, cross, fine, short, other, level, skew = swaps(lax.axis_size("row"))
     right, tiles, links = rhs[0, 0], op_tiles[0, 0], link_tiles[0, 0]
     slots, size, width = right.shape
     blocks, pair = (right.shape, F32), ((2, size, width), F32)
     big = slots * size
     codes, goals = jnp.swapaxes(op_cols, 1, 2), jnp.swapaxes(level_links, 2, 3)
     long = ((2 * size + 8, width), F32)
-    mids, skewed, payload, restrict = call(
+    mids, skewed, payload, wide, restrict = call(
         restrict_kernel,
-        [pair, long, blocks, ((4 * size, big), BF16)],
+        [pair, long, blocks, ((2 * size + 8, width), F32), ((4 * size, big), BF16)],
         [goals, right, links],
         anywhere=3,
         scratch=[
@@ -376,16 +464,23 @@
             pltpu.SemaphoreType.DMA((3,)),
         ],
     )
-    down = result = matrix = prolong = None
+    down = result = matrix = prolong = tall = None
     for cycle in range(CYCLES):
         if cycle > 0:
-            result_cross = cross(result)
-            (part,) = call(near_kernel, [blocks], [matrix, result, core(result[:-1]), core(result[-1:])])
-            payload, mids, skewed = call(residual_kernel, [blocks, pair, long], [matrix, part, result_cross, right, restrict])
+            result_cross = short(result)
+            (part,) = call(
+                residual_near_kernel,
+                [((big + 2 * size, width), F32)],
+                [tall, result, core(result[:-1]), core(result[-1:])],
+            )
+            payload, mids, skewed = call(
+                residual_far_kernel,
+                [blocks, pair, long],
+                [tall, part, result_cross, right, mids],
+            )
         mid_here, mid_cross = level(mids), skew(skewed)
-        around = (payload, core(payload[:-1]), core(payload[-1:]), cross(payload) if cycle == 0 else fine(payload))
-        mid_core = core(mid_here[:1]), core(mid_here[1:])
         if cycle == 0:
+            beyond, beside, mid_core = short(payload), [core(payload)], [core(mid_here)]
             matrix, prolong = call(
                 operator_kernel,
                 [((2 * big, 3 * big), BF16), ((2 * big, 2 * size), BF16)],
@@ -400,26 +495,43 @@
                     pltpu.SemaphoreType.DMA((3 + slots,)),
                 ],
             )
-            down = around[0], around[1], around[3]
-        level_resid, part = call(
-            first_near_kernel,
-            [blocks, blocks],
-            [matrix, *around[:3], *down[:2], mid_here, *mid_core],
-            scratch=[pltpu.VMEM((2 * big, 2 * width), BF16)],
-        )
-        (first,) = call(
-            first_far_kernel,
-            [blocks],
-            [matrix, part, around[3], down[2], mid_cross],
-            scratch=[pltpu.VMEM((big, 2 * width), BF16)],
-        )
+            down = payload, beside[0], other(wide)
+            part, level_resid = call(
+                start_near_kernel,
+                [blocks, blocks],
+                [matrix, payload, *down[:2], mid_here, *mid_core],
+            )
+            (first,) = call(
+                start_far_kernel,
+                [blocks],
+                [matrix, part, beyond, down[2], mid_cross],
+            )
+            (tall,) = call(tall_kernel, [((2 * big + 4 * size, 3 * big), BF16)], [matrix, restrict])
+        else:
+            beyond, beside = fine(payload), [core(payload[:-1]), core(payload[-1:])]
+            mid_core = [core(mid_here[:1]), core(mid_here[1:])]
+            (part,) = call(first_fine_kernel, [blocks], [matrix, payload, *beside])
+            part, level_resid = call(
+                first_near_kernel,
+                [blocks, blocks],
+                [part, matrix, payload, *down[:2], mid_here, *mid_core],
+                aliases={0: 0},
+            )
+            (first,) = call(first_far_kernel, [blocks], [matrix, part, beyond, down[2], mid_cross])
         first_cross = cross(first)
         (part,) = call(near_kernel, [blocks], [matrix, first, core(first[:-1]), core(first[-1:])])
-        smooth, fixes = call(second_kernel, [blocks, pair], [matrix, level_resid, first, part, first_cross, links])
+        smooth, fixes = call(second_kernel, [blocks, pair], [matrix, level_resid, first, part, first_cross, prolong])
         fixes = level(fixes)
         args = [smooth, fixes, prolong] + ([] if cycle == 0 else [result])
         (result,) = call(solution_kernel, [blocks], args)
     return result[None, None]
+
+
+def body(rhs, *rest):
+    rows = lax.axis_size("row")
+    square = rhs.shape[-1] == rhs.shape[-2]
+    plan = paired if lax.axis_size("lvl") == 2 and rows % 2 == 0 and rows > 2 and square else per_device
+    return plan(rhs, *rest)
 
 
 def solution(mesh):
@@ -430,9 +542,8 @@
         P("lvl", "row", None, None, None, None),
         P("lvl", "row", None, None),
     )
-    pairs = mesh.shape["lvl"] == 2 and mesh.shape["row"] % 2 == 0
     return jax.shard_map(
-        paired if pairs else per_device,
+        body,
         mesh=mesh,
         in_specs=placed,
         out_specs=P("lvl", "row", None, None, None),

time: 54.5 us -> 53.9 us (0.989)
  starting transfers between devices: 23 us -> 16.6 us
  waiting for transfers between devices: 21.6 us -> 26.4 us
  Pallas kernels: 9.23 us -> 10.5 us
    ppermute x25 -> x24, starting transfers between devices: 23 us -> 16.6 us  [swaps(): lax.ppermute(x, ('lvl', 'row'), pairs)]
    ppermute x25 -> x24, waiting for transfers between devices: 21.6 us -> 26.4 us  [swaps(): lax.ppermute(x, ('lvl', 'row'), pairs)]
    pallas_call x14 -> x16, Pallas kernels: 9.23 us -> 10.5 us  [call(): pl.pallas_call(kernel, out_shape=[jax.ShapeDtypeStruct(shape, dtype) for...]
  transfers between devices with their start and end apart: 25 -> 24, of which waited for: 13 -> 16; matrix products, arithmetic and copies ran while one was open for 0% -> 0% of each run, Pallas kernels for 8% -> 11%
where the time goes in v4:
time: 53.9 us; the launch traced here: 53.8 us
  waiting for transfers between devices  26.4 us (49%)
  starting transfers between devices  16.6 us (31%)
  Pallas kernels  10.5 us (19%)
    ppermute x24, waiting for transfers between devices, swaps(): lax.ppermute(x, ('lvl', 'row'), pairs)  26.4 us
    ppermute x24, starting transfers between devices, swaps(): lax.ppermute(x, ('lvl', 'row'), pairs)  16.6 us
    pallas_call x16, Pallas kernels, call(): pl.pallas_call(kernel, out_shape=[jax.ShapeDtypeStruct(shape, dtype) for...  10.5 us
  transfers between devices with their start and end apart: 24, of which 16 were waited for; matrix products, arithmetic and copies ran while one was open for 0% of the time, Pallas kernels for 11%

profile of v4, /device:TPU:0, one launch (start us, length us, event | category | flops | bytes accessed | tf_op | source)
XLA Modules:
  0.0 53.8 jit_solution(743780641649533473)
XLA Ops:
  0.0 1.4 %shard_map.56 = (f32[2,128,128]{2,1,0:T(8,128)S(1)}, f32[264,128]{1,0:T(8,128)S(1)}, f32[3,128,128]{2,1,0:T(8,128)S(1)}, f32[264,128]{1,0:T(8,128)S(1)}, bf16[512,384]{1,0:T(8,128)(2,1)S(1)}) custom-call(s32[1,1,2,3]{3,2,1,0:T(2,128)} %bitcast.11, f32[3,128,128]{2,1,0:T(8,128)} %bitcast.6, f32[3,2,128,128]{3,2,1,0:T(8,128)} %bitcast.8), custom_call_target="tpu_custom_call" | custom-call | tf_op jit(solution)/shard_map/pallas_call | solution.py:415
  1.4 2.7 %collective-permute-start.1 = (f32[2,128,128]{2,1,0:T(8,128)S(1)}, f32[2,128,128]{2,1,0:T(8,128)S(1)}, u32[]{:S(2)}, u32[]{:S(2)}) collective-permute-start(f32[2,128,128]{2,1,0:T(8,128)S(1)} %get-tuple-element.26.before), channel_id=1, source_target_pairs={{0,16},{1,17},{2,18},{3,19},{4,20},{5,21},{6,22},{7,23},{8,24},{9,... | collective-permute-start | bytes 393224 | tf_op jit(solution)/shard_map/ppermute | solution.py:445
  4.2 1.5 %collective-permute-start.4 = (f32[264,128]{1,0:T(8,128)S(1)}, f32[264,128]{1,0:T(8,128)S(1)}, u32[]{:S(2)}, u32[]{:S(2)}) collective-permute-start(f32[264,128]{1,0:T(8,128)S(1)} %get-tuple-element.29), channel_id=1, source_target_pairs={{2,3},{3,2},{4,5},{5,4},{6,7},{7,6},{8,9},{9,8},{10,11},{11,10},{1... | collective-permute-start | bytes 405512 | tf_op jit(solution)/shard_map/ppermute | solution.py:445
  5.7 2.3 %collective-permute-done.1.mid_own = f32[2,128,128]{2,1,0:T(8,128)S(1)} collective-permute-done((f32[2,128,128]{2,1,0:T(8,128)S(1)}, f32[2,128,128]{2,1,0:T(8,128)S(1)}, u32[]{:S(2)}, u32[]{:S(2)}) %collective-permute-start.1) | collective-permute-done | bytes 131104 | tf_op jit(solution)/shard_map/ppermute | solution.py:445
  8.0 1.7 %shard_map.55 = (bf16[768,1152]{1,0:T(8,128)(2,1)S(1)}, bf16[768,256]{1,0:T(8,128)(2,1)S(1)}) custom-call(s32[1,3,1,7]{3,2,1,0:T(1,128)} %bitcast.13, s32[1,1,2,3]{3,2,1,0:T(2,128)} %bitcast.12, f32[3,2,128,128]{3,2,1,0:T(8,128)} %bitcast.9, f32[3,7,128,128]{3,2,1,0:T(8,128)} %bitcast.10), custom_call_target="tpu_custom_call" | custom-call | tf_op jit(solution)/shard_map/pallas_call | solution.py:415
  10.9 1.7 %collective-permute-done.5.skewed = f32[264,128]{1,0:T(8,128)S(1)} collective-permute-done((f32[264,128]{1,0:T(8,128)S(1)}, f32[264,128]{1,0:T(8,128)S(1)}, u32[]{:S(2)}, u32[]{:S(2)}) %collective-permute-start.5) | collective-permute-done | bytes 135200 | tf_op jit(solution)/shard_map/ppermute | solution.py:445
  13.6 2.6 %collective-permute-start.8 = (f32[3,128,128]{2,1,0:T(8,128)S(1)}, f32[3,128,128]{2,1,0:T(8,128)S(1)}, u32[]{:S(2)}, u32[]{:S(2)}) collective-permute-start(f32[3,128,128]{2,1,0:T(8,128)S(1)} %shard_map.59.own), channel_id=1, source_target_pairs={{1,2},{2,1},{3,4},{4,3},{5,6},{6,5},{7,8},{8,7},{9,10},{10,9},{11,... | collective-permute-start | bytes 589832 | tf_op jit(solution)/shard_map/ppermute | solution.py:445
  16.8 0.9 %collective-permute-done.7.core_last = f32[1,128,128]{2,1,0:T(8,128)S(1)} collective-permute-done((f32[1,128,128]{2,1,0:T(8,128)S(1)}, f32[1,128,128]{2,1,0:T(8,128)S(1)}, u32[]{:S(2)}, u32[]{:S(2)}) %collective-permute-start.7) | collective-permute-done | bytes 65568 | tf_op jit(solution)/shard_map/ppermute | solution.py:445
  18.2 1.6 %collective-permute-done.8.cross = f32[3,128,128]{2,1,0:T(8,128)S(1)} collective-permute-done((f32[3,128,128]{2,1,0:T(8,128)S(1)}, f32[3,128,128]{2,1,0:T(8,128)S(1)}, u32[]{:S(2)}, u32[]{:S(2)}) %collective-permute-start.8) | collective-permute-done | bytes 196640 | tf_op jit(solution)/shard_map/ppermute | solution.py:445
  20.2 2.2 %collective-permute-start.9 = (f32[2,128,128]{2,1,0:T(8,128)S(1)}, f32[2,128,128]{2,1,0:T(8,128)S(1)}, u32[]{:S(2)}, u32[]{:S(2)}) collective-permute-start(f32[2,128,128]{2,1,0:T(8,128)S(1)} %get-tuple-element.33), channel_id=1, source_target_pairs={{0,16},{1,17},{2,18},{3,19},{4,20},{5,21},{6,22},{7,23},{8,24},{9,... | collective-permute-start | bytes 393224 | tf_op jit(solution)/shard_map/ppermute | solution.py:445
  22.5 3.4 %collective-permute-done.9.fixes = f32[2,128,128]{2,1,0:T(8,128)S(1)} collective-permute-done((f32[2,128,128]{2,1,0:T(8,128)S(1)}, f32[2,128,128]{2,1,0:T(8,128)S(1)}, u32[]{:S(2)}, u32[]{:S(2)}) %collective-permute-start.9) | collective-permute-done | bytes 131104 | tf_op jit(solution)/shard_map/ppermute | solution.py:445
  26.1 1.5 %collective-permute-start.12 = (f32[3,128,128]{2,1,0:T(8,128)S(1)}, f32[3,128,128]{2,1,0:T(8,128)S(1)}, u32[]{:S(2)}, u32[]{:S(2)}) collective-permute-start(f32[3,128,128]{2,1,0:T(8,128)S(1)} %shard_map.62.own.rest_0_), channel_id=1, source_target_pairs={{1,2},{2,1},{3,4},{4,3},{5,6},{6,5},{7,8},{8,7},{9,10},{10,9},{11,... | collective-permute-start | bytes 589832 | tf_op jit(solution)/shard_map/ppermute | solution.py:445
  28.2 1.5 %shard_map.57.tall = bf16[1280,1152]{1,0:T(8,128)(2,1)S(1)} custom-call(bf16[768,1152]{1,0:T(8,128)(2,1)S(1)} %get-tuple-element.23.matrix, bf16[512,384]{1,0:T(8,128)(2,1)S(1)} %get-tuple-element.24.restrict), custom_call_target="tpu_custom_call" | custom-call | tf_op jit(solution)/shard_map/pallas_call | solution.py:415
  29.8 0.7 %shard_map.63.part = f32[640,128]{1,0:T(8,128)S(1)} custom-call(bf16[1280,1152]{1,0:T(8,128)(2,1)S(1)} %shard_map.57.tall, f32[3,128,128]{2,1,0:T(8,128)S(1)} %shard_map.62.own.rest_0_, f32[2,128,128]{2,1,0:T(8,128)S(1)} %collective-permute-done.10.core, f32[1,128,128]{2,1,0:T(8,128)S(1)} %collective-permute-done.11.core_last), custom_call_target="tpu_custom_call" | custom-call | tf_op jit(solution)/shard_map/pallas_call | solution.py:415
  30.5 0.7 %collective-permute-done.12.cross = f32[3,128,128]{2,1,0:T(8,128)S(1)} collective-permute-done((f32[3,128,128]{2,1,0:T(8,128)S(1)}, f32[3,128,128]{2,1,0:T(8,128)S(1)}, u32[]{:S(2)}, u32[]{:S(2)}) %collective-permute-start.12) | collective-permute-done | bytes 196640 | tf_op jit(solution)/shard_map/ppermute | solution.py:445
  31.8 1.7 %collective-permute-start.15 = (f32[2,128,128]{2,1,0:T(8,128)S(1)}, f32[2,128,128]{2,1,0:T(8,128)S(1)}, u32[]{:S(2)}, u32[]{:S(2)}) collective-permute-start(f32[2,128,128]{2,1,0:T(8,128)S(1)} %get-tuple-element.35), channel_id=1, source_target_pairs={{0,16},{1,17},{2,18},{3,19},{4,20},{5,21},{6,22},{7,23},{8,24},{9,... | collective-permute-start | bytes 393224 | tf_op jit(solution)/shard_map/ppermute | solution.py:445
  33.4 1.2 %collective-permute-start.18 = (f32[3,128,128]{2,1,0:T(8,128)S(1)}, f32[3,128,128]{2,1,0:T(8,128)S(1)}, u32[]{:S(2)}, u32[]{:S(2)}) collective-permute-start(f32[3,128,128]{2,1,0:T(8,128)S(1)} %get-tuple-element.34.own), channel_id=1, source_target_pairs={{1,2},{2,1},{3,4},{4,3},{5,6},{6,5},{7,8},{8,7},{9,10},{10,9},{11,... | collective-permute-start | bytes 589832 | tf_op jit(solution)/shard_map/ppermute | solution.py:445
  35.1 2.2 %collective-permute-done.15.mid_own = f32[2,128,128]{2,1,0:T(8,128)S(1)} collective-permute-done((f32[2,128,128]{2,1,0:T(8,128)S(1)}, f32[2,128,128]{2,1,0:T(8,128)S(1)}, u32[]{:S(2)}, u32[]{:S(2)}) %collective-permute-start.15) | collective-permute-done | bytes 131104 | tf_op jit(solution)/shard_map/ppermute | solution.py:445
  38.9 1.3 %collective-permute-done.19.skewed = f32[264,128]{1,0:T(8,128)S(1)} collective-permute-done((f32[264,128]{1,0:T(8,128)S(1)}, f32[264,128]{1,0:T(8,128)S(1)}, u32[]{:S(2)}, u32[]{:S(2)}) %collective-permute-start.19) | collective-permute-done | bytes 135200 | tf_op jit(solution)/shard_map/ppermute | solution.py:445
  40.1 1.1 %collective-permute-done.18.cross = f32[3,128,128]{2,1,0:T(8,128)S(1)} collective-permute-done((f32[3,128,128]{2,1,0:T(8,128)S(1)}, f32[3,128,128]{2,1,0:T(8,128)S(1)}, u32[]{:S(2)}, u32[]{:S(2)}) %collective-permute-start.18) | collective-permute-done | bytes 196640 | tf_op jit(solution)/shard_map/ppermute | solution.py:445
  42.4 1.2 %collective-permute-done.21.core_last = f32[1,128,128]{2,1,0:T(8,128)S(1)} collective-permute-done((f32[1,128,128]{2,1,0:T(8,128)S(1)}, f32[1,128,128]{2,1,0:T(8,128)S(1)}, u32[]{:S(2)}, u32[]{:S(2)}) %collective-permute-start.21) | collective-permute-done | bytes 65568 | tf_op jit(solution)/shard_map/ppermute | solution.py:445
  44.0 3.4 %collective-permute-done.22.cross = f32[3,128,128]{2,1,0:T(8,128)S(1)} collective-permute-done((f32[3,128,128]{2,1,0:T(8,128)S(1)}, f32[3,128,128]{2,1,0:T(8,128)S(1)}, u32[]{:S(2)}, u32[]{:S(2)}) %collective-permute-start.22) | collective-permute-done | bytes 196640 | tf_op jit(solution)/shard_map/ppermute | solution.py:445
  48.0 4.8 %collective-permute-done.23.fixes = f32[2,128,128]{2,1,0:T(8,128)S(1)} collective-permute-done((f32[2,128,128]{2,1,0:T(8,128)S(1)}, f32[2,128,128]{2,1,0:T(8,128)S(1)}, u32[]{:S(2)}, u32[]{:S(2)}) %collective-permute-start.23) | collective-permute-done | bytes 131104 | tf_op jit(solution)/shard_map/ppermute | solution.py:445
  52.8 1.0 %shard_map.70 = f32[3,128,128]{2,1,0:T(8,128)} custom-call(f32[3,128,128]{2,1,0:T(8,128)S(1)} %get-tuple-element.39.smooth, f32[2,128,128]{2,1,0:T(8,128)S(1)} %collective-permute-done.23.fixes, bf16[768,256]{1,0:T(8,128)(2,1)S(1)} %get-tuple-element.31.prolong, f32[3,128,128]{2,1,0:T(8,128)S(1)} %shard_map.62.own.rest_0_), custom_call_target="tpu_custom_call" | custom-call | tf_op jit(solution)/shard_map/pallas_call | solution.py:415
  (51 shorter events, 9.3 us)
Async XLA Ops:
  1.4 6.6 %collective-permute-start.1 = (f32[2,128,128]{2,1,0:T(8,128)S(1)}, f32[2,128,128]{2,1,0:T(8,128)S(1)}, u32[]{:S(2)}, u32[]{:S(2)}) collective-permute-start(f32[2,128,128]{2,1,0:T(8,128)S(1)} %get-tuple-element.26.before), channel_id=1, source_target_pairs={{0,16},{1,17},{2,18},{3,19},{4,20},{5,21},{6,22},{7,23},{8,24},{9,... | collective-permute-start | bytes 393224 | tf_op jit(solution)/shard_map/ppermute | solution.py:445
  4.1 5.6 %collective-permute-start = (f32[3,128,128]{2,1,0:T(8,128)S(1)}, f32[3,128,128]{2,1,0:T(8,128)S(1)}, u32[]{:S(2)}, u32[]{:S(2)}) collective-permute-start(f32[3,128,128]{2,1,0:T(8,128)S(1)} %get-tuple-element.25.own.down_own), channel_id=1, source_target_pairs={{0,1},{1,0},{2,3},{3,2},{4,5},{5,4},{6,7},{7,6},{8,9},{9,8},{10,11... | collective-permute-start | bytes 589832 | tf_op jit(solution)/shard_map/ppermute | solution.py:445
  4.1 9.1 %collective-permute-start.3 = (f32[3,128,128]{2,1,0:T(8,128)S(1)}, f32[3,128,128]{2,1,0:T(8,128)S(1)}, u32[]{:S(2)}, u32[]{:S(2)}) collective-permute-start(f32[3,128,128]{2,1,0:T(8,128)S(1)} %get-tuple-element.25.own.down_own), channel_id=1, source_target_pairs={{1,2},{2,1},{3,4},{4,3},{5,6},{6,5},{7,8},{8,7},{9,10},{10,9},{11,... | collective-permute-start | bytes 589832 | tf_op jit(solution)/shard_map/ppermute | solution.py:445
  4.2 6.7 %collective-permute-start.4 = (f32[264,128]{1,0:T(8,128)S(1)}, f32[264,128]{1,0:T(8,128)S(1)}, u32[]{:S(2)}, u32[]{:S(2)}) collective-permute-start(f32[264,128]{1,0:T(8,128)S(1)} %get-tuple-element.29), channel_id=1, source_target_pairs={{2,3},{3,2},{4,5},{5,4},{6,7},{7,6},{8,9},{9,8},{10,11},{11,10},{1... | collective-permute-start | bytes 405512 | tf_op jit(solution)/shard_map/ppermute | solution.py:445
  5.7 6.9 %collective-permute-start.5 = (f32[264,128]{1,0:T(8,128)S(1)}, f32[264,128]{1,0:T(8,128)S(1)}, u32[]{:S(2)}, u32[]{:S(2)}) collective-permute-start(f32[264,128]{1,0:T(8,128)S(1)} %get-tuple-element.30), channel_id=1, source_target_pairs={{1,18},{2,17},{3,20},{4,19},{5,22},{6,21},{7,24},{8,23},{9,26},{10... | collective-permute-start | bytes 405512 | tf_op jit(solution)/shard_map/ppermute | solution.py:445
  8.0 1.7 %collective-permute-start.2 = (f32[2,128,128]{2,1,0:T(8,128)S(1)}, f32[2,128,128]{2,1,0:T(8,128)S(1)}, u32[]{:S(2)}, u32[]{:S(2)}) collective-permute-start(f32[2,128,128]{2,1,0:T(8,128)S(1)} %collective-permute-done.1.mid_own), channel_id=1, source_target_pairs={{0,1},{1,0},{2,3},{3,2},{4,5},{5,4},{6,7},{7,6},{8,9},{9,8},{10,11... | collective-permute-start | bytes 393224 | tf_op jit(solution)/shard_map/ppermute | solution.py:445
  13.6 6.3 %collective-permute-start.8 = (f32[3,128,128]{2,1,0:T(8,128)S(1)}, f32[3,128,128]{2,1,0:T(8,128)S(1)}, u32[]{:S(2)}, u32[]{:S(2)}) collective-permute-start(f32[3,128,128]{2,1,0:T(8,128)S(1)} %shard_map.59.own), channel_id=1, source_target_pairs={{1,2},{2,1},{3,4},{4,3},{5,6},{6,5},{7,8},{8,7},{9,10},{10,9},{11,... | collective-permute-start | bytes 589832 | tf_op jit(solution)/shard_map/ppermute | solution.py:445
  16.2 1.5 %collective-permute-start.6 = (f32[2,128,128]{2,1,0:T(8,128)S(1)}, f32[2,128,128]{2,1,0:T(8,128)S(1)}, u32[]{:S(2)}, u32[]{:S(2)}) collective-permute-start(f32[2,128,128]{2,1,0:T(8,128)S(1)} %slice.40), channel_id=1, source_target_pairs={{0,1},{1,0},{2,3},{3,2},{4,5},{5,4},{6,7},{7,6},{8,9},{9,8},{10,11... | collective-permute-start | bytes 393224 | tf_op jit(solution)/shard_map/ppermute | solution.py:445
  16.3 1.4 %collective-permute-start.7 = (f32[1,128,128]{2,1,0:T(8,128)S(1)}, f32[1,128,128]{2,1,0:T(8,128)S(1)}, u32[]{:S(2)}, u32[]{:S(2)}) collective-permute-start(f32[1,128,128]{2,1,0:T(8,128)S(1)} %slice.41), channel_id=1, source_target_pairs={{0,1},{1,0},{2,3},{3,2},{4,5},{5,4},{6,7},{7,6},{8,9},{9,8},{10,11... | collective-permute-start | bytes 196616 | tf_op jit(solution)/shard_map/ppermute | solution.py:445
  20.2 5.6 %collective-permute-start.9 = (f32[2,128,128]{2,1,0:T(8,128)S(1)}, f32[2,128,128]{2,1,0:T(8,128)S(1)}, u32[]{:S(2)}, u32[]{:S(2)}) collective-permute-start(f32[2,128,128]{2,1,0:T(8,128)S(1)} %get-tuple-element.33), channel_id=1, source_target_pairs={{0,16},{1,17},{2,18},{3,19},{4,20},{5,21},{6,22},{7,23},{8,24},{9,... | collective-permute-start | bytes 393224 | tf_op jit(solution)/shard_map/ppermute | solution.py:445
  26.1 5.1 %collective-permute-start.12 = (f32[3,128,128]{2,1,0:T(8,128)S(1)}, f32[3,128,128]{2,1,0:T(8,128)S(1)}, u32[]{:S(2)}, u32[]{:S(2)}) collective-permute-start(f32[3,128,128]{2,1,0:T(8,128)S(1)} %shard_map.62.own.rest_0_), channel_id=1, source_target_pairs={{1,2},{2,1},{3,4},{4,3},{5,6},{6,5},{7,8},{8,7},{9,10},{10,9},{11,... | collective-permute-start | bytes 589832 | tf_op jit(solution)/shard_map/ppermute | solution.py:445
  27.6 2.1 %collective-permute-start.10 = (f32[2,128,128]{2,1,0:T(8,128)S(1)}, f32[2,128,128]{2,1,0:T(8,128)S(1)}, u32[]{:S(2)}, u32[]{:S(2)}) collective-permute-start(f32[2,128,128]{2,1,0:T(8,128)S(1)} %slice.42), channel_id=1, source_target_pairs={{0,1},{1,0},{2,3},{3,2},{4,5},{5,4},{6,7},{7,6},{8,9},{9,8},{10,11... | collective-permute-start | bytes 393224 | tf_op jit(solution)/shard_map/ppermute | solution.py:445
  28.0 1.8 %collective-permute-start.11 = (f32[1,128,128]{2,1,0:T(8,128)S(1)}, f32[1,128,128]{2,1,0:T(8,128)S(1)}, u32[]{:S(2)}, u32[]{:S(2)}) collective-permute-start(f32[1,128,128]{2,1,0:T(8,128)S(1)} %slice.43), channel_id=1, source_target_pairs={{0,1},{1,0},{2,3},{3,2},{4,5},{5,4},{6,7},{7,6},{8,9},{9,8},{10,11... | collective-permute-start | bytes 196616 | tf_op jit(solution)/shard_map/ppermute | solution.py:445
  31.8 5.6 %collective-permute-start.15 = (f32[2,128,128]{2,1,0:T(8,128)S(1)}, f32[2,128,128]{2,1,0:T(8,128)S(1)}, u32[]{:S(2)}, u32[]{:S(2)}) collective-permute-start(f32[2,128,128]{2,1,0:T(8,128)S(1)} %get-tuple-element.35), channel_id=1, source_target_pairs={{0,16},{1,17},{2,18},{3,19},{4,20},{5,21},{6,22},{7,23},{8,24},{9,... | collective-permute-start | bytes 393224 | tf_op jit(solution)/shard_map/ppermute | solution.py:445
  33.4 7.9 %collective-permute-start.18 = (f32[3,128,128]{2,1,0:T(8,128)S(1)}, f32[3,128,128]{2,1,0:T(8,128)S(1)}, u32[]{:S(2)}, u32[]{:S(2)}) collective-permute-start(f32[3,128,128]{2,1,0:T(8,128)S(1)} %get-tuple-element.34.own), channel_id=1, source_target_pairs={{1,2},{2,1},{3,4},{4,3},{5,6},{6,5},{7,8},{8,7},{9,10},{10,9},{11,... | collective-permute-start | bytes 589832 | tf_op jit(solution)/shard_map/ppermute | solution.py:445
  34.6 2.8 %collective-permute-start.14 = (f32[1,128,128]{2,1,0:T(8,128)S(1)}, f32[1,128,128]{2,1,0:T(8,128)S(1)}, u32[]{:S(2)}, u32[]{:S(2)}) collective-permute-start(f32[1,128,128]{2,1,0:T(8,128)S(1)} %slice.35), channel_id=1, source_target_pairs={{0,1},{1,0},{2,3},{3,2},{4,5},{5,4},{6,7},{7,6},{8,9},{9,8},{10,11... | collective-permute-start | bytes 196616 | tf_op jit(solution)/shard_map/ppermute | solution.py:445
  34.6 3.3 %collective-permute-start.13 = (f32[2,128,128]{2,1,0:T(8,128)S(1)}, f32[2,128,128]{2,1,0:T(8,128)S(1)}, u32[]{:S(2)}, u32[]{:S(2)}) collective-permute-start(f32[2,128,128]{2,1,0:T(8,128)S(1)} %slice.34), channel_id=1, source_target_pairs={{0,1},{1,0},{2,3},{3,2},{4,5},{5,4},{6,7},{7,6},{8,9},{9,8},{10,11... | collective-permute-start | bytes 393224 | tf_op jit(solution)/shard_map/ppermute | solution.py:445
  35.1 5.0 %collective-permute-start.19 = (f32[264,128]{1,0:T(8,128)S(1)}, f32[264,128]{1,0:T(8,128)S(1)}, u32[]{:S(2)}, u32[]{:S(2)}) collective-permute-start(f32[264,128]{1,0:T(8,128)S(1)} %get-tuple-element.38), channel_id=1, source_target_pairs={{1,18},{2,17},{3,20},{4,19},{5,22},{6,21},{7,24},{8,23},{9,26},{10... | collective-permute-start | bytes 405512 | tf_op jit(solution)/shard_map/ppermute | solution.py:445
  37.3 1.3 %collective-permute-start.17 = (f32[1,128,128]{2,1,0:T(8,128)S(1)}, f32[1,128,128]{2,1,0:T(8,128)S(1)}, u32[]{:S(2)}, u32[]{:S(2)}) collective-permute-start(f32[1,128,128]{2,1,0:T(8,128)S(1)} %get-tuple-element.41), channel_id=1, source_target_pairs={{0,1},{1,0},{2,3},{3,2},{4,5},{5,4},{6,7},{7,6},{8,9},{9,8},{10,11... | collective-permute-start | bytes 196616 | tf_op jit(solution)/shard_map/ppermute | solution.py:445
  37.4 1.4 %collective-permute-start.16 = (f32[1,128,128]{2,1,0:T(8,128)S(1)}, f32[1,128,128]{2,1,0:T(8,128)S(1)}, u32[]{:S(2)}, u32[]{:S(2)}) collective-permute-start(f32[1,128,128]{2,1,0:T(8,128)S(1)} %get-tuple-element.42), channel_id=1, source_target_pairs={{0,1},{1,0},{2,3},{3,2},{4,5},{5,4},{6,7},{7,6},{8,9},{9,8},{10,11... | collective-permute-start | bytes 196616 | tf_op jit(solution)/shard_map/ppermute | solution.py:445
  41.7 5.7 %collective-permute-start.22 = (f32[3,128,128]{2,1,0:T(8,128)S(1)}, f32[3,128,128]{2,1,0:T(8,128)S(1)}, u32[]{:S(2)}, u32[]{:S(2)}) collective-permute-start(f32[3,128,128]{2,1,0:T(8,128)S(1)} %shard_map.67.own), channel_id=1, source_target_pairs={{1,2},{2,1},{3,4},{4,3},{5,6},{6,5},{7,8},{8,7},{9,10},{10,9},{11,... | collective-permute-start | bytes 589832 | tf_op jit(solution)/shard_map/ppermute | solution.py:445
  41.7 1.8 %collective-permute-start.20 = (f32[2,128,128]{2,1,0:T(8,128)S(1)}, f32[2,128,128]{2,1,0:T(8,128)S(1)}, u32[]{:S(2)}, u32[]{:S(2)}) collective-permute-start(f32[2,128,128]{2,1,0:T(8,128)S(1)} %slice.46), channel_id=1, source_target_pairs={{0,1},{1,0},{2,3},{3,2},{4,5},{5,4},{6,7},{7,6},{8,9},{9,8},{10,11... | collective-permute-start | bytes 393224 | tf_op jit(solution)/shard_map/ppermute | solution.py:445
  42.3 1.3 %collective-permute-start.21 = (f32[1,128,128]{2,1,0:T(8,128)S(1)}, f32[1,128,128]{2,1,0:T(8,128)S(1)}, u32[]{:S(2)}, u32[]{:S(2)}) collective-permute-start(f32[1,128,128]{2,1,0:T(8,128)S(1)} %slice.47), channel_id=1, source_target_pairs={{0,1},{1,0},{2,3},{3,2},{4,5},{5,4},{6,7},{7,6},{8,9},{9,8},{10,11... | collective-permute-start | bytes 196616 | tf_op jit(solution)/shard_map/ppermute | solution.py:445
  47.8 5.0 %collective-permute-start.23 = (f32[2,128,128]{2,1,0:T(8,128)S(1)}, f32[2,128,128]{2,1,0:T(8,128)S(1)}, u32[]{:S(2)}, u32[]{:S(2)}) collective-permute-start(f32[2,128,128]{2,1,0:T(8,128)S(1)} %get-tuple-element.40), channel_id=1, source_target_pairs={{0,16},{1,17},{2,18},{3,19},{4,20},{5,21},{6,22},{7,23},{8,24},{9,... | collective-permute-start | bytes 393224 | tf_op jit(solution)/shard_map/ppermute | solution.py:445
  (1 other events, 1.5 us)

commit v5 on v4

--- a/solution.py
+++ b/solution.py
@@ -270,10 +270,12 @@
     return [ref[k * size:(k + 1) * size, :] for k in range(2)]
 
 
-def first_fine_kernel(matrix, own, core, core_last, part):
-    @pl.when(lax.axis_index("lvl") == 0)
-    def _():
-        part[...] = near(matrix, joined(blocks_of(own, core, core_last))).reshape(part.shape)
+def first_fine_kernel(matrix, own, *rest):
+    *core, part = rest
+
+    @pl.when(lax.axis_index("lvl") == 0)
+    def _():
+        part[...] = near(matrix, joined(blocks_of(own, *core))).reshape(part.shape)
 
 
 def first_near_kernel(fine_part, matrix, own, down_own, down_core, mid_own, mid_core, mid_core_last, part, level):
@@ -335,11 +337,9 @@
         part[...] = own_slots(matrix, (0, 1), (blocks_of(own), blocks_of(core, core_last)))
 
 
-def second_kernel(matrix, level, own, part, cross, prolong, smooth, fixes):
-    @pl.when(lax.axis_index("lvl") == 0)
-    def _():
-        second = part[...] + far(matrix, joined(blocks_of(cross))).reshape(part.shape)
-        smooth[...] = COEF_ZERO * level[...] + COEF_ONE * own[...] + COEF_TWO * second
+def fix_kernel(matrix, level, own, part, cross, prolong, smooth, fixes):
+    @pl.when(lax.axis_index("lvl") == 0)
+    def _():
         fixes[...] = jnp.zeros_like(fixes)
 
     @pl.when(lax.axis_index("lvl") != 0)
@@ -350,22 +350,27 @@
         size = coarse.shape[0]
         up = product(prolong[:4 * size, :size], split_columns(coarse))
         low, high = value[0] + up[:size], value[2] + up[size:]
+        fixes[0] = low + coarse
+        fixes[1] = high + coarse
         smooth[0] = low
         smooth[1] = coarse
         smooth[2] = high
-        fixes[0] = low + coarse
-        fixes[1] = high + coarse
-
-
-def solution_kernel(smooth, fixes, prolong, *rest):
-    result = rest[-1]
-
-    @pl.when(lax.axis_index("lvl") == 0)
-    def _():
-        value = smooth[...] + product(prolong[...], joined((fixes[0], fixes[1]))).reshape(smooth.shape)
-        if len(rest) == 2:
-            value = value + rest[0][...]
-        result[...] = value
+
+
+def smooth_kernel(passed, matrix, level, own, part, cross, *rest):
+    smooth = rest[-1]
+
+    @pl.when(lax.axis_index("lvl") == 0)
+    def _():
+        second = part[...] + far(matrix, joined(blocks_of(cross))).reshape(part.shape)
+        value = COEF_ZERO * level[...] + COEF_ONE * own[...] + COEF_TWO * second
+        smooth[...] = value if len(rest) == 1 else rest[0][...] + value
+
+
+def solution_kernel(smooth, fixes, prolong, result):
+    @pl.when(lax.axis_index("lvl") == 0)
+    def _():
+        result[...] = smooth[...] + product(prolong[...], joined(blocks_of(fixes))).reshape(smooth.shape)
 
     @pl.when(lax.axis_index("lvl") != 0)
     def _():
@@ -433,7 +438,7 @@
     fine += [(rows + r, rows + (r ^ 1)) for r in range(rows)]
     short = [(r, across[r]) for r in range(1, rows - 1)] + [(rows + r, rows + (r ^ 1)) for r in range(2, rows - 2)]
     for end, beside in ((0, 1), (rows - 1, rows - 2)):
-        short += [(end, rows + end), (rows + end, rows + beside), (rows + beside, end)]
+        short += [(end, rows + beside), (rows + beside, rows + end), (rows + end, end)]
     other = [(r, r ^ 1) for r in range(2, rows - 2)] + [(rows + r, rows + across[r]) for r in range(1, rows - 1)]
     for end, beside in ((0, 1), (rows - 1, rows - 2)):
         other += [(rows + end, end), (end, beside), (beside, rows + end)]
@@ -508,7 +513,7 @@
             )
             (tall,) = call(tall_kernel, [((2 * big + 4 * size, 3 * big), BF16)], [matrix, restrict])
         else:
-            beyond, beside = fine(payload), [core(payload[:-1]), core(payload[-1:])]
+            beyond, beside = fine(payload), [core(payload)]
             mid_core = [core(mid_here[:1]), core(mid_here[1:])]
             (part,) = call(first_fine_kernel, [blocks], [matrix, payload, *beside])
             part, level_resid = call(
@@ -520,10 +525,12 @@
             (first,) = call(first_far_kernel, [blocks], [matrix, part, beyond, down[2], mid_cross])
         first_cross = cross(first)
         (part,) = call(near_kernel, [blocks], [matrix, first, core(first[:-1]), core(first[-1:])])
-        smooth, fixes = call(second_kernel, [blocks, pair], [matrix, level_resid, first, part, first_cross, prolong])
+        known = [matrix, level_resid, first, part, first_cross]
+        smooth, fixes = call(fix_kernel, [blocks, pair], [*known, prolong])
         fixes = level(fixes)
-        args = [smooth, fixes, prolong] + ([] if cycle == 0 else [result])
-        (result,) = call(solution_kernel, [blocks], args)
+        before = [] if cycle == 0 else [result]
+        (smooth,) = call(smooth_kernel, [blocks], [smooth, *known, *before], aliases={0: 0})
+        (result,) = call(solution_kernel, [blocks], [smooth, fixes, prolong])
     return result[None, None]
 
 

time: 53.9 us -> 52.7 us (0.978); the launches traced: 53.8 us -> 52 us
  waiting for transfers between devices: 26.4 us -> 23.4 us
  starting transfers between devices: 16.6 us -> 17.8 us
    ppermute x24 -> x23, waiting for transfers between devices: 26.4 us -> 23.4 us  [swaps(): lax.ppermute(x, ('lvl', 'row'), pairs)]
    ppermute x24 -> x23, starting transfers between devices: 16.6 us -> 17.8 us  [swaps(): lax.ppermute(x, ('lvl', 'row'), pairs)]
    pallas_call x16 -> x18, Pallas kernels: 10.5 us -> 10.5 us  [call(): pl.pallas_call(kernel, out_shape=[jax.ShapeDtypeStruct(shape, dtype) for...]
  transfers between devices with their start and end apart: 24 -> 23, of which waited for: 16 -> 15; matrix products, arithmetic and copies ran while one was open for 0% -> 0% of each run, Pallas kernels for 11% -> 13%
where the time goes in v5:
time: 52.7 us; the launch traced here: 52 us
  waiting for transfers between devices  23.4 us (44%)
  starting transfers between devices  17.8 us (34%)
  Pallas kernels  10.5 us (20%)
    ppermute x23, waiting for transfers between devices, swaps(): lax.ppermute(x, ('lvl', 'row'), pairs)  23.4 us
    ppermute x23, starting transfers between devices, swaps(): lax.ppermute(x, ('lvl', 'row'), pairs)  17.8 us
    pallas_call x18, Pallas kernels, call(): pl.pallas_call(kernel, out_shape=[jax.ShapeDtypeStruct(shape, dtype) for...  10.5 us
  transfers between devices with their start and end apart: 23, of which 15 were waited for; matrix products, arithmetic and copies ran while one was open for 0% of the time, Pallas kernels for 13%

profile of v5, /device:TPU:0, one launch (start us, length us, event | category | flops | bytes accessed | tf_op | source)
XLA Modules:
  0.0 52.0 jit_solution(5759998035760409468)
XLA Ops:
  0.0 1.4 %shard_map.56 = (f32[2,128,128]{2,1,0:T(8,128)S(1)}, f32[264,128]{1,0:T(8,128)S(1)}, f32[3,128,128]{2,1,0:T(8,128)S(1)}, f32[264,128]{1,0:T(8,128)S(1)}, bf16[512,384]{1,0:T(8,128)(2,1)S(1)}) custom-call(s32[1,1,2,3]{3,2,1,0:T(2,128)} %bitcast.11, f32[3,128,128]{2,1,0:T(8,128)} %bitcast.6, f32[3,2,128,128]{3,2,1,0:T(8,128)} %bitcast.8), custom_call_target="tpu_custom_call" | custom-call | tf_op jit(solution)/shard_map/pallas_call | solution.py:420
  1.4 2.7 %collective-permute-start.1 = (f32[2,128,128]{2,1,0:T(8,128)S(1)}, f32[2,128,128]{2,1,0:T(8,128)S(1)}, u32[]{:S(2)}, u32[]{:S(2)}) collective-permute-start(f32[2,128,128]{2,1,0:T(8,128)S(1)} %get-tuple-element.26.before), channel_id=1, source_target_pairs={{0,16},{1,17},{2,18},{3,19},{4,20},{5,21},{6,22},{7,23},{8,24},{9,... | collective-permute-start | bytes 393224 | tf_op jit(solution)/shard_map/ppermute | solution.py:450
  4.3 1.4 %collective-permute-start.4 = (f32[264,128]{1,0:T(8,128)S(1)}, f32[264,128]{1,0:T(8,128)S(1)}, u32[]{:S(2)}, u32[]{:S(2)}) collective-permute-start(f32[264,128]{1,0:T(8,128)S(1)} %get-tuple-element.29), channel_id=1, source_target_pairs={{2,3},{3,2},{4,5},{5,4},{6,7},{7,6},{8,9},{9,8},{10,11},{11,10},{1... | collective-permute-start | bytes 405512 | tf_op jit(solution)/shard_map/ppermute | solution.py:450
  6.2 1.4 %collective-permute-done.1.mid_own = f32[2,128,128]{2,1,0:T(8,128)S(1)} collective-permute-done((f32[2,128,128]{2,1,0:T(8,128)S(1)}, f32[2,128,128]{2,1,0:T(8,128)S(1)}, u32[]{:S(2)}, u32[]{:S(2)}) %collective-permute-start.1) | collective-permute-done | bytes 131104 | tf_op jit(solution)/shard_map/ppermute | solution.py:450
  7.6 1.7 %shard_map.55 = (bf16[768,1152]{1,0:T(8,128)(2,1)S(1)}, bf16[768,256]{1,0:T(8,128)(2,1)S(1)}) custom-call(s32[1,3,1,7]{3,2,1,0:T(1,128)} %bitcast.13, s32[1,1,2,3]{3,2,1,0:T(2,128)} %bitcast.12, f32[3,2,128,128]{3,2,1,0:T(8,128)} %bitcast.9, f32[3,7,128,128]{3,2,1,0:T(8,128)} %bitcast.10), custom_call_target="tpu_custom_call" | custom-call | tf_op jit(solution)/shard_map/pallas_call | solution.py:420
  9.8 1.4 %collective-permute-done.4.down_cross = f32[264,128]{1,0:T(8,128)S(1)} collective-permute-done((f32[264,128]{1,0:T(8,128)S(1)}, f32[264,128]{1,0:T(8,128)S(1)}, u32[]{:S(2)}, u32[]{:S(2)}) %collective-permute-start.4) | collective-permute-done | bytes 135200 | tf_op jit(solution)/shard_map/ppermute | solution.py:450
  11.2 1.4 %collective-permute-done.5.skewed = f32[264,128]{1,0:T(8,128)S(1)} collective-permute-done((f32[264,128]{1,0:T(8,128)S(1)}, f32[264,128]{1,0:T(8,128)S(1)}, u32[]{:S(2)}, u32[]{:S(2)}) %collective-permute-start.5) | collective-permute-done | bytes 135200 | tf_op jit(solution)/shard_map/ppermute | solution.py:450
  13.1 0.8 %collective-permute-start.6 = (f32[2,128,128]{2,1,0:T(8,128)S(1)}, f32[2,128,128]{2,1,0:T(8,128)S(1)}, u32[]{:S(2)}, u32[]{:S(2)}) collective-permute-start(f32[2,128,128]{2,1,0:T(8,128)S(1)} %slice.32), channel_id=1, source_target_pairs={{0,1},{1,0},{2,3},{3,2},{4,5},{5,4},{6,7},{7,6},{8,9},{9,8},{10,11... | collective-permute-start | bytes 393224 | tf_op jit(solution)/shard_map/ppermute | solution.py:450
  14.0 1.2 %collective-permute-done.7.core_last = f32[1,128,128]{2,1,0:T(8,128)S(1)} collective-permute-done((f32[1,128,128]{2,1,0:T(8,128)S(1)}, f32[1,128,128]{2,1,0:T(8,128)S(1)}, u32[]{:S(2)}, u32[]{:S(2)}) %collective-permute-start.7) | collective-permute-done | bytes 65568 | tf_op jit(solution)/shard_map/ppermute | solution.py:450
  15.7 3.1 %collective-permute-done.8.cross = f32[3,128,128]{2,1,0:T(8,128)S(1)} collective-permute-done((f32[3,128,128]{2,1,0:T(8,128)S(1)}, f32[3,128,128]{2,1,0:T(8,128)S(1)}, u32[]{:S(2)}, u32[]{:S(2)}) %collective-permute-start.8) | collective-permute-done | bytes 196640 | tf_op jit(solution)/shard_map/ppermute | solution.py:450
  18.8 1.3 %collective-permute-start.9 = (f32[2,128,128]{2,1,0:T(8,128)S(1)}, f32[2,128,128]{2,1,0:T(8,128)S(1)}, u32[]{:S(2)}, u32[]{:S(2)}) collective-permute-start(f32[2,128,128]{2,1,0:T(8,128)S(1)} %get-tuple-element.33), channel_id=1, source_target_pairs={{0,16},{1,17},{2,18},{3,19},{4,20},{5,21},{6,22},{7,23},{8,24},{9,... | collective-permute-start | bytes 393224 | tf_op jit(solution)/shard_map/ppermute | solution.py:450
  20.5 4.2 %collective-permute-done.9.fixes = f32[2,128,128]{2,1,0:T(8,128)S(1)} collective-permute-done((f32[2,128,128]{2,1,0:T(8,128)S(1)}, f32[2,128,128]{2,1,0:T(8,128)S(1)}, u32[]{:S(2)}, u32[]{:S(2)}) %collective-permute-start.9) | collective-permute-done | bytes 131104 | tf_op jit(solution)/shard_map/ppermute | solution.py:450
  24.9 1.0 %collective-permute-start.12 = (f32[3,128,128]{2,1,0:T(8,128)S(1)}, f32[3,128,128]{2,1,0:T(8,128)S(1)}, u32[]{:S(2)}, u32[]{:S(2)}) collective-permute-start(f32[3,128,128]{2,1,0:T(8,128)S(1)} %shard_map.63.own.rest_0_), channel_id=1, source_target_pairs={{1,2},{2,1},{3,4},{4,3},{5,6},{6,5},{7,8},{8,7},{9,10},{10,9},{11,... | collective-permute-start | bytes 589832 | tf_op jit(solution)/shard_map/ppermute | solution.py:450
  26.0 2.0 %collective-permute-start.10 = (f32[2,128,128]{2,1,0:T(8,128)S(1)}, f32[2,128,128]{2,1,0:T(8,128)S(1)}, u32[]{:S(2)}, u32[]{:S(2)}) collective-permute-start(f32[2,128,128]{2,1,0:T(8,128)S(1)} %slice.34), channel_id=1, source_target_pairs={{0,1},{1,0},{2,3},{3,2},{4,5},{5,4},{6,7},{7,6},{8,9},{9,8},{10,11... | collective-permute-start | bytes 393224 | tf_op jit(solution)/shard_map/ppermute | solution.py:450
  28.1 1.5 %shard_map.57.tall = bf16[1280,1152]{1,0:T(8,128)(2,1)S(1)} custom-call(bf16[768,1152]{1,0:T(8,128)(2,1)S(1)} %get-tuple-element.23.matrix, bf16[512,384]{1,0:T(8,128)(2,1)S(1)} %get-tuple-element.24.restrict), custom_call_target="tpu_custom_call" | custom-call | tf_op jit(solution)/shard_map/pallas_call | solution.py:420
  29.7 0.7 %shard_map.64.part = f32[640,128]{1,0:T(8,128)S(1)} custom-call(bf16[1280,1152]{1,0:T(8,128)(2,1)S(1)} %shard_map.57.tall, f32[3,128,128]{2,1,0:T(8,128)S(1)} %shard_map.63.own.rest_0_, f32[2,128,128]{2,1,0:T(8,128)S(1)} %collective-permute-done.10.core, f32[1,128,128]{2,1,0:T(8,128)S(1)} %collective-permute-done.11.core_last), custom_call_target="tpu_custom_call" | custom-call | tf_op jit(solution)/shard_map/pallas_call | solution.py:420
  31.2 2.9 %collective-permute-start.17 = (f32[3,128,128]{2,1,0:T(8,128)S(1)}, f32[3,128,128]{2,1,0:T(8,128)S(1)}, u32[]{:S(2)}, u32[]{:S(2)}) collective-permute-start(f32[3,128,128]{2,1,0:T(8,128)S(1)} %get-tuple-element.34.own), channel_id=1, source_target_pairs={{1,2},{2,1},{3,4},{4,3},{5,6},{6,5},{7,8},{8,7},{9,10},{10,9},{11,... | collective-permute-start | bytes 589832 | tf_op jit(solution)/shard_map/ppermute | solution.py:450
  34.6 2.6 %collective-permute-done.14.mid_own = f32[2,128,128]{2,1,0:T(8,128)S(1)} collective-permute-done((f32[2,128,128]{2,1,0:T(8,128)S(1)}, f32[2,128,128]{2,1,0:T(8,128)S(1)}, u32[]{:S(2)}, u32[]{:S(2)}) %collective-permute-start.14) | collective-permute-done | bytes 131104 | tf_op jit(solution)/shard_map/ppermute | solution.py:450
  40.1 2.0 %collective-permute-start.19 = (f32[2,128,128]{2,1,0:T(8,128)S(1)}, f32[2,128,128]{2,1,0:T(8,128)S(1)}, u32[]{:S(2)}, u32[]{:S(2)}) collective-permute-start(f32[2,128,128]{2,1,0:T(8,128)S(1)} %slice.38), channel_id=1, source_target_pairs={{0,1},{1,0},{2,3},{3,2},{4,5},{5,4},{6,7},{7,6},{8,9},{9,8},{10,11... | collective-permute-start | bytes 393224 | tf_op jit(solution)/shard_map/ppermute | solution.py:450
  42.1 1.2 %collective-permute-done.20.core_last = f32[1,128,128]{2,1,0:T(8,128)S(1)} collective-permute-done((f32[1,128,128]{2,1,0:T(8,128)S(1)}, f32[1,128,128]{2,1,0:T(8,128)S(1)}, u32[]{:S(2)}, u32[]{:S(2)}) %collective-permute-start.20) | collective-permute-done | bytes 65568 | tf_op jit(solution)/shard_map/ppermute | solution.py:450
  43.8 1.5 %collective-permute-done.21.cross = f32[3,128,128]{2,1,0:T(8,128)S(1)} collective-permute-done((f32[3,128,128]{2,1,0:T(8,128)S(1)}, f32[3,128,128]{2,1,0:T(8,128)S(1)}, u32[]{:S(2)}, u32[]{:S(2)}) %collective-permute-start.21) | collective-permute-done | bytes 196640 | tf_op jit(solution)/shard_map/ppermute | solution.py:450
  45.3 1.0 %collective-permute-start.22 = (f32[2,128,128]{2,1,0:T(8,128)S(1)}, f32[2,128,128]{2,1,0:T(8,128)S(1)}, u32[]{:S(2)}, u32[]{:S(2)}) collective-permute-start(f32[2,128,128]{2,1,0:T(8,128)S(1)} %get-tuple-element.40), channel_id=1, source_target_pairs={{0,16},{1,17},{2,18},{3,19},{4,20},{5,21},{6,22},{7,23},{8,24},{9,... | collective-permute-start | bytes 393224 | tf_op jit(solution)/shard_map/ppermute | solution.py:450
  46.7 4.3 %collective-permute-done.22.fixes = f32[2,128,128]{2,1,0:T(8,128)S(1)} collective-permute-done((f32[2,128,128]{2,1,0:T(8,128)S(1)}, f32[2,128,128]{2,1,0:T(8,128)S(1)}, u32[]{:S(2)}, u32[]{:S(2)}) %collective-permute-start.22) | collective-permute-done | bytes 131104 | tf_op jit(solution)/shard_map/ppermute | solution.py:450
  51.0 0.9 %shard_map.72 = f32[3,128,128]{2,1,0:T(8,128)} custom-call(f32[3,128,128]{2,1,0:T(8,128)S(1)} %shard_map.71.smooth, f32[2,128,128]{2,1,0:T(8,128)S(1)} %collective-permute-done.22.fixes, bf16[768,256]{1,0:T(8,128)(2,1)S(1)} %get-tuple-element.31.prolong), custom_call_target="tpu_custom_call" | custom-call | tf_op jit(solution)/shard_map/pallas_call | solution.py:420
  (49 shorter events, 8.1 us)
Async XLA Ops:
  1.4 6.2 %collective-permute-start.1 = (f32[2,128,128]{2,1,0:T(8,128)S(1)}, f32[2,128,128]{2,1,0:T(8,128)S(1)}, u32[]{:S(2)}, u32[]{:S(2)}) collective-permute-start(f32[2,128,128]{2,1,0:T(8,128)S(1)} %get-tuple-element.26.before), channel_id=1, source_target_pairs={{0,16},{1,17},{2,18},{3,19},{4,20},{5,21},{6,22},{7,23},{8,24},{9,... | collective-permute-start | bytes 393224 | tf_op jit(solution)/shard_map/ppermute | solution.py:450
  4.1 5.2 %collective-permute-start = (f32[3,128,128]{2,1,0:T(8,128)S(1)}, f32[3,128,128]{2,1,0:T(8,128)S(1)}, u32[]{:S(2)}, u32[]{:S(2)}) collective-permute-start(f32[3,128,128]{2,1,0:T(8,128)S(1)} %get-tuple-element.25.own.down_own), channel_id=1, source_target_pairs={{0,1},{1,0},{2,3},{3,2},{4,5},{5,4},{6,7},{7,6},{8,9},{9,8},{10,11... | collective-permute-start | bytes 589832 | tf_op jit(solution)/shard_map/ppermute | solution.py:450
  4.1 8.6 %collective-permute-start.3 = (f32[3,128,128]{2,1,0:T(8,128)S(1)}, f32[3,128,128]{2,1,0:T(8,128)S(1)}, u32[]{:S(2)}, u32[]{:S(2)}) collective-permute-start(f32[3,128,128]{2,1,0:T(8,128)S(1)} %get-tuple-element.25.own.down_own), channel_id=1, source_target_pairs={{1,2},{2,1},{3,4},{4,3},{5,6},{6,5},{7,8},{8,7},{9,10},{10,9},{11,... | collective-permute-start | bytes 589832 | tf_op jit(solution)/shard_map/ppermute | solution.py:450
  4.3 6.9 %collective-permute-start.4 = (f32[264,128]{1,0:T(8,128)S(1)}, f32[264,128]{1,0:T(8,128)S(1)}, u32[]{:S(2)}, u32[]{:S(2)}) collective-permute-start(f32[264,128]{1,0:T(8,128)S(1)} %get-tuple-element.29), channel_id=1, source_target_pairs={{2,3},{3,2},{4,5},{5,4},{6,7},{7,6},{8,9},{9,8},{10,11},{11,10},{1... | collective-permute-start | bytes 405512 | tf_op jit(solution)/shard_map/ppermute | solution.py:450
  5.7 6.9 %collective-permute-start.5 = (f32[264,128]{1,0:T(8,128)S(1)}, f32[264,128]{1,0:T(8,128)S(1)}, u32[]{:S(2)}, u32[]{:S(2)}) collective-permute-start(f32[264,128]{1,0:T(8,128)S(1)} %get-tuple-element.30), channel_id=1, source_target_pairs={{1,18},{2,17},{3,20},{4,19},{5,22},{6,21},{7,24},{8,23},{9,26},{10... | collective-permute-start | bytes 405512 | tf_op jit(solution)/shard_map/ppermute | solution.py:450
  7.6 1.7 %collective-permute-start.2 = (f32[2,128,128]{2,1,0:T(8,128)S(1)}, f32[2,128,128]{2,1,0:T(8,128)S(1)}, u32[]{:S(2)}, u32[]{:S(2)}) collective-permute-start(f32[2,128,128]{2,1,0:T(8,128)S(1)} %collective-permute-done.1.mid_own), channel_id=1, source_target_pairs={{0,1},{1,0},{2,3},{3,2},{4,5},{5,4},{6,7},{7,6},{8,9},{9,8},{10,11... | collective-permute-start | bytes 393224 | tf_op jit(solution)/shard_map/ppermute | solution.py:450
  13.0 5.7 %collective-permute-start.8 = (f32[3,128,128]{2,1,0:T(8,128)S(1)}, f32[3,128,128]{2,1,0:T(8,128)S(1)}, u32[]{:S(2)}, u32[]{:S(2)}) collective-permute-start(f32[3,128,128]{2,1,0:T(8,128)S(1)} %shard_map.59.own), channel_id=1, source_target_pairs={{1,2},{2,1},{3,4},{4,3},{5,6},{6,5},{7,8},{8,7},{9,10},{10,9},{11,... | collective-permute-start | bytes 589832 | tf_op jit(solution)/shard_map/ppermute | solution.py:450
  13.1 2.1 %collective-permute-start.6 = (f32[2,128,128]{2,1,0:T(8,128)S(1)}, f32[2,128,128]{2,1,0:T(8,128)S(1)}, u32[]{:S(2)}, u32[]{:S(2)}) collective-permute-start(f32[2,128,128]{2,1,0:T(8,128)S(1)} %slice.32), channel_id=1, source_target_pairs={{0,1},{1,0},{2,3},{3,2},{4,5},{5,4},{6,7},{7,6},{8,9},{9,8},{10,11... | collective-permute-start | bytes 393224 | tf_op jit(solution)/shard_map/ppermute | solution.py:450
  13.9 1.3 %collective-permute-start.7 = (f32[1,128,128]{2,1,0:T(8,128)S(1)}, f32[1,128,128]{2,1,0:T(8,128)S(1)}, u32[]{:S(2)}, u32[]{:S(2)}) collective-permute-start(f32[1,128,128]{2,1,0:T(8,128)S(1)} %slice.33), channel_id=1, source_target_pairs={{0,1},{1,0},{2,3},{3,2},{4,5},{5,4},{6,7},{7,6},{8,9},{9,8},{10,11... | collective-permute-start | bytes 196616 | tf_op jit(solution)/shard_map/ppermute | solution.py:450
  18.8 5.9 %collective-permute-start.9 = (f32[2,128,128]{2,1,0:T(8,128)S(1)}, f32[2,128,128]{2,1,0:T(8,128)S(1)}, u32[]{:S(2)}, u32[]{:S(2)}) collective-permute-start(f32[2,128,128]{2,1,0:T(8,128)S(1)} %get-tuple-element.33), channel_id=1, source_target_pairs={{0,16},{1,17},{2,18},{3,19},{4,20},{5,21},{6,22},{7,23},{8,24},{9,... | collective-permute-start | bytes 393224 | tf_op jit(solution)/shard_map/ppermute | solution.py:450
  24.9 5.7 %collective-permute-start.12 = (f32[3,128,128]{2,1,0:T(8,128)S(1)}, f32[3,128,128]{2,1,0:T(8,128)S(1)}, u32[]{:S(2)}, u32[]{:S(2)}) collective-permute-start(f32[3,128,128]{2,1,0:T(8,128)S(1)} %shard_map.63.own.rest_0_), channel_id=1, source_target_pairs={{1,2},{2,1},{3,4},{4,3},{5,6},{6,5},{7,8},{8,7},{9,10},{10,9},{11,... | collective-permute-start | bytes 589832 | tf_op jit(solution)/shard_map/ppermute | solution.py:450
  26.0 3.7 %collective-permute-start.10 = (f32[2,128,128]{2,1,0:T(8,128)S(1)}, f32[2,128,128]{2,1,0:T(8,128)S(1)}, u32[]{:S(2)}, u32[]{:S(2)}) collective-permute-start(f32[2,128,128]{2,1,0:T(8,128)S(1)} %slice.34), channel_id=1, source_target_pairs={{0,1},{1,0},{2,3},{3,2},{4,5},{5,4},{6,7},{7,6},{8,9},{9,8},{10,11... | collective-permute-start | bytes 393224 | tf_op jit(solution)/shard_map/ppermute | solution.py:450
  28.0 1.6 %collective-permute-start.11 = (f32[1,128,128]{2,1,0:T(8,128)S(1)}, f32[1,128,128]{2,1,0:T(8,128)S(1)}, u32[]{:S(2)}, u32[]{:S(2)}) collective-permute-start(f32[1,128,128]{2,1,0:T(8,128)S(1)} %slice.35), channel_id=1, source_target_pairs={{0,1},{1,0},{2,3},{3,2},{4,5},{5,4},{6,7},{7,6},{8,9},{9,8},{10,11... | collective-permute-start | bytes 196616 | tf_op jit(solution)/shard_map/ppermute | solution.py:450
  29.6 1.0 %copy-start = (f32[1,1,3,128,128]{4,3,2,1,0:T(8,128)S(1)}, f32[1,1,3,128,128]{4,3,2,1,0:T(8,128)}, u32[]{:S(2)}) copy-start(f32[1,1,3,128,128]{4,3,2,1,0:T(8,128)} %param.5) | copy-start | bytes 589828
  31.2 6.1 %collective-permute-start.14 = (f32[2,128,128]{2,1,0:T(8,128)S(1)}, f32[2,128,128]{2,1,0:T(8,128)S(1)}, u32[]{:S(2)}, u32[]{:S(2)}) collective-permute-start(f32[2,128,128]{2,1,0:T(8,128)S(1)} %get-tuple-element.35), channel_id=1, source_target_pairs={{0,16},{1,17},{2,18},{3,19},{4,20},{5,21},{6,22},{7,23},{8,24},{9,... | collective-permute-start | bytes 393224 | tf_op jit(solution)/shard_map/ppermute | solution.py:450
  31.2 8.0 %collective-permute-start.17 = (f32[3,128,128]{2,1,0:T(8,128)S(1)}, f32[3,128,128]{2,1,0:T(8,128)S(1)}, u32[]{:S(2)}, u32[]{:S(2)}) collective-permute-start(f32[3,128,128]{2,1,0:T(8,128)S(1)} %get-tuple-element.34.own), channel_id=1, source_target_pairs={{1,2},{2,1},{3,4},{4,3},{5,6},{6,5},{7,8},{8,7},{9,10},{10,9},{11,... | collective-permute-start | bytes 589832 | tf_op jit(solution)/shard_map/ppermute | solution.py:450
  34.1 3.7 %collective-permute-start.13 = (f32[3,128,128]{2,1,0:T(8,128)S(1)}, f32[3,128,128]{2,1,0:T(8,128)S(1)}, u32[]{:S(2)}, u32[]{:S(2)}) collective-permute-start(f32[3,128,128]{2,1,0:T(8,128)S(1)} %get-tuple-element.34.own), channel_id=1, source_target_pairs={{0,1},{1,0},{2,3},{3,2},{4,5},{5,4},{6,7},{7,6},{8,9},{9,8},{10,11... | collective-permute-start | bytes 589832 | tf_op jit(solution)/shard_map/ppermute | solution.py:450
  34.1 5.0 %collective-permute-start.18 = (f32[264,128]{1,0:T(8,128)S(1)}, f32[264,128]{1,0:T(8,128)S(1)}, u32[]{:S(2)}, u32[]{:S(2)}) collective-permute-start(f32[264,128]{1,0:T(8,128)S(1)} %get-tuple-element.38), channel_id=1, source_target_pairs={{1,18},{2,17},{3,20},{4,19},{5,22},{6,21},{7,24},{8,23},{9,26},{10... | collective-permute-start | bytes 405512 | tf_op jit(solution)/shard_map/ppermute | solution.py:450
  37.3 1.3 %collective-permute-start.16 = (f32[1,128,128]{2,1,0:T(8,128)S(1)}, f32[1,128,128]{2,1,0:T(8,128)S(1)}, u32[]{:S(2)}, u32[]{:S(2)}) collective-permute-start(f32[1,128,128]{2,1,0:T(8,128)S(1)} %get-tuple-element.41), channel_id=1, source_target_pairs={{0,1},{1,0},{2,3},{3,2},{4,5},{5,4},{6,7},{7,6},{8,9},{9,8},{10,11... | collective-permute-start | bytes 196616 | tf_op jit(solution)/shard_map/ppermute | solution.py:450
  37.3 1.4 %collective-permute-start.15 = (f32[1,128,128]{2,1,0:T(8,128)S(1)}, f32[1,128,128]{2,1,0:T(8,128)S(1)}, u32[]{:S(2)}, u32[]{:S(2)}) collective-permute-start(f32[1,128,128]{2,1,0:T(8,128)S(1)} %get-tuple-element.42), channel_id=1, source_target_pairs={{0,1},{1,0},{2,3},{3,2},{4,5},{5,4},{6,7},{7,6},{8,9},{9,8},{10,11... | collective-permute-start | bytes 196616 | tf_op jit(solution)/shard_map/ppermute | solution.py:450
  39.6 5.7 %collective-permute-start.21 = (f32[3,128,128]{2,1,0:T(8,128)S(1)}, f32[3,128,128]{2,1,0:T(8,128)S(1)}, u32[]{:S(2)}, u32[]{:S(2)}) collective-permute-start(f32[3,128,128]{2,1,0:T(8,128)S(1)} %shard_map.68.own), channel_id=1, source_target_pairs={{1,2},{2,1},{3,4},{4,3},{5,6},{6,5},{7,8},{8,7},{9,10},{10,9},{11,... | collective-permute-start | bytes 589832 | tf_op jit(solution)/shard_map/ppermute | solution.py:450
  40.1 3.2 %collective-permute-start.19 = (f32[2,128,128]{2,1,0:T(8,128)S(1)}, f32[2,128,128]{2,1,0:T(8,128)S(1)}, u32[]{:S(2)}, u32[]{:S(2)}) collective-permute-start(f32[2,128,128]{2,1,0:T(8,128)S(1)} %slice.38), channel_id=1, source_target_pairs={{0,1},{1,0},{2,3},{3,2},{4,5},{5,4},{6,7},{7,6},{8,9},{9,8},{10,11... | collective-permute-start | bytes 393224 | tf_op jit(solution)/shard_map/ppermute | solution.py:450
  42.0 1.3 %collective-permute-start.20 = (f32[1,128,128]{2,1,0:T(8,128)S(1)}, f32[1,128,128]{2,1,0:T(8,128)S(1)}, u32[]{:S(2)}, u32[]{:S(2)}) collective-permute-start(f32[1,128,128]{2,1,0:T(8,128)S(1)} %slice.39), channel_id=1, source_target_pairs={{0,1},{1,0},{2,3},{3,2},{4,5},{5,4},{6,7},{7,6},{8,9},{9,8},{10,11... | collective-permute-start | bytes 196616 | tf_op jit(solution)/shard_map/ppermute | solution.py:450
  45.3 5.7 %collective-permute-start.22 = (f32[2,128,128]{2,1,0:T(8,128)S(1)}, f32[2,128,128]{2,1,0:T(8,128)S(1)}, u32[]{:S(2)}, u32[]{:S(2)}) collective-permute-start(f32[2,128,128]{2,1,0:T(8,128)S(1)} %get-tuple-element.40), channel_id=1, source_target_pairs={{0,16},{1,17},{2,18},{3,19},{4,20},{5,21},{6,22},{7,23},{8,24},{9,... | collective-permute-start | bytes 393224 | tf_op jit(solution)/shard_map/ppermute | solution.py:450

commit v6 on v5

--- a/solution.py
+++ b/solution.py
@@ -327,7 +327,9 @@
         first[...] = part[...] + own_slots(matrix, (2,), (beside,))
 
 
-def near_kernel(matrix, own, core, core_last, part):
+def near_kernel(matrix, own, core, core_last, *rest):
+    part = rest[-1]
+
     @pl.when(lax.axis_index("lvl") == 0)
     def _():
         part[...] = near(matrix, joined(blocks_of(own, core, core_last))).reshape(part.shape)
@@ -397,20 +399,34 @@
         part[...] = near(tall, joined(blocks_of(own, core, core_last)))
 
 
-def residual_far_kernel(tall, part, cross, rhs, before, resid, mids, skewed):
-    big, size = rhs.shape[0] * rhs.shape[1], rhs.shape[1]
-
-    @pl.when(lax.axis_index("lvl") == 0)
-    def _():
-        value = part[...] + far(tall, joined(blocks_of(cross)))
-        store_mids(before[...].reshape(2 * size, -1) - value[big:], mids, skewed)
-        resid[...] = rhs[...] - value[:big].reshape(rhs.shape)
-
-    @pl.when(lax.axis_index("lvl") != 0)
-    def _():
-        resid[...] = jnp.zeros_like(resid)
+def residual_mid_kernel(tall, part, cross, before, mids, skewed):
+    size = mids.shape[1]
+    big, half = part.shape[0] - 2 * size, tall.shape[0] // 2
+
+    @pl.when(lax.axis_index("lvl") == 0)
+    def _():
+        columns = 2 * (tall.shape[1] // 3)
+        left = stacked(tall[big:half, columns:], tall[half + big:, columns:])
+        value = part[big:, :] + product(left, joined(blocks_of(cross)))
+        store_mids(before[...].reshape(2 * size, -1) - value, mids, skewed)
+
+    @pl.when(lax.axis_index("lvl") != 0)
+    def _():
         mids[...] = jnp.zeros_like(mids)
         skewed[...] = jnp.zeros_like(skewed)
+
+
+def residual_far_kernel(matrix, part, cross, rhs, resid):
+    big = rhs.shape[0] * rhs.shape[1]
+
+    @pl.when(lax.axis_index("lvl") == 0)
+    def _():
+        value = part[:big, :] + far(matrix, joined(blocks_of(cross)))
+        resid[...] = rhs[...] - value.reshape(rhs.shape)
+
+    @pl.when(lax.axis_index("lvl") != 0)
+    def _():
+        resid[...] = jnp.zeros_like(resid)
 
 
 def call(kernel, outs, args, anywhere=0, scratch=(), aliases={}):
@@ -478,11 +494,8 @@
                 [((big + 2 * size, width), F32)],
                 [tall, result, core(result[:-1]), core(result[-1:])],
             )
-            payload, mids, skewed = call(
-                residual_far_kernel,
-                [blocks, pair, long],
-                [tall, part, result_cross, right, mids],
-            )
+            mids, skewed = call(residual_mid_kernel, [pair, long], [tall, part, result_cross, mids])
+            (payload,) = call(residual_far_kernel, [blocks], [matrix, part, result_cross, right])
         mid_here, mid_cross = level(mids), skew(skewed)
         if cycle == 0:
             beyond, beside, mid_core = short(payload), [core(payload)], [core(mid_here)]
@@ -524,7 +537,7 @@
             )
             (first,) = call(first_far_kernel, [blocks], [matrix, part, beyond, down[2], mid_cross])
         first_cross = cross(first)
-        (part,) = call(near_kernel, [blocks], [matrix, first, core(first[:-1]), core(first[-1:])])
+        (part,) = call(near_kernel, [blocks], [matrix, first, core(first[:-1]), core(first[-1:])] + ([tall] if cycle == 0 else []))
         known = [matrix, level_resid, first, part, first_cross]
         smooth, fixes = call(fix_kernel, [blocks, pair], [*known, prolong])
         fixes = level(fixes)

time: 52.7 us -> 52.7 us (level); the launches traced: 52 us -> 52.5 us
  waiting for transfers between devices: 23.4 us -> 24.8 us
  starting transfers between devices: 17.8 us -> 16.8 us
    ppermute x23, waiting for transfers between devices: 23.4 us -> 24.8 us  [swaps(): lax.ppermute(x, ('lvl', 'row'), pairs)]
    ppermute x23, starting transfers between devices: 17.8 us -> 16.8 us  [swaps(): lax.ppermute(x, ('lvl', 'row'), pairs)]
    pallas_call x18 -> x19, Pallas kernels: 10.5 us -> 10.7 us  [call(): pl.pallas_call(kernel, out_shape=[jax.ShapeDtypeStruct(shape, dtype) for...]
where the time goes in v6:
time: 52.7 us; the launch traced here: 52.5 us
  waiting for transfers between devices  24.8 us (47%)
  starting transfers between devices  16.8 us (32%)
  Pallas kernels  10.7 us (20%)
    ppermute x23, waiting for transfers between devices, swaps(): lax.ppermute(x, ('lvl', 'row'), pairs)  24.8 us
    ppermute x23, starting transfers between devices, swaps(): lax.ppermute(x, ('lvl', 'row'), pairs)  16.8 us
    pallas_call x19, Pallas kernels, call(): pl.pallas_call(kernel, out_shape=[jax.ShapeDtypeStruct(shape, dtype) for...  10.7 us
  transfers between devices with their start and end apart: 23, of which 15 were waited for; matrix products, arithmetic and copies ran while one was open for 0% of the time, Pallas kernels for 13%

profile of v6, /device:TPU:0, one launch (start us, length us, event | category | flops | bytes accessed | tf_op | source)
XLA Modules:
  0.0 52.5 jit_solution(5716519736402255592)
XLA Ops:
  0.0 1.4 %shard_map.56 = (f32[2,128,128]{2,1,0:T(8,128)S(1)}, f32[264,128]{1,0:T(8,128)S(1)}, f32[3,128,128]{2,1,0:T(8,128)S(1)}, f32[264,128]{1,0:T(8,128)S(1)}, bf16[512,384]{1,0:T(8,128)(2,1)S(1)}) custom-call(s32[1,1,2,3]{3,2,1,0:T(2,128)} %bitcast.11, f32[3,128,128]{2,1,0:T(8,128)} %bitcast.6, f32[3,2,128,128]{3,2,1,0:T(8,128)} %bitcast.8), custom_call_target="tpu_custom_call" | custom-call | tf_op jit(solution)/shard_map/pallas_call | solution.py:436
  1.4 2.7 %collective-permute-start.1 = (f32[2,128,128]{2,1,0:T(8,128)S(1)}, f32[2,128,128]{2,1,0:T(8,128)S(1)}, u32[]{:S(2)}, u32[]{:S(2)}) collective-permute-start(f32[2,128,128]{2,1,0:T(8,128)S(1)} %get-tuple-element.25.before), channel_id=1, source_target_pairs={{0,16},{1,17},{2,18},{3,19},{4,20},{5,21},{6,22},{7,23},{8,24},{9,... | collective-permute-start | bytes 393224 | tf_op jit(solution)/shard_map/ppermute | solution.py:466
  4.3 1.4 %collective-permute-start.4 = (f32[264,128]{1,0:T(8,128)S(1)}, f32[264,128]{1,0:T(8,128)S(1)}, u32[]{:S(2)}, u32[]{:S(2)}) collective-permute-start(f32[264,128]{1,0:T(8,128)S(1)} %get-tuple-element.28), channel_id=1, source_target_pairs={{2,3},{3,2},{4,5},{5,4},{6,7},{7,6},{8,9},{9,8},{10,11},{11,10},{1... | collective-permute-start | bytes 405512 | tf_op jit(solution)/shard_map/ppermute | solution.py:466
  6.2 1.4 %collective-permute-done.1.mid_own = f32[2,128,128]{2,1,0:T(8,128)S(1)} collective-permute-done((f32[2,128,128]{2,1,0:T(8,128)S(1)}, f32[2,128,128]{2,1,0:T(8,128)S(1)}, u32[]{:S(2)}, u32[]{:S(2)}) %collective-permute-start.1) | collective-permute-done | bytes 131104 | tf_op jit(solution)/shard_map/ppermute | solution.py:466
  7.6 1.7 %shard_map.55 = (bf16[768,1152]{1,0:T(8,128)(2,1)S(1)}, bf16[768,256]{1,0:T(8,128)(2,1)S(1)}) custom-call(s32[1,3,1,7]{3,2,1,0:T(1,128)} %bitcast.13, s32[1,1,2,3]{3,2,1,0:T(2,128)} %bitcast.12, f32[3,2,128,128]{3,2,1,0:T(8,128)} %bitcast.9, f32[3,7,128,128]{3,2,1,0:T(8,128)} %bitcast.10), custom_call_target="tpu_custom_call" | custom-call | tf_op jit(solution)/shard_map/pallas_call | solution.py:436
  9.8 1.4 %collective-permute-done.4.down_cross = f32[264,128]{1,0:T(8,128)S(1)} collective-permute-done((f32[264,128]{1,0:T(8,128)S(1)}, f32[264,128]{1,0:T(8,128)S(1)}, u32[]{:S(2)}, u32[]{:S(2)}) %collective-permute-start.4) | collective-permute-done | bytes 135200 | tf_op jit(solution)/shard_map/ppermute | solution.py:466
  11.2 1.4 %collective-permute-done.5.skewed = f32[264,128]{1,0:T(8,128)S(1)} collective-permute-done((f32[264,128]{1,0:T(8,128)S(1)}, f32[264,128]{1,0:T(8,128)S(1)}, u32[]{:S(2)}, u32[]{:S(2)}) %collective-permute-start.5) | collective-permute-done | bytes 135200 | tf_op jit(solution)/shard_map/ppermute | solution.py:466
  13.1 0.8 %collective-permute-start.6 = (f32[2,128,128]{2,1,0:T(8,128)S(1)}, f32[2,128,128]{2,1,0:T(8,128)S(1)}, u32[]{:S(2)}, u32[]{:S(2)}) collective-permute-start(f32[2,128,128]{2,1,0:T(8,128)S(1)} %slice.32), channel_id=1, source_target_pairs={{0,1},{1,0},{2,3},{3,2},{4,5},{5,4},{6,7},{7,6},{8,9},{9,8},{10,11... | collective-permute-start | bytes 393224 | tf_op jit(solution)/shard_map/ppermute | solution.py:466
  14.0 1.6 %shard_map.57.rest_0_.tall = bf16[1280,1152]{1,0:T(8,128)(2,1)S(1)} custom-call(bf16[768,1152]{1,0:T(8,128)(2,1)S(1)} %get-tuple-element.22.matrix, bf16[512,384]{1,0:T(8,128)(2,1)S(1)} %get-tuple-element.23.restrict), custom_call_target="tpu_custom_call" | custom-call | tf_op jit(solution)/shard_map/pallas_call | solution.py:436
  16.1 2.6 %collective-permute-done.8.cross = f32[3,128,128]{2,1,0:T(8,128)S(1)} collective-permute-done((f32[3,128,128]{2,1,0:T(8,128)S(1)}, f32[3,128,128]{2,1,0:T(8,128)S(1)}, u32[]{:S(2)}, u32[]{:S(2)}) %collective-permute-start.8) | collective-permute-done | bytes 196640 | tf_op jit(solution)/shard_map/ppermute | solution.py:466
  18.8 1.3 %collective-permute-start.9 = (f32[2,128,128]{2,1,0:T(8,128)S(1)}, f32[2,128,128]{2,1,0:T(8,128)S(1)}, u32[]{:S(2)}, u32[]{:S(2)}) collective-permute-start(f32[2,128,128]{2,1,0:T(8,128)S(1)} %get-tuple-element.32), channel_id=1, source_target_pairs={{0,16},{1,17},{2,18},{3,19},{4,20},{5,21},{6,22},{7,23},{8,24},{9,... | collective-permute-start | bytes 393224 | tf_op jit(solution)/shard_map/ppermute | solution.py:466
  20.5 4.2 %collective-permute-done.9.fixes = f32[2,128,128]{2,1,0:T(8,128)S(1)} collective-permute-done((f32[2,128,128]{2,1,0:T(8,128)S(1)}, f32[2,128,128]{2,1,0:T(8,128)S(1)}, u32[]{:S(2)}, u32[]{:S(2)}) %collective-permute-start.9) | collective-permute-done | bytes 131104 | tf_op jit(solution)/shard_map/ppermute | solution.py:466
  24.9 1.0 %collective-permute-start.12 = (f32[3,128,128]{2,1,0:T(8,128)S(1)}, f32[3,128,128]{2,1,0:T(8,128)S(1)}, u32[]{:S(2)}, u32[]{:S(2)}) collective-permute-start(f32[3,128,128]{2,1,0:T(8,128)S(1)} %shard_map.63.own.rest_0_), channel_id=1, source_target_pairs={{1,2},{2,1},{3,4},{4,3},{5,6},{6,5},{7,8},{8,7},{9,10},{10,9},{11,... | collective-permute-start | bytes 589832 | tf_op jit(solution)/shard_map/ppermute | solution.py:466
  26.0 2.0 %collective-permute-start.10 = (f32[2,128,128]{2,1,0:T(8,128)S(1)}, f32[2,128,128]{2,1,0:T(8,128)S(1)}, u32[]{:S(2)}, u32[]{:S(2)}) collective-permute-start(f32[2,128,128]{2,1,0:T(8,128)S(1)} %slice.34), channel_id=1, source_target_pairs={{0,1},{1,0},{2,3},{3,2},{4,5},{5,4},{6,7},{7,6},{8,9},{9,8},{10,11... | collective-permute-start | bytes 393224 | tf_op jit(solution)/shard_map/ppermute | solution.py:466
  28.1 1.2 %collective-permute-done.11.core_last = f32[1,128,128]{2,1,0:T(8,128)S(1)} collective-permute-done((f32[1,128,128]{2,1,0:T(8,128)S(1)}, f32[1,128,128]{2,1,0:T(8,128)S(1)}, u32[]{:S(2)}, u32[]{:S(2)}) %collective-permute-start.11) | collective-permute-done | bytes 65568 | tf_op jit(solution)/shard_map/ppermute | solution.py:466
  29.3 0.7 %shard_map.64.part = f32[640,128]{1,0:T(8,128)S(1)} custom-call(bf16[1280,1152]{1,0:T(8,128)(2,1)S(1)} %shard_map.57.rest_0_.tall, f32[3,128,128]{2,1,0:T(8,128)S(1)} %shard_map.63.own.rest_0_, f32[2,128,128]{2,1,0:T(8,128)S(1)} %collective-permute-done.10.core, f32[1,128,128]{2,1,0:T(8,128)S(1)} %collective-permute-done.11.core_last), custom_call_target="tpu_custom_call" | custom-call | tf_op jit(solution)/shard_map/pallas_call | solution.py:436
  30.0 0.7 %collective-permute-done.12.cross = f32[3,128,128]{2,1,0:T(8,128)S(1)} collective-permute-done((f32[3,128,128]{2,1,0:T(8,128)S(1)}, f32[3,128,128]{2,1,0:T(8,128)S(1)}, u32[]{:S(2)}, u32[]{:S(2)}) %collective-permute-start.12) | collective-permute-done | bytes 196640 | tf_op jit(solution)/shard_map/ppermute | solution.py:466
  31.4 2.6 %collective-permute-start.17 = (f32[3,128,128]{2,1,0:T(8,128)S(1)}, f32[3,128,128]{2,1,0:T(8,128)S(1)}, u32[]{:S(2)}, u32[]{:S(2)}) collective-permute-start(f32[3,128,128]{2,1,0:T(8,128)S(1)} %shard_map.65.own), channel_id=1, source_target_pairs={{1,2},{2,1},{3,4},{4,3},{5,6},{6,5},{7,8},{8,7},{9,10},{10,9},{11,... | collective-permute-start | bytes 589832 | tf_op jit(solution)/shard_map/ppermute | solution.py:466
  34.5 2.5 %collective-permute-done.14.mid_own = f32[2,128,128]{2,1,0:T(8,128)S(1)} collective-permute-done((f32[2,128,128]{2,1,0:T(8,128)S(1)}, f32[2,128,128]{2,1,0:T(8,128)S(1)}, u32[]{:S(2)}, u32[]{:S(2)}) %collective-permute-start.14) | collective-permute-done | bytes 131104 | tf_op jit(solution)/shard_map/ppermute | solution.py:466
  39.9 2.0 %collective-permute-start.19 = (f32[2,128,128]{2,1,0:T(8,128)S(1)}, f32[2,128,128]{2,1,0:T(8,128)S(1)}, u32[]{:S(2)}, u32[]{:S(2)}) collective-permute-start(f32[2,128,128]{2,1,0:T(8,128)S(1)} %slice.38), channel_id=1, source_target_pairs={{0,1},{1,0},{2,3},{3,2},{4,5},{5,4},{6,7},{7,6},{8,9},{9,8},{10,11... | collective-permute-start | bytes 393224 | tf_op jit(solution)/shard_map/ppermute | solution.py:466
  42.0 1.2 %collective-permute-done.20.core_last = f32[1,128,128]{2,1,0:T(8,128)S(1)} collective-permute-done((f32[1,128,128]{2,1,0:T(8,128)S(1)}, f32[1,128,128]{2,1,0:T(8,128)S(1)}, u32[]{:S(2)}, u32[]{:S(2)}) %collective-permute-start.20) | collective-permute-done | bytes 65568 | tf_op jit(solution)/shard_map/ppermute | solution.py:466
  43.6 1.9 %collective-permute-done.21.cross = f32[3,128,128]{2,1,0:T(8,128)S(1)} collective-permute-done((f32[3,128,128]{2,1,0:T(8,128)S(1)}, f32[3,128,128]{2,1,0:T(8,128)S(1)}, u32[]{:S(2)}, u32[]{:S(2)}) %collective-permute-start.21) | collective-permute-done | bytes 196640 | tf_op jit(solution)/shard_map/ppermute | solution.py:466
  46.5 5.1 %collective-permute-done.22.fixes = f32[2,128,128]{2,1,0:T(8,128)S(1)} collective-permute-done((f32[2,128,128]{2,1,0:T(8,128)S(1)}, f32[2,128,128]{2,1,0:T(8,128)S(1)}, u32[]{:S(2)}, u32[]{:S(2)}) %collective-permute-start.22) | collective-permute-done | bytes 131104 | tf_op jit(solution)/shard_map/ppermute | solution.py:466
  51.6 1.0 %shard_map.73 = f32[3,128,128]{2,1,0:T(8,128)} custom-call(f32[3,128,128]{2,1,0:T(8,128)S(1)} %shard_map.72.smooth, f32[2,128,128]{2,1,0:T(8,128)S(1)} %collective-permute-done.22.fixes, bf16[768,256]{1,0:T(8,128)(2,1)S(1)} %get-tuple-element.30.prolong), custom_call_target="tpu_custom_call" | custom-call | tf_op jit(solution)/shard_map/pallas_call | solution.py:436
  (50 shorter events, 8.5 us)
Async XLA Ops:
  1.4 6.2 %collective-permute-start.1 = (f32[2,128,128]{2,1,0:T(8,128)S(1)}, f32[2,128,128]{2,1,0:T(8,128)S(1)}, u32[]{:S(2)}, u32[]{:S(2)}) collective-permute-start(f32[2,128,128]{2,1,0:T(8,128)S(1)} %get-tuple-element.25.before), channel_id=1, source_target_pairs={{0,16},{1,17},{2,18},{3,19},{4,20},{5,21},{6,22},{7,23},{8,24},{9,... | collective-permute-start | bytes 393224 | tf_op jit(solution)/shard_map/ppermute | solution.py:466
  4.1 5.2 %collective-permute-start = (f32[3,128,128]{2,1,0:T(8,128)S(1)}, f32[3,128,128]{2,1,0:T(8,128)S(1)}, u32[]{:S(2)}, u32[]{:S(2)}) collective-permute-start(f32[3,128,128]{2,1,0:T(8,128)S(1)} %get-tuple-element.24.own.down_own), channel_id=1, source_target_pairs={{0,1},{1,0},{2,3},{3,2},{4,5},{5,4},{6,7},{7,6},{8,9},{9,8},{10,11... | collective-permute-start | bytes 589832 | tf_op jit(solution)/shard_map/ppermute | solution.py:466
  4.1 8.6 %collective-permute-start.3 = (f32[3,128,128]{2,1,0:T(8,128)S(1)}, f32[3,128,128]{2,1,0:T(8,128)S(1)}, u32[]{:S(2)}, u32[]{:S(2)}) collective-permute-start(f32[3,128,128]{2,1,0:T(8,128)S(1)} %get-tuple-element.24.own.down_own), channel_id=1, source_target_pairs={{1,2},{2,1},{3,4},{4,3},{5,6},{6,5},{7,8},{8,7},{9,10},{10,9},{11,... | collective-permute-start | bytes 589832 | tf_op jit(solution)/shard_map/ppermute | solution.py:466
  4.3 6.9 %collective-permute-start.4 = (f32[264,128]{1,0:T(8,128)S(1)}, f32[264,128]{1,0:T(8,128)S(1)}, u32[]{:S(2)}, u32[]{:S(2)}) collective-permute-start(f32[264,128]{1,0:T(8,128)S(1)} %get-tuple-element.28), channel_id=1, source_target_pairs={{2,3},{3,2},{4,5},{5,4},{6,7},{7,6},{8,9},{9,8},{10,11},{11,10},{1... | collective-permute-start | bytes 405512 | tf_op jit(solution)/shard_map/ppermute | solution.py:466
  5.7 6.9 %collective-permute-start.5 = (f32[264,128]{1,0:T(8,128)S(1)}, f32[264,128]{1,0:T(8,128)S(1)}, u32[]{:S(2)}, u32[]{:S(2)}) collective-permute-start(f32[264,128]{1,0:T(8,128)S(1)} %get-tuple-element.29), channel_id=1, source_target_pairs={{1,18},{2,17},{3,20},{4,19},{5,22},{6,21},{7,24},{8,23},{9,26},{10... | collective-permute-start | bytes 405512 | tf_op jit(solution)/shard_map/ppermute | solution.py:466
  7.6 1.7 %collective-permute-start.2 = (f32[2,128,128]{2,1,0:T(8,128)S(1)}, f32[2,128,128]{2,1,0:T(8,128)S(1)}, u32[]{:S(2)}, u32[]{:S(2)}) collective-permute-start(f32[2,128,128]{2,1,0:T(8,128)S(1)} %collective-permute-done.1.mid_own), channel_id=1, source_target_pairs={{0,1},{1,0},{2,3},{3,2},{4,5},{5,4},{6,7},{7,6},{8,9},{9,8},{10,11... | collective-permute-start | bytes 393224 | tf_op jit(solution)/shard_map/ppermute | solution.py:466
  13.0 5.7 %collective-permute-start.8 = (f32[3,128,128]{2,1,0:T(8,128)S(1)}, f32[3,128,128]{2,1,0:T(8,128)S(1)}, u32[]{:S(2)}, u32[]{:S(2)}) collective-permute-start(f32[3,128,128]{2,1,0:T(8,128)S(1)} %shard_map.59.own), channel_id=1, source_target_pairs={{1,2},{2,1},{3,4},{4,3},{5,6},{6,5},{7,8},{8,7},{9,10},{10,9},{11,... | collective-permute-start | bytes 589832 | tf_op jit(solution)/shard_map/ppermute | solution.py:466
  13.1 2.5 %collective-permute-start.6 = (f32[2,128,128]{2,1,0:T(8,128)S(1)}, f32[2,128,128]{2,1,0:T(8,128)S(1)}, u32[]{:S(2)}, u32[]{:S(2)}) collective-permute-start(f32[2,128,128]{2,1,0:T(8,128)S(1)} %slice.32), channel_id=1, source_target_pairs={{0,1},{1,0},{2,3},{3,2},{4,5},{5,4},{6,7},{7,6},{8,9},{9,8},{10,11... | collective-permute-start | bytes 393224 | tf_op jit(solution)/shard_map/ppermute | solution.py:466
  13.9 1.7 %collective-permute-start.7 = (f32[1,128,128]{2,1,0:T(8,128)S(1)}, f32[1,128,128]{2,1,0:T(8,128)S(1)}, u32[]{:S(2)}, u32[]{:S(2)}) collective-permute-start(f32[1,128,128]{2,1,0:T(8,128)S(1)} %slice.33), channel_id=1, source_target_pairs={{0,1},{1,0},{2,3},{3,2},{4,5},{5,4},{6,7},{7,6},{8,9},{9,8},{10,11... | collective-permute-start | bytes 196616 | tf_op jit(solution)/shard_map/ppermute | solution.py:466
  18.8 5.9 %collective-permute-start.9 = (f32[2,128,128]{2,1,0:T(8,128)S(1)}, f32[2,128,128]{2,1,0:T(8,128)S(1)}, u32[]{:S(2)}, u32[]{:S(2)}) collective-permute-start(f32[2,128,128]{2,1,0:T(8,128)S(1)} %get-tuple-element.32), channel_id=1, source_target_pairs={{0,16},{1,17},{2,18},{3,19},{4,20},{5,21},{6,22},{7,23},{8,24},{9,... | collective-permute-start | bytes 393224 | tf_op jit(solution)/shard_map/ppermute | solution.py:466
  24.9 5.7 %collective-permute-start.12 = (f32[3,128,128]{2,1,0:T(8,128)S(1)}, f32[3,128,128]{2,1,0:T(8,128)S(1)}, u32[]{:S(2)}, u32[]{:S(2)}) collective-permute-start(f32[3,128,128]{2,1,0:T(8,128)S(1)} %shard_map.63.own.rest_0_), channel_id=1, source_target_pairs={{1,2},{2,1},{3,4},{4,3},{5,6},{6,5},{7,8},{8,7},{9,10},{10,9},{11,... | collective-permute-start | bytes 589832 | tf_op jit(solution)/shard_map/ppermute | solution.py:466
  26.0 3.3 %collective-permute-start.10 = (f32[2,128,128]{2,1,0:T(8,128)S(1)}, f32[2,128,128]{2,1,0:T(8,128)S(1)}, u32[]{:S(2)}, u32[]{:S(2)}) collective-permute-start(f32[2,128,128]{2,1,0:T(8,128)S(1)} %slice.34), channel_id=1, source_target_pairs={{0,1},{1,0},{2,3},{3,2},{4,5},{5,4},{6,7},{7,6},{8,9},{9,8},{10,11... | collective-permute-start | bytes 393224 | tf_op jit(solution)/shard_map/ppermute | solution.py:466
  28.0 1.3 %collective-permute-start.11 = (f32[1,128,128]{2,1,0:T(8,128)S(1)}, f32[1,128,128]{2,1,0:T(8,128)S(1)}, u32[]{:S(2)}, u32[]{:S(2)}) collective-permute-start(f32[1,128,128]{2,1,0:T(8,128)S(1)} %slice.35), channel_id=1, source_target_pairs={{0,1},{1,0},{2,3},{3,2},{4,5},{5,4},{6,7},{7,6},{8,9},{9,8},{10,11... | collective-permute-start | bytes 196616 | tf_op jit(solution)/shard_map/ppermute | solution.py:466
  30.0 1.1 %copy-start = (f32[1,1,3,128,128]{4,3,2,1,0:T(8,128)S(1)}, f32[1,1,3,128,128]{4,3,2,1,0:T(8,128)}, u32[]{:S(2)}) copy-start(f32[1,1,3,128,128]{4,3,2,1,0:T(8,128)} %param.5) | copy-start | bytes 589828
  30.9 6.1 %collective-permute-start.14 = (f32[2,128,128]{2,1,0:T(8,128)S(1)}, f32[2,128,128]{2,1,0:T(8,128)S(1)}, u32[]{:S(2)}, u32[]{:S(2)}) collective-permute-start(f32[2,128,128]{2,1,0:T(8,128)S(1)} %get-tuple-element.33), channel_id=1, source_target_pairs={{0,16},{1,17},{2,18},{3,19},{4,20},{5,21},{6,22},{7,23},{8,24},{9,... | collective-permute-start | bytes 393224 | tf_op jit(solution)/shard_map/ppermute | solution.py:466
  31.4 8.0 %collective-permute-start.17 = (f32[3,128,128]{2,1,0:T(8,128)S(1)}, f32[3,128,128]{2,1,0:T(8,128)S(1)}, u32[]{:S(2)}, u32[]{:S(2)}) collective-permute-start(f32[3,128,128]{2,1,0:T(8,128)S(1)} %shard_map.65.own), channel_id=1, source_target_pairs={{1,2},{2,1},{3,4},{4,3},{5,6},{6,5},{7,8},{8,7},{9,10},{10,9},{11,... | collective-permute-start | bytes 589832 | tf_op jit(solution)/shard_map/ppermute | solution.py:466
  34.0 3.6 %collective-permute-start.13 = (f32[3,128,128]{2,1,0:T(8,128)S(1)}, f32[3,128,128]{2,1,0:T(8,128)S(1)}, u32[]{:S(2)}, u32[]{:S(2)}) collective-permute-start(f32[3,128,128]{2,1,0:T(8,128)S(1)} %shard_map.65.own), channel_id=1, source_target_pairs={{0,1},{1,0},{2,3},{3,2},{4,5},{5,4},{6,7},{7,6},{8,9},{9,8},{10,11... | collective-permute-start | bytes 589832 | tf_op jit(solution)/shard_map/ppermute | solution.py:466
  34.0 5.0 %collective-permute-start.18 = (f32[264,128]{1,0:T(8,128)S(1)}, f32[264,128]{1,0:T(8,128)S(1)}, u32[]{:S(2)}, u32[]{:S(2)}) collective-permute-start(f32[264,128]{1,0:T(8,128)S(1)} %get-tuple-element.36), channel_id=1, source_target_pairs={{1,18},{2,17},{3,20},{4,19},{5,22},{6,21},{7,24},{8,23},{9,26},{10... | collective-permute-start | bytes 405512 | tf_op jit(solution)/shard_map/ppermute | solution.py:466
  37.1 1.3 %collective-permute-start.16 = (f32[1,128,128]{2,1,0:T(8,128)S(1)}, f32[1,128,128]{2,1,0:T(8,128)S(1)}, u32[]{:S(2)}, u32[]{:S(2)}) collective-permute-start(f32[1,128,128]{2,1,0:T(8,128)S(1)} %get-tuple-element.39), channel_id=1, source_target_pairs={{0,1},{1,0},{2,3},{3,2},{4,5},{5,4},{6,7},{7,6},{8,9},{9,8},{10,11... | collective-permute-start | bytes 196616 | tf_op jit(solution)/shard_map/ppermute | solution.py:466
  37.1 1.4 %collective-permute-start.15 = (f32[1,128,128]{2,1,0:T(8,128)S(1)}, f32[1,128,128]{2,1,0:T(8,128)S(1)}, u32[]{:S(2)}, u32[]{:S(2)}) collective-permute-start(f32[1,128,128]{2,1,0:T(8,128)S(1)} %get-tuple-element.40), channel_id=1, source_target_pairs={{0,1},{1,0},{2,3},{3,2},{4,5},{5,4},{6,7},{7,6},{8,9},{9,8},{10,11... | collective-permute-start | bytes 196616 | tf_op jit(solution)/shard_map/ppermute | solution.py:466
  39.8 5.7 %collective-permute-start.21 = (f32[3,128,128]{2,1,0:T(8,128)S(1)}, f32[3,128,128]{2,1,0:T(8,128)S(1)}, u32[]{:S(2)}, u32[]{:S(2)}) collective-permute-start(f32[3,128,128]{2,1,0:T(8,128)S(1)} %shard_map.69.own), channel_id=1, source_target_pairs={{1,2},{2,1},{3,4},{4,3},{5,6},{6,5},{7,8},{8,7},{9,10},{10,9},{11,... | collective-permute-start | bytes 589832 | tf_op jit(solution)/shard_map/ppermute | solution.py:466
  39.9 3.3 %collective-permute-start.19 = (f32[2,128,128]{2,1,0:T(8,128)S(1)}, f32[2,128,128]{2,1,0:T(8,128)S(1)}, u32[]{:S(2)}, u32[]{:S(2)}) collective-permute-start(f32[2,128,128]{2,1,0:T(8,128)S(1)} %slice.38), channel_id=1, source_target_pairs={{0,1},{1,0},{2,3},{3,2},{4,5},{5,4},{6,7},{7,6},{8,9},{9,8},{10,11... | collective-permute-start | bytes 393224 | tf_op jit(solution)/shard_map/ppermute | solution.py:466
  41.9 1.3 %collective-permute-start.20 = (f32[1,128,128]{2,1,0:T(8,128)S(1)}, f32[1,128,128]{2,1,0:T(8,128)S(1)}, u32[]{:S(2)}, u32[]{:S(2)}) collective-permute-start(f32[1,128,128]{2,1,0:T(8,128)S(1)} %slice.39), channel_id=1, source_target_pairs={{0,1},{1,0},{2,3},{3,2},{4,5},{5,4},{6,7},{7,6},{8,9},{9,8},{10,11... | collective-permute-start | bytes 196616 | tf_op jit(solution)/shard_map/ppermute | solution.py:466
  45.5 6.1 %collective-permute-start.22 = (f32[2,128,128]{2,1,0:T(8,128)S(1)}, f32[2,128,128]{2,1,0:T(8,128)S(1)}, u32[]{:S(2)}, u32[]{:S(2)}) collective-permute-start(f32[2,128,128]{2,1,0:T(8,128)S(1)} %get-tuple-element.38), channel_id=1, source_target_pairs={{0,16},{1,17},{2,18},{3,19},{4,20},{5,21},{6,22},{7,23},{8,24},{9,... | collective-permute-start | bytes 393224 | tf_op jit(solution)/shard_map/ppermute | solution.py:466

commit v7 on v6

--- a/solution.py
+++ b/solution.py
@@ -226,6 +226,10 @@
     @pl.when(lax.axis_index("lvl") != 0)
     def _():
         prolong[:4 * size, :size] = split_rows(stacked(links[0, 1], links[2, 1]))
+        at, big = (2 * slots + 1) * size, slots * size
+        coarse = [matrix[first + size:first + 2 * size, at:at + size] for first in (0, big)]
+        lifted = product(prolong[:4 * size, :size], jnp.concatenate(coarse, axis=1))
+        prolong[:4 * size, size:] = split_rows(lifted)
 
 
 def joined(blocks):
@@ -327,8 +331,8 @@
         first[...] = part[...] + own_slots(matrix, (2,), (beside,))
 
 
-def near_kernel(matrix, own, core, core_last, *rest):
-    part = rest[-1]
+def near_kernel(matrix, own, core, core_last, level, prolong, *rest):
+    part, lift = rest[-2:]
 
     @pl.when(lax.axis_index("lvl") == 0)
     def _():
@@ -336,22 +340,28 @@
 
     @pl.when(lax.axis_index("lvl") != 0)
     def _():
-        part[...] = own_slots(matrix, (0, 1), (blocks_of(own), blocks_of(core, core_last)))
-
-
-def fix_kernel(matrix, level, own, part, cross, prolong, smooth, fixes):
+        size = own.shape[1]
+        beside = own_slots(matrix, (0, 1), (blocks_of(own), blocks_of(core, core_last)))
+        value = COEF_ZERO * level[...] + COEF_ONE * own[...] + COEF_TWO * beside
+        up = product(prolong[:4 * size, :size], split_columns(value[1]))
+        part[...] = value
+        lift[0] = value[0] + up[:size]
+        lift[1] = value[2] + up[size:]
+
+
+def fix_kernel(matrix, part, lift, cross, prolong, smooth, fixes):
     @pl.when(lax.axis_index("lvl") == 0)
     def _():
         fixes[...] = jnp.zeros_like(fixes)
 
     @pl.when(lax.axis_index("lvl") != 0)
     def _():
-        second = part[...] + own_slots(matrix, (2,), (blocks_of(cross),))
-        value = COEF_ZERO * level[...] + COEF_ONE * own[...] + COEF_TWO * second
-        coarse = value[1]
-        size = coarse.shape[0]
-        up = product(prolong[:4 * size, :size], split_columns(coarse))
-        low, high = value[0] + up[:size], value[2] + up[size:]
+        size = cross.shape[1]
+        up = product(prolong[:4 * size, size:], split_columns(cross[1]))
+        beyond = own_slots(matrix, (2,), (blocks_of(cross),))
+        coarse = part[1] + COEF_TWO * beyond[1]
+        low = lift[0] + COEF_TWO * (beyond[0] + up[:size])
+        high = lift[1] + COEF_TWO * (beyond[2] + up[size:])
         fixes[0] = low + coarse
         fixes[1] = high + coarse
         smooth[0] = low
@@ -537,9 +547,11 @@
             )
             (first,) = call(first_far_kernel, [blocks], [matrix, part, beyond, down[2], mid_cross])
         first_cross = cross(first)
-        (part,) = call(near_kernel, [blocks], [matrix, first, core(first[:-1]), core(first[-1:])] + ([tall] if cycle == 0 else []))
+        halves = [core(first[:-1]), core(first[-1:])]
+        more = [tall] if cycle == 0 else []
+        part, lift = call(near_kernel, [blocks, pair], [matrix, first, *halves, level_resid, prolong, *more])
         known = [matrix, level_resid, first, part, first_cross]
-        smooth, fixes = call(fix_kernel, [blocks, pair], [*known, prolong])
+        smooth, fixes = call(fix_kernel, [blocks, pair], [matrix, part, lift, first_cross, prolong])
         fixes = level(fixes)
         before = [] if cycle == 0 else [result]
         (smooth,) = call(smooth_kernel, [blocks], [smooth, *known, *before], aliases={0: 0})

time: 52.7 us -> 53.1 us (level)
  waiting for transfers between devices: 24.8 us -> 26.5 us
  starting transfers between devices: 16.8 us -> 15.5 us
    ppermute x23, waiting for transfers between devices: 24.8 us -> 26.5 us  [swaps(): lax.ppermute(x, ('lvl', 'row'), pairs)]
    ppermute x23, starting transfers between devices: 16.8 us -> 15.5 us  [swaps(): lax.ppermute(x, ('lvl', 'row'), pairs)]
where the time goes in v7:
time: 53.1 us; the launch traced here: 53 us
  waiting for transfers between devices  26.5 us (50%)
  starting transfers between devices  15.5 us (29%)
  Pallas kernels  10.6 us (20%)
    ppermute x23, waiting for transfers between devices, swaps(): lax.ppermute(x, ('lvl', 'row'), pairs)  26.5 us
    ppermute x23, starting transfers between devices, swaps(): lax.ppermute(x, ('lvl', 'row'), pairs)  15.5 us
    pallas_call x19, Pallas kernels, call(): pl.pallas_call(kernel, out_shape=[jax.ShapeDtypeStruct(shape, dtype) for...  10.6 us
  transfers between devices with their start and end apart: 23, of which 15 were waited for; matrix products, arithmetic and copies ran while one was open for 0% of the time, Pallas kernels for 13%

profile of v7, /device:TPU:0, one launch (start us, length us, event | category | flops | bytes accessed | tf_op | source)
XLA Modules:
  0.0 53.0 jit_solution(15037048393598692240)
XLA Ops:
  0.0 1.4 %shard_map.56 = (f32[2,128,128]{2,1,0:T(8,128)S(1)}, f32[264,128]{1,0:T(8,128)S(1)}, f32[3,128,128]{2,1,0:T(8,128)S(1)}, f32[264,128]{1,0:T(8,128)S(1)}, bf16[512,384]{1,0:T(8,128)(2,1)S(1)}) custom-call(s32[1,1,2,3]{3,2,1,0:T(2,128)} %bitcast.11, f32[3,128,128]{2,1,0:T(8,128)} %bitcast.6, f32[3,2,128,128]{3,2,1,0:T(8,128)} %bitcast.8), custom_call_target="tpu_custom_call" | custom-call | tf_op jit(solution)/shard_map/pallas_call | solution.py:446
  1.4 2.7 %collective-permute-start.1 = (f32[2,128,128]{2,1,0:T(8,128)S(1)}, f32[2,128,128]{2,1,0:T(8,128)S(1)}, u32[]{:S(2)}, u32[]{:S(2)}) collective-permute-start(f32[2,128,128]{2,1,0:T(8,128)S(1)} %get-tuple-element.29.before), channel_id=1, source_target_pairs={{0,16},{1,17},{2,18},{3,19},{4,20},{5,21},{6,22},{7,23},{8,24},{9,... | collective-permute-start | bytes 393224 | tf_op jit(solution)/shard_map/ppermute | solution.py:476
  4.3 1.4 %collective-permute-start.4 = (f32[264,128]{1,0:T(8,128)S(1)}, f32[264,128]{1,0:T(8,128)S(1)}, u32[]{:S(2)}, u32[]{:S(2)}) collective-permute-start(f32[264,128]{1,0:T(8,128)S(1)} %get-tuple-element.31), channel_id=1, source_target_pairs={{2,3},{3,2},{4,5},{5,4},{6,7},{7,6},{8,9},{9,8},{10,11},{11,10},{1... | collective-permute-start | bytes 405512 | tf_op jit(solution)/shard_map/ppermute | solution.py:476
  6.2 1.4 %collective-permute-done.1.mid_own = f32[2,128,128]{2,1,0:T(8,128)S(1)} collective-permute-done((f32[2,128,128]{2,1,0:T(8,128)S(1)}, f32[2,128,128]{2,1,0:T(8,128)S(1)}, u32[]{:S(2)}, u32[]{:S(2)}) %collective-permute-start.1) | collective-permute-done | bytes 131104 | tf_op jit(solution)/shard_map/ppermute | solution.py:476
  7.6 1.7 %shard_map.55 = (bf16[768,1152]{1,0:T(8,128)(2,1)S(1)}, bf16[768,256]{1,0:T(8,128)(2,1)S(1)}) custom-call(s32[1,3,1,7]{3,2,1,0:T(1,128)} %bitcast.13, s32[1,1,2,3]{3,2,1,0:T(2,128)} %bitcast.12, f32[3,2,128,128]{3,2,1,0:T(8,128)} %bitcast.9, f32[3,7,128,128]{3,2,1,0:T(8,128)} %bitcast.10), custom_call_target="tpu_custom_call" | custom-call | tf_op jit(solution)/shard_map/pallas_call | solution.py:446
  9.8 1.4 %collective-permute-done.4.down_cross = f32[264,128]{1,0:T(8,128)S(1)} collective-permute-done((f32[264,128]{1,0:T(8,128)S(1)}, f32[264,128]{1,0:T(8,128)S(1)}, u32[]{:S(2)}, u32[]{:S(2)}) %collective-permute-start.4) | collective-permute-done | bytes 135200 | tf_op jit(solution)/shard_map/ppermute | solution.py:476
  11.2 1.4 %collective-permute-done.5.skewed = f32[264,128]{1,0:T(8,128)S(1)} collective-permute-done((f32[264,128]{1,0:T(8,128)S(1)}, f32[264,128]{1,0:T(8,128)S(1)}, u32[]{:S(2)}, u32[]{:S(2)}) %collective-permute-start.5) | collective-permute-done | bytes 135200 | tf_op jit(solution)/shard_map/ppermute | solution.py:476
  13.1 0.8 %collective-permute-start.6 = (f32[2,128,128]{2,1,0:T(8,128)S(1)}, f32[2,128,128]{2,1,0:T(8,128)S(1)}, u32[]{:S(2)}, u32[]{:S(2)}) collective-permute-start(f32[2,128,128]{2,1,0:T(8,128)S(1)} %slice.32), channel_id=1, source_target_pairs={{0,1},{1,0},{2,3},{3,2},{4,5},{5,4},{6,7},{7,6},{8,9},{9,8},{10,11... | collective-permute-start | bytes 393224 | tf_op jit(solution)/shard_map/ppermute | solution.py:476
  14.0 1.5 %shard_map.57.rest_0_.tall = bf16[1280,1152]{1,0:T(8,128)(2,1)S(1)} custom-call(bf16[768,1152]{1,0:T(8,128)(2,1)S(1)} %get-tuple-element.26.matrix, bf16[512,384]{1,0:T(8,128)(2,1)S(1)} %get-tuple-element.27.restrict), custom_call_target="tpu_custom_call" | custom-call | tf_op jit(solution)/shard_map/pallas_call | solution.py:446
  16.1 2.7 %collective-permute-done.8.cross = f32[3,128,128]{2,1,0:T(8,128)S(1)} collective-permute-done((f32[3,128,128]{2,1,0:T(8,128)S(1)}, f32[3,128,128]{2,1,0:T(8,128)S(1)}, u32[]{:S(2)}, u32[]{:S(2)}) %collective-permute-start.8) | collective-permute-done | bytes 196640 | tf_op jit(solution)/shard_map/ppermute | solution.py:476
  18.8 1.4 %collective-permute-start.9 = (f32[2,128,128]{2,1,0:T(8,128)S(1)}, f32[2,128,128]{2,1,0:T(8,128)S(1)}, u32[]{:S(2)}, u32[]{:S(2)}) collective-permute-start(f32[2,128,128]{2,1,0:T(8,128)S(1)} %get-tuple-element.38), channel_id=1, source_target_pairs={{0,16},{1,17},{2,18},{3,19},{4,20},{5,21},{6,22},{7,23},{8,24},{9,... | collective-permute-start | bytes 393224 | tf_op jit(solution)/shard_map/ppermute | solution.py:476
  20.5 4.3 %collective-permute-done.9.fixes = f32[2,128,128]{2,1,0:T(8,128)S(1)} collective-permute-done((f32[2,128,128]{2,1,0:T(8,128)S(1)}, f32[2,128,128]{2,1,0:T(8,128)S(1)}, u32[]{:S(2)}, u32[]{:S(2)}) %collective-permute-start.9) | collective-permute-done | bytes 131104 | tf_op jit(solution)/shard_map/ppermute | solution.py:476
  25.1 0.9 %collective-permute-start.12 = (f32[3,128,128]{2,1,0:T(8,128)S(1)}, f32[3,128,128]{2,1,0:T(8,128)S(1)}, u32[]{:S(2)}, u32[]{:S(2)}) collective-permute-start(f32[3,128,128]{2,1,0:T(8,128)S(1)} %shard_map.63.own.rest_0_), channel_id=1, source_target_pairs={{1,2},{2,1},{3,4},{4,3},{5,6},{6,5},{7,8},{8,7},{9,10},{10,9},{11,... | collective-permute-start | bytes 589832 | tf_op jit(solution)/shard_map/ppermute | solution.py:476
  26.0 1.8 %collective-permute-start.10 = (f32[2,128,128]{2,1,0:T(8,128)S(1)}, f32[2,128,128]{2,1,0:T(8,128)S(1)}, u32[]{:S(2)}, u32[]{:S(2)}) collective-permute-start(f32[2,128,128]{2,1,0:T(8,128)S(1)} %slice.34), channel_id=1, source_target_pairs={{0,1},{1,0},{2,3},{3,2},{4,5},{5,4},{6,7},{7,6},{8,9},{9,8},{10,11... | collective-permute-start | bytes 393224 | tf_op jit(solution)/shard_map/ppermute | solution.py:476
  27.9 1.2 %collective-permute-done.11.core_last = f32[1,128,128]{2,1,0:T(8,128)S(1)} collective-permute-done((f32[1,128,128]{2,1,0:T(8,128)S(1)}, f32[1,128,128]{2,1,0:T(8,128)S(1)}, u32[]{:S(2)}, u32[]{:S(2)}) %collective-permute-start.11) | collective-permute-done | bytes 65568 | tf_op jit(solution)/shard_map/ppermute | solution.py:476
  29.1 0.7 %shard_map.64.part = f32[640,128]{1,0:T(8,128)S(1)} custom-call(bf16[1280,1152]{1,0:T(8,128)(2,1)S(1)} %shard_map.57.rest_0_.tall, f32[3,128,128]{2,1,0:T(8,128)S(1)} %shard_map.63.own.rest_0_, f32[2,128,128]{2,1,0:T(8,128)S(1)} %collective-permute-done.10.core, f32[1,128,128]{2,1,0:T(8,128)S(1)} %collective-permute-done.11.core_last), custom_call_target="tpu_custom_call" | custom-call | tf_op jit(solution)/shard_map/pallas_call | solution.py:446
  29.8 1.1 %collective-permute-done.12.cross = f32[3,128,128]{2,1,0:T(8,128)S(1)} collective-permute-done((f32[3,128,128]{2,1,0:T(8,128)S(1)}, f32[3,128,128]{2,1,0:T(8,128)S(1)}, u32[]{:S(2)}, u32[]{:S(2)}) %collective-permute-start.12) | collective-permute-done | bytes 196640 | tf_op jit(solution)/shard_map/ppermute | solution.py:476
  31.6 2.2 %collective-permute-start.17 = (f32[3,128,128]{2,1,0:T(8,128)S(1)}, f32[3,128,128]{2,1,0:T(8,128)S(1)}, u32[]{:S(2)}, u32[]{:S(2)}) collective-permute-start(f32[3,128,128]{2,1,0:T(8,128)S(1)} %shard_map.65.own), channel_id=1, source_target_pairs={{1,2},{2,1},{3,4},{4,3},{5,6},{6,5},{7,8},{8,7},{9,10},{10,9},{11,... | collective-permute-start | bytes 589832 | tf_op jit(solution)/shard_map/ppermute | solution.py:476
  34.3 2.5 %collective-permute-done.14.mid_own = f32[2,128,128]{2,1,0:T(8,128)S(1)} collective-permute-done((f32[2,128,128]{2,1,0:T(8,128)S(1)}, f32[2,128,128]{2,1,0:T(8,128)S(1)}, u32[]{:S(2)}, u32[]{:S(2)}) %collective-permute-start.14) | collective-permute-done | bytes 131104 | tf_op jit(solution)/shard_map/ppermute | solution.py:476
  40.0 1.7 %collective-permute-start.19 = (f32[2,128,128]{2,1,0:T(8,128)S(1)}, f32[2,128,128]{2,1,0:T(8,128)S(1)}, u32[]{:S(2)}, u32[]{:S(2)}) collective-permute-start(f32[2,128,128]{2,1,0:T(8,128)S(1)} %slice.38), channel_id=1, source_target_pairs={{0,1},{1,0},{2,3},{3,2},{4,5},{5,4},{6,7},{7,6},{8,9},{9,8},{10,11... | collective-permute-start | bytes 393224 | tf_op jit(solution)/shard_map/ppermute | solution.py:476
  41.8 1.2 %collective-permute-done.20.core_last = f32[1,128,128]{2,1,0:T(8,128)S(1)} collective-permute-done((f32[1,128,128]{2,1,0:T(8,128)S(1)}, f32[1,128,128]{2,1,0:T(8,128)S(1)}, u32[]{:S(2)}, u32[]{:S(2)}) %collective-permute-start.20) | collective-permute-done | bytes 65568 | tf_op jit(solution)/shard_map/ppermute | solution.py:476
  43.4 2.2 %collective-permute-done.21.cross = f32[3,128,128]{2,1,0:T(8,128)S(1)} collective-permute-done((f32[3,128,128]{2,1,0:T(8,128)S(1)}, f32[3,128,128]{2,1,0:T(8,128)S(1)}, u32[]{:S(2)}, u32[]{:S(2)}) %collective-permute-start.21) | collective-permute-done | bytes 196640 | tf_op jit(solution)/shard_map/ppermute | solution.py:476
  46.4 5.6 %collective-permute-done.22.fixes = f32[2,128,128]{2,1,0:T(8,128)S(1)} collective-permute-done((f32[2,128,128]{2,1,0:T(8,128)S(1)}, f32[2,128,128]{2,1,0:T(8,128)S(1)}, u32[]{:S(2)}, u32[]{:S(2)}) %collective-permute-start.22) | collective-permute-done | bytes 131104 | tf_op jit(solution)/shard_map/ppermute | solution.py:476
  52.0 1.0 %shard_map.73 = f32[3,128,128]{2,1,0:T(8,128)} custom-call(f32[3,128,128]{2,1,0:T(8,128)S(1)} %shard_map.72.smooth, f32[2,128,128]{2,1,0:T(8,128)S(1)} %collective-permute-done.22.fixes, bf16[768,256]{1,0:T(8,128)(2,1)S(1)} %get-tuple-element.34.prolong), custom_call_target="tpu_custom_call" | custom-call | tf_op jit(solution)/shard_map/pallas_call | solution.py:446
  (50 shorter events, 8.6 us)
Async XLA Ops:
  1.4 6.2 %collective-permute-start.1 = (f32[2,128,128]{2,1,0:T(8,128)S(1)}, f32[2,128,128]{2,1,0:T(8,128)S(1)}, u32[]{:S(2)}, u32[]{:S(2)}) collective-permute-start(f32[2,128,128]{2,1,0:T(8,128)S(1)} %get-tuple-element.29.before), channel_id=1, source_target_pairs={{0,16},{1,17},{2,18},{3,19},{4,20},{5,21},{6,22},{7,23},{8,24},{9,... | collective-permute-start | bytes 393224 | tf_op jit(solution)/shard_map/ppermute | solution.py:476
  4.1 5.2 %collective-permute-start = (f32[3,128,128]{2,1,0:T(8,128)S(1)}, f32[3,128,128]{2,1,0:T(8,128)S(1)}, u32[]{:S(2)}, u32[]{:S(2)}) collective-permute-start(f32[3,128,128]{2,1,0:T(8,128)S(1)} %get-tuple-element.28.own.down_own), channel_id=1, source_target_pairs={{0,1},{1,0},{2,3},{3,2},{4,5},{5,4},{6,7},{7,6},{8,9},{9,8},{10,11... | collective-permute-start | bytes 589832 | tf_op jit(solution)/shard_map/ppermute | solution.py:476
  4.1 8.6 %collective-permute-start.3 = (f32[3,128,128]{2,1,0:T(8,128)S(1)}, f32[3,128,128]{2,1,0:T(8,128)S(1)}, u32[]{:S(2)}, u32[]{:S(2)}) collective-permute-start(f32[3,128,128]{2,1,0:T(8,128)S(1)} %get-tuple-element.28.own.down_own), channel_id=1, source_target_pairs={{1,2},{2,1},{3,4},{4,3},{5,6},{6,5},{7,8},{8,7},{9,10},{10,9},{11,... | collective-permute-start | bytes 589832 | tf_op jit(solution)/shard_map/ppermute | solution.py:476
  4.3 6.9 %collective-permute-start.4 = (f32[264,128]{1,0:T(8,128)S(1)}, f32[264,128]{1,0:T(8,128)S(1)}, u32[]{:S(2)}, u32[]{:S(2)}) collective-permute-start(f32[264,128]{1,0:T(8,128)S(1)} %get-tuple-element.31), channel_id=1, source_target_pairs={{2,3},{3,2},{4,5},{5,4},{6,7},{7,6},{8,9},{9,8},{10,11},{11,10},{1... | collective-permute-start | bytes 405512 | tf_op jit(solution)/shard_map/ppermute | solution.py:476
  5.7 6.9 %collective-permute-start.5 = (f32[264,128]{1,0:T(8,128)S(1)}, f32[264,128]{1,0:T(8,128)S(1)}, u32[]{:S(2)}, u32[]{:S(2)}) collective-permute-start(f32[264,128]{1,0:T(8,128)S(1)} %get-tuple-element.32), channel_id=1, source_target_pairs={{1,18},{2,17},{3,20},{4,19},{5,22},{6,21},{7,24},{8,23},{9,26},{10... | collective-permute-start | bytes 405512 | tf_op jit(solution)/shard_map/ppermute | solution.py:476
  7.6 1.7 %collective-permute-start.2 = (f32[2,128,128]{2,1,0:T(8,128)S(1)}, f32[2,128,128]{2,1,0:T(8,128)S(1)}, u32[]{:S(2)}, u32[]{:S(2)}) collective-permute-start(f32[2,128,128]{2,1,0:T(8,128)S(1)} %collective-permute-done.1.mid_own), channel_id=1, source_target_pairs={{0,1},{1,0},{2,3},{3,2},{4,5},{5,4},{6,7},{7,6},{8,9},{9,8},{10,11... | collective-permute-start | bytes 393224 | tf_op jit(solution)/shard_map/ppermute | solution.py:476
  13.0 5.7 %collective-permute-start.8 = (f32[3,128,128]{2,1,0:T(8,128)S(1)}, f32[3,128,128]{2,1,0:T(8,128)S(1)}, u32[]{:S(2)}, u32[]{:S(2)}) collective-permute-start(f32[3,128,128]{2,1,0:T(8,128)S(1)} %shard_map.59.own), channel_id=1, source_target_pairs={{1,2},{2,1},{3,4},{4,3},{5,6},{6,5},{7,8},{8,7},{9,10},{10,9},{11,... | collective-permute-start | bytes 589832 | tf_op jit(solution)/shard_map/ppermute | solution.py:476
  13.1 2.5 %collective-permute-start.6 = (f32[2,128,128]{2,1,0:T(8,128)S(1)}, f32[2,128,128]{2,1,0:T(8,128)S(1)}, u32[]{:S(2)}, u32[]{:S(2)}) collective-permute-start(f32[2,128,128]{2,1,0:T(8,128)S(1)} %slice.32), channel_id=1, source_target_pairs={{0,1},{1,0},{2,3},{3,2},{4,5},{5,4},{6,7},{7,6},{8,9},{9,8},{10,11... | collective-permute-start | bytes 393224 | tf_op jit(solution)/shard_map/ppermute | solution.py:476
  13.9 1.6 %collective-permute-start.7 = (f32[1,128,128]{2,1,0:T(8,128)S(1)}, f32[1,128,128]{2,1,0:T(8,128)S(1)}, u32[]{:S(2)}, u32[]{:S(2)}) collective-permute-start(f32[1,128,128]{2,1,0:T(8,128)S(1)} %slice.33), channel_id=1, source_target_pairs={{0,1},{1,0},{2,3},{3,2},{4,5},{5,4},{6,7},{7,6},{8,9},{9,8},{10,11... | collective-permute-start | bytes 196616 | tf_op jit(solution)/shard_map/ppermute | solution.py:476
  18.8 6.1 %collective-permute-start.9 = (f32[2,128,128]{2,1,0:T(8,128)S(1)}, f32[2,128,128]{2,1,0:T(8,128)S(1)}, u32[]{:S(2)}, u32[]{:S(2)}) collective-permute-start(f32[2,128,128]{2,1,0:T(8,128)S(1)} %get-tuple-element.38), channel_id=1, source_target_pairs={{0,16},{1,17},{2,18},{3,19},{4,20},{5,21},{6,22},{7,23},{8,24},{9,... | collective-permute-start | bytes 393224 | tf_op jit(solution)/shard_map/ppermute | solution.py:476
  25.1 5.7 %collective-permute-start.12 = (f32[3,128,128]{2,1,0:T(8,128)S(1)}, f32[3,128,128]{2,1,0:T(8,128)S(1)}, u32[]{:S(2)}, u32[]{:S(2)}) collective-permute-start(f32[3,128,128]{2,1,0:T(8,128)S(1)} %shard_map.63.own.rest_0_), channel_id=1, source_target_pairs={{1,2},{2,1},{3,4},{4,3},{5,6},{6,5},{7,8},{8,7},{9,10},{10,9},{11,... | collective-permute-start | bytes 589832 | tf_op jit(solution)/shard_map/ppermute | solution.py:476
  26.0 3.0 %collective-permute-start.10 = (f32[2,128,128]{2,1,0:T(8,128)S(1)}, f32[2,128,128]{2,1,0:T(8,128)S(1)}, u32[]{:S(2)}, u32[]{:S(2)}) collective-permute-start(f32[2,128,128]{2,1,0:T(8,128)S(1)} %slice.34), channel_id=1, source_target_pairs={{0,1},{1,0},{2,3},{3,2},{4,5},{5,4},{6,7},{7,6},{8,9},{9,8},{10,11... | collective-permute-start | bytes 393224 | tf_op jit(solution)/shard_map/ppermute | solution.py:476
  27.8 1.3 %collective-permute-start.11 = (f32[1,128,128]{2,1,0:T(8,128)S(1)}, f32[1,128,128]{2,1,0:T(8,128)S(1)}, u32[]{:S(2)}, u32[]{:S(2)}) collective-permute-start(f32[1,128,128]{2,1,0:T(8,128)S(1)} %slice.35), channel_id=1, source_target_pairs={{0,1},{1,0},{2,3},{3,2},{4,5},{5,4},{6,7},{7,6},{8,9},{9,8},{10,11... | collective-permute-start | bytes 196616 | tf_op jit(solution)/shard_map/ppermute | solution.py:476
  29.8 1.5 %copy-start = (f32[1,1,3,128,128]{4,3,2,1,0:T(8,128)S(1)}, f32[1,1,3,128,128]{4,3,2,1,0:T(8,128)}, u32[]{:S(2)}) copy-start(f32[1,1,3,128,128]{4,3,2,1,0:T(8,128)} %param.5) | copy-start | bytes 589828
  31.2 5.7 %collective-permute-start.14 = (f32[2,128,128]{2,1,0:T(8,128)S(1)}, f32[2,128,128]{2,1,0:T(8,128)S(1)}, u32[]{:S(2)}, u32[]{:S(2)}) collective-permute-start(f32[2,128,128]{2,1,0:T(8,128)S(1)} %get-tuple-element.39), channel_id=1, source_target_pairs={{0,16},{1,17},{2,18},{3,19},{4,20},{5,21},{6,22},{7,23},{8,24},{9,... | collective-permute-start | bytes 393224 | tf_op jit(solution)/shard_map/ppermute | solution.py:476
  31.6 7.9 %collective-permute-start.17 = (f32[3,128,128]{2,1,0:T(8,128)S(1)}, f32[3,128,128]{2,1,0:T(8,128)S(1)}, u32[]{:S(2)}, u32[]{:S(2)}) collective-permute-start(f32[3,128,128]{2,1,0:T(8,128)S(1)} %shard_map.65.own), channel_id=1, source_target_pairs={{1,2},{2,1},{3,4},{4,3},{5,6},{6,5},{7,8},{8,7},{9,10},{10,9},{11,... | collective-permute-start | bytes 589832 | tf_op jit(solution)/shard_map/ppermute | solution.py:476
  33.8 3.6 %collective-permute-start.13 = (f32[3,128,128]{2,1,0:T(8,128)S(1)}, f32[3,128,128]{2,1,0:T(8,128)S(1)}, u32[]{:S(2)}, u32[]{:S(2)}) collective-permute-start(f32[3,128,128]{2,1,0:T(8,128)S(1)} %shard_map.65.own), channel_id=1, source_target_pairs={{0,1},{1,0},{2,3},{3,2},{4,5},{5,4},{6,7},{7,6},{8,9},{9,8},{10,11... | collective-permute-start | bytes 589832 | tf_op jit(solution)/shard_map/ppermute | solution.py:476
  33.8 5.0 %collective-permute-start.18 = (f32[264,128]{1,0:T(8,128)S(1)}, f32[264,128]{1,0:T(8,128)S(1)}, u32[]{:S(2)}, u32[]{:S(2)}) collective-permute-start(f32[264,128]{1,0:T(8,128)S(1)} %get-tuple-element.41), channel_id=1, source_target_pairs={{1,18},{2,17},{3,20},{4,19},{5,22},{6,21},{7,24},{8,23},{9,26},{10... | collective-permute-start | bytes 405512 | tf_op jit(solution)/shard_map/ppermute | solution.py:476
  36.9 1.3 %collective-permute-start.16 = (f32[1,128,128]{2,1,0:T(8,128)S(1)}, f32[1,128,128]{2,1,0:T(8,128)S(1)}, u32[]{:S(2)}, u32[]{:S(2)}) collective-permute-start(f32[1,128,128]{2,1,0:T(8,128)S(1)} %get-tuple-element.47), channel_id=1, source_target_pairs={{0,1},{1,0},{2,3},{3,2},{4,5},{5,4},{6,7},{7,6},{8,9},{9,8},{10,11... | collective-permute-start | bytes 196616 | tf_op jit(solution)/shard_map/ppermute | solution.py:476
  36.9 1.4 %collective-permute-start.15 = (f32[1,128,128]{2,1,0:T(8,128)S(1)}, f32[1,128,128]{2,1,0:T(8,128)S(1)}, u32[]{:S(2)}, u32[]{:S(2)}) collective-permute-start(f32[1,128,128]{2,1,0:T(8,128)S(1)} %get-tuple-element.48), channel_id=1, source_target_pairs={{0,1},{1,0},{2,3},{3,2},{4,5},{5,4},{6,7},{7,6},{8,9},{9,8},{10,11... | collective-permute-start | bytes 196616 | tf_op jit(solution)/shard_map/ppermute | solution.py:476
  39.9 5.7 %collective-permute-start.21 = (f32[3,128,128]{2,1,0:T(8,128)S(1)}, f32[3,128,128]{2,1,0:T(8,128)S(1)}, u32[]{:S(2)}, u32[]{:S(2)}) collective-permute-start(f32[3,128,128]{2,1,0:T(8,128)S(1)} %shard_map.69.own), channel_id=1, source_target_pairs={{1,2},{2,1},{3,4},{4,3},{5,6},{6,5},{7,8},{8,7},{9,10},{10,9},{11,... | collective-permute-start | bytes 589832 | tf_op jit(solution)/shard_map/ppermute | solution.py:476
  40.0 3.0 %collective-permute-start.19 = (f32[2,128,128]{2,1,0:T(8,128)S(1)}, f32[2,128,128]{2,1,0:T(8,128)S(1)}, u32[]{:S(2)}, u32[]{:S(2)}) collective-permute-start(f32[2,128,128]{2,1,0:T(8,128)S(1)} %slice.38), channel_id=1, source_target_pairs={{0,1},{1,0},{2,3},{3,2},{4,5},{5,4},{6,7},{7,6},{8,9},{9,8},{10,11... | collective-permute-start | bytes 393224 | tf_op jit(solution)/shard_map/ppermute | solution.py:476
  41.7 1.3 %collective-permute-start.20 = (f32[1,128,128]{2,1,0:T(8,128)S(1)}, f32[1,128,128]{2,1,0:T(8,128)S(1)}, u32[]{:S(2)}, u32[]{:S(2)}) collective-permute-start(f32[1,128,128]{2,1,0:T(8,128)S(1)} %slice.39), channel_id=1, source_target_pairs={{0,1},{1,0},{2,3},{3,2},{4,5},{5,4},{6,7},{7,6},{8,9},{9,8},{10,11... | collective-permute-start | bytes 196616 | tf_op jit(solution)/shard_map/ppermute | solution.py:476
  45.6 6.4 %collective-permute-start.22 = (f32[2,128,128]{2,1,0:T(8,128)S(1)}, f32[2,128,128]{2,1,0:T(8,128)S(1)}, u32[]{:S(2)}, u32[]{:S(2)}) collective-permute-start(f32[2,128,128]{2,1,0:T(8,128)S(1)} %get-tuple-element.46), channel_id=1, source_target_pairs={{0,16},{1,17},{2,18},{3,19},{4,20},{5,21},{6,22},{7,23},{8,24},{9,... | collective-permute-start | bytes 393224 | tf_op jit(solution)/shard_map/ppermute | solution.py:476

commit v8 on v6

--- a/solution.py
+++ b/solution.py
@@ -149,7 +149,7 @@
     size = payload.shape[-1]
     slots = payload.shape[0]
     fetch_targets = pltpu.make_async_copy(targets_in.at[0, 0], targets, sems.at[0])
-    fetch_links = pltpu.make_async_copy(links_in, links, sems.at[1])
+    fetch_links = pltpu.make_async_copy(links_in.at[:, 0], links, sems.at[1])
     fetch_rhs = pltpu.make_async_copy(rhs_in, payload, sems.at[2])
     fetch_targets.start()
     fetch_links.start()
@@ -161,7 +161,7 @@
         fetch_links.wait()
         for s in range(slots):
             for k in range(2):
-                down = jnp.where(targets[0, s] == k, links[s, 0], 0.0)
+                down = jnp.where(targets[0, s] == k, links[s], 0.0)
                 high, low = split(down)
                 restrict[k * size:(k + 1) * size, s * size:(s + 1) * size] = high
                 restrict[(2 + k) * size:(3 + k) * size, s * size:(s + 1) * size] = low
@@ -174,10 +174,10 @@
     def _():
         fetch_targets.wait()
         fetch_links.wait()
-        payload[0] = links[0, 0]
-        payload[1] = links[2, 0]
+        payload[0] = links[0]
+        payload[1] = links[2]
         payload[2] = jnp.zeros_like(payload[2])
-        wide[:2 * size, :] = stacked(links[0, 0], links[2, 0])
+        wide[:2 * size, :] = stacked(links[0], links[2])
         wide[2 * size:, :] = jnp.zeros_like(wide[2 * size:, :])
         mids[...] = jnp.zeros_like(mids)
         skewed[...] = jnp.zeros_like(skewed)
@@ -481,7 +481,7 @@
         anywhere=3,
         scratch=[
             pltpu.SMEM(goals.shape[2:], goals.dtype),
-            pltpu.VMEM(links.shape, links.dtype),
+            pltpu.VMEM((slots, size, size), links.dtype),
             pltpu.SemaphoreType.DMA((3,)),
         ],
     )

time: 52.7 us -> 52.7 us (level)
  no operation moved by 1% of the time
where the time goes in v8:
time: 52.7 us; the launch traced here: 52.5 us
  waiting for transfers between devices  24.9 us (47%)
  starting transfers between devices  16.7 us (32%)
  Pallas kernels  10.6 us (20%)
    ppermute x23, waiting for transfers between devices, swaps(): lax.ppermute(x, ('lvl', 'row'), pairs)  24.9 us
    ppermute x23, starting transfers between devices, swaps(): lax.ppermute(x, ('lvl', 'row'), pairs)  16.7 us
    pallas_call x19, Pallas kernels, call(): pl.pallas_call(kernel, out_shape=[jax.ShapeDtypeStruct(shape, dtype) for...  10.6 us
  transfers between devices with their start and end apart: 23, of which 15 were waited for; matrix products, arithmetic and copies ran while one was open for 0% of the time, Pallas kernels for 13%

profile of v8, /device:TPU:0, one launch (start us, length us, event | category | flops | bytes accessed | tf_op | source)
XLA Modules:
  0.0 52.5 jit_solution(8030886817865251345)
XLA Ops:
  0.0 1.3 %shard_map.56 = (f32[2,128,128]{2,1,0:T(8,128)S(1)}, f32[264,128]{1,0:T(8,128)S(1)}, f32[3,128,128]{2,1,0:T(8,128)S(1)}, f32[264,128]{1,0:T(8,128)S(1)}, bf16[512,384]{1,0:T(8,128)(2,1)S(1)}) custom-call(s32[1,1,2,3]{3,2,1,0:T(2,128)} %bitcast.11, f32[3,128,128]{2,1,0:T(8,128)} %bitcast.6, f32[3,2,128,128]{3,2,1,0:T(8,128)} %bitcast.8), custom_call_target="tpu_custom_call" | custom-call | tf_op jit(solution)/shard_map/pallas_call | solution.py:436
  1.4 2.7 %collective-permute-start.1 = (f32[2,128,128]{2,1,0:T(8,128)S(1)}, f32[2,128,128]{2,1,0:T(8,128)S(1)}, u32[]{:S(2)}, u32[]{:S(2)}) collective-permute-start(f32[2,128,128]{2,1,0:T(8,128)S(1)} %get-tuple-element.25.before), channel_id=1, source_target_pairs={{0,16},{1,17},{2,18},{3,19},{4,20},{5,21},{6,22},{7,23},{8,24},{9,... | collective-permute-start | bytes 393224 | tf_op jit(solution)/shard_map/ppermute | solution.py:466
  4.2 1.4 %collective-permute-start.4 = (f32[264,128]{1,0:T(8,128)S(1)}, f32[264,128]{1,0:T(8,128)S(1)}, u32[]{:S(2)}, u32[]{:S(2)}) collective-permute-start(f32[264,128]{1,0:T(8,128)S(1)} %get-tuple-element.28), channel_id=1, source_target_pairs={{2,3},{3,2},{4,5},{5,4},{6,7},{7,6},{8,9},{9,8},{10,11},{11,10},{1... | collective-permute-start | bytes 405512 | tf_op jit(solution)/shard_map/ppermute | solution.py:466
  6.1 1.4 %collective-permute-done.1.mid_own = f32[2,128,128]{2,1,0:T(8,128)S(1)} collective-permute-done((f32[2,128,128]{2,1,0:T(8,128)S(1)}, f32[2,128,128]{2,1,0:T(8,128)S(1)}, u32[]{:S(2)}, u32[]{:S(2)}) %collective-permute-start.1) | collective-permute-done | bytes 131104 | tf_op jit(solution)/shard_map/ppermute | solution.py:466
  7.5 1.7 %shard_map.55 = (bf16[768,1152]{1,0:T(8,128)(2,1)S(1)}, bf16[768,256]{1,0:T(8,128)(2,1)S(1)}) custom-call(s32[1,3,1,7]{3,2,1,0:T(1,128)} %bitcast.13, s32[1,1,2,3]{3,2,1,0:T(2,128)} %bitcast.12, f32[3,2,128,128]{3,2,1,0:T(8,128)} %bitcast.9, f32[3,7,128,128]{3,2,1,0:T(8,128)} %bitcast.10), custom_call_target="tpu_custom_call" | custom-call | tf_op jit(solution)/shard_map/pallas_call | solution.py:436
  9.7 1.4 %collective-permute-done.4.down_cross = f32[264,128]{1,0:T(8,128)S(1)} collective-permute-done((f32[264,128]{1,0:T(8,128)S(1)}, f32[264,128]{1,0:T(8,128)S(1)}, u32[]{:S(2)}, u32[]{:S(2)}) %collective-permute-start.4) | collective-permute-done | bytes 135200 | tf_op jit(solution)/shard_map/ppermute | solution.py:466
  11.1 1.4 %collective-permute-done.5.skewed = f32[264,128]{1,0:T(8,128)S(1)} collective-permute-done((f32[264,128]{1,0:T(8,128)S(1)}, f32[264,128]{1,0:T(8,128)S(1)}, u32[]{:S(2)}, u32[]{:S(2)}) %collective-permute-start.5) | collective-permute-done | bytes 135200 | tf_op jit(solution)/shard_map/ppermute | solution.py:466
  13.0 0.8 %collective-permute-start.6 = (f32[2,128,128]{2,1,0:T(8,128)S(1)}, f32[2,128,128]{2,1,0:T(8,128)S(1)}, u32[]{:S(2)}, u32[]{:S(2)}) collective-permute-start(f32[2,128,128]{2,1,0:T(8,128)S(1)} %slice.32), channel_id=1, source_target_pairs={{0,1},{1,0},{2,3},{3,2},{4,5},{5,4},{6,7},{7,6},{8,9},{9,8},{10,11... | collective-permute-start | bytes 393224 | tf_op jit(solution)/shard_map/ppermute | solution.py:466
  14.0 1.6 %shard_map.57.rest_0_.tall = bf16[1280,1152]{1,0:T(8,128)(2,1)S(1)} custom-call(bf16[768,1152]{1,0:T(8,128)(2,1)S(1)} %get-tuple-element.22.matrix, bf16[512,384]{1,0:T(8,128)(2,1)S(1)} %get-tuple-element.23.restrict), custom_call_target="tpu_custom_call" | custom-call | tf_op jit(solution)/shard_map/pallas_call | solution.py:436
  16.0 2.6 %collective-permute-done.8.cross = f32[3,128,128]{2,1,0:T(8,128)S(1)} collective-permute-done((f32[3,128,128]{2,1,0:T(8,128)S(1)}, f32[3,128,128]{2,1,0:T(8,128)S(1)}, u32[]{:S(2)}, u32[]{:S(2)}) %collective-permute-start.8) | collective-permute-done | bytes 196640 | tf_op jit(solution)/shard_map/ppermute | solution.py:466
  18.7 1.3 %collective-permute-start.9 = (f32[2,128,128]{2,1,0:T(8,128)S(1)}, f32[2,128,128]{2,1,0:T(8,128)S(1)}, u32[]{:S(2)}, u32[]{:S(2)}) collective-permute-start(f32[2,128,128]{2,1,0:T(8,128)S(1)} %get-tuple-element.32), channel_id=1, source_target_pairs={{0,16},{1,17},{2,18},{3,19},{4,20},{5,21},{6,22},{7,23},{8,24},{9,... | collective-permute-start | bytes 393224 | tf_op jit(solution)/shard_map/ppermute | solution.py:466
  20.4 4.2 %collective-permute-done.9.fixes = f32[2,128,128]{2,1,0:T(8,128)S(1)} collective-permute-done((f32[2,128,128]{2,1,0:T(8,128)S(1)}, f32[2,128,128]{2,1,0:T(8,128)S(1)}, u32[]{:S(2)}, u32[]{:S(2)}) %collective-permute-start.9) | collective-permute-done | bytes 131104 | tf_op jit(solution)/shard_map/ppermute | solution.py:466
  24.9 1.0 %collective-permute-start.12 = (f32[3,128,128]{2,1,0:T(8,128)S(1)}, f32[3,128,128]{2,1,0:T(8,128)S(1)}, u32[]{:S(2)}, u32[]{:S(2)}) collective-permute-start(f32[3,128,128]{2,1,0:T(8,128)S(1)} %shard_map.63.own.rest_0_), channel_id=1, source_target_pairs={{1,2},{2,1},{3,4},{4,3},{5,6},{6,5},{7,8},{8,7},{9,10},{10,9},{11,... | collective-permute-start | bytes 589832 | tf_op jit(solution)/shard_map/ppermute | solution.py:466
  25.9 2.0 %collective-permute-start.10 = (f32[2,128,128]{2,1,0:T(8,128)S(1)}, f32[2,128,128]{2,1,0:T(8,128)S(1)}, u32[]{:S(2)}, u32[]{:S(2)}) collective-permute-start(f32[2,128,128]{2,1,0:T(8,128)S(1)} %slice.34), channel_id=1, source_target_pairs={{0,1},{1,0},{2,3},{3,2},{4,5},{5,4},{6,7},{7,6},{8,9},{9,8},{10,11... | collective-permute-start | bytes 393224 | tf_op jit(solution)/shard_map/ppermute | solution.py:466
  28.0 1.2 %collective-permute-done.11.core_last = f32[1,128,128]{2,1,0:T(8,128)S(1)} collective-permute-done((f32[1,128,128]{2,1,0:T(8,128)S(1)}, f32[1,128,128]{2,1,0:T(8,128)S(1)}, u32[]{:S(2)}, u32[]{:S(2)}) %collective-permute-start.11) | collective-permute-done | bytes 65568 | tf_op jit(solution)/shard_map/ppermute | solution.py:466
  29.2 0.7 %shard_map.64.part = f32[640,128]{1,0:T(8,128)S(1)} custom-call(bf16[1280,1152]{1,0:T(8,128)(2,1)S(1)} %shard_map.57.rest_0_.tall, f32[3,128,128]{2,1,0:T(8,128)S(1)} %shard_map.63.own.rest_0_, f32[2,128,128]{2,1,0:T(8,128)S(1)} %collective-permute-done.10.core, f32[1,128,128]{2,1,0:T(8,128)S(1)} %collective-permute-done.11.core_last), custom_call_target="tpu_custom_call" | custom-call | tf_op jit(solution)/shard_map/pallas_call | solution.py:436
  29.9 0.7 %collective-permute-done.12.cross = f32[3,128,128]{2,1,0:T(8,128)S(1)} collective-permute-done((f32[3,128,128]{2,1,0:T(8,128)S(1)}, f32[3,128,128]{2,1,0:T(8,128)S(1)}, u32[]{:S(2)}, u32[]{:S(2)}) %collective-permute-start.12) | collective-permute-done | bytes 196640 | tf_op jit(solution)/shard_map/ppermute | solution.py:466
  31.4 2.6 %collective-permute-start.17 = (f32[3,128,128]{2,1,0:T(8,128)S(1)}, f32[3,128,128]{2,1,0:T(8,128)S(1)}, u32[]{:S(2)}, u32[]{:S(2)}) collective-permute-start(f32[3,128,128]{2,1,0:T(8,128)S(1)} %shard_map.65.own), channel_id=1, source_target_pairs={{1,2},{2,1},{3,4},{4,3},{5,6},{6,5},{7,8},{8,7},{9,10},{10,9},{11,... | collective-permute-start | bytes 589832 | tf_op jit(solution)/shard_map/ppermute | solution.py:466
  34.4 2.5 %collective-permute-done.14.mid_own = f32[2,128,128]{2,1,0:T(8,128)S(1)} collective-permute-done((f32[2,128,128]{2,1,0:T(8,128)S(1)}, f32[2,128,128]{2,1,0:T(8,128)S(1)}, u32[]{:S(2)}, u32[]{:S(2)}) %collective-permute-start.14) | collective-permute-done | bytes 131104 | tf_op jit(solution)/shard_map/ppermute | solution.py:466
  39.8 2.0 %collective-permute-start.19 = (f32[2,128,128]{2,1,0:T(8,128)S(1)}, f32[2,128,128]{2,1,0:T(8,128)S(1)}, u32[]{:S(2)}, u32[]{:S(2)}) collective-permute-start(f32[2,128,128]{2,1,0:T(8,128)S(1)} %slice.38), channel_id=1, source_target_pairs={{0,1},{1,0},{2,3},{3,2},{4,5},{5,4},{6,7},{7,6},{8,9},{9,8},{10,11... | collective-permute-start | bytes 393224 | tf_op jit(solution)/shard_map/ppermute | solution.py:466
  41.9 1.2 %collective-permute-done.20.core_last = f32[1,128,128]{2,1,0:T(8,128)S(1)} collective-permute-done((f32[1,128,128]{2,1,0:T(8,128)S(1)}, f32[1,128,128]{2,1,0:T(8,128)S(1)}, u32[]{:S(2)}, u32[]{:S(2)}) %collective-permute-start.20) | collective-permute-done | bytes 65568 | tf_op jit(solution)/shard_map/ppermute | solution.py:466
  43.6 1.9 %collective-permute-done.21.cross = f32[3,128,128]{2,1,0:T(8,128)S(1)} collective-permute-done((f32[3,128,128]{2,1,0:T(8,128)S(1)}, f32[3,128,128]{2,1,0:T(8,128)S(1)}, u32[]{:S(2)}, u32[]{:S(2)}) %collective-permute-start.21) | collective-permute-done | bytes 196640 | tf_op jit(solution)/shard_map/ppermute | solution.py:466
  46.4 5.1 %collective-permute-done.22.fixes = f32[2,128,128]{2,1,0:T(8,128)S(1)} collective-permute-done((f32[2,128,128]{2,1,0:T(8,128)S(1)}, f32[2,128,128]{2,1,0:T(8,128)S(1)}, u32[]{:S(2)}, u32[]{:S(2)}) %collective-permute-start.22) | collective-permute-done | bytes 131104 | tf_op jit(solution)/shard_map/ppermute | solution.py:466
  51.5 0.9 %shard_map.73 = f32[3,128,128]{2,1,0:T(8,128)} custom-call(f32[3,128,128]{2,1,0:T(8,128)S(1)} %shard_map.72.smooth, f32[2,128,128]{2,1,0:T(8,128)S(1)} %collective-permute-done.22.fixes, bf16[768,256]{1,0:T(8,128)(2,1)S(1)} %get-tuple-element.30.prolong), custom_call_target="tpu_custom_call" | custom-call | tf_op jit(solution)/shard_map/pallas_call | solution.py:436
  (50 shorter events, 8.5 us)
Async XLA Ops:
  1.4 6.1 %collective-permute-start.1 = (f32[2,128,128]{2,1,0:T(8,128)S(1)}, f32[2,128,128]{2,1,0:T(8,128)S(1)}, u32[]{:S(2)}, u32[]{:S(2)}) collective-permute-start(f32[2,128,128]{2,1,0:T(8,128)S(1)} %get-tuple-element.25.before), channel_id=1, source_target_pairs={{0,16},{1,17},{2,18},{3,19},{4,20},{5,21},{6,22},{7,23},{8,24},{9,... | collective-permute-start | bytes 393224 | tf_op jit(solution)/shard_map/ppermute | solution.py:466
  4.0 5.2 %collective-permute-start = (f32[3,128,128]{2,1,0:T(8,128)S(1)}, f32[3,128,128]{2,1,0:T(8,128)S(1)}, u32[]{:S(2)}, u32[]{:S(2)}) collective-permute-start(f32[3,128,128]{2,1,0:T(8,128)S(1)} %get-tuple-element.24.own.down_own), channel_id=1, source_target_pairs={{0,1},{1,0},{2,3},{3,2},{4,5},{5,4},{6,7},{7,6},{8,9},{9,8},{10,11... | collective-permute-start | bytes 589832 | tf_op jit(solution)/shard_map/ppermute | solution.py:466
  4.0 8.6 %collective-permute-start.3 = (f32[3,128,128]{2,1,0:T(8,128)S(1)}, f32[3,128,128]{2,1,0:T(8,128)S(1)}, u32[]{:S(2)}, u32[]{:S(2)}) collective-permute-start(f32[3,128,128]{2,1,0:T(8,128)S(1)} %get-tuple-element.24.own.down_own), channel_id=1, source_target_pairs={{1,2},{2,1},{3,4},{4,3},{5,6},{6,5},{7,8},{8,7},{9,10},{10,9},{11,... | collective-permute-start | bytes 589832 | tf_op jit(solution)/shard_map/ppermute | solution.py:466
  4.2 6.9 %collective-permute-start.4 = (f32[264,128]{1,0:T(8,128)S(1)}, f32[264,128]{1,0:T(8,128)S(1)}, u32[]{:S(2)}, u32[]{:S(2)}) collective-permute-start(f32[264,128]{1,0:T(8,128)S(1)} %get-tuple-element.28), channel_id=1, source_target_pairs={{2,3},{3,2},{4,5},{5,4},{6,7},{7,6},{8,9},{9,8},{10,11},{11,10},{1... | collective-permute-start | bytes 405512 | tf_op jit(solution)/shard_map/ppermute | solution.py:466
  5.6 6.9 %collective-permute-start.5 = (f32[264,128]{1,0:T(8,128)S(1)}, f32[264,128]{1,0:T(8,128)S(1)}, u32[]{:S(2)}, u32[]{:S(2)}) collective-permute-start(f32[264,128]{1,0:T(8,128)S(1)} %get-tuple-element.29), channel_id=1, source_target_pairs={{1,18},{2,17},{3,20},{4,19},{5,22},{6,21},{7,24},{8,23},{9,26},{10... | collective-permute-start | bytes 405512 | tf_op jit(solution)/shard_map/ppermute | solution.py:466
  7.5 1.7 %collective-permute-start.2 = (f32[2,128,128]{2,1,0:T(8,128)S(1)}, f32[2,128,128]{2,1,0:T(8,128)S(1)}, u32[]{:S(2)}, u32[]{:S(2)}) collective-permute-start(f32[2,128,128]{2,1,0:T(8,128)S(1)} %collective-permute-done.1.mid_own), channel_id=1, source_target_pairs={{0,1},{1,0},{2,3},{3,2},{4,5},{5,4},{6,7},{7,6},{8,9},{9,8},{10,11... | collective-permute-start | bytes 393224 | tf_op jit(solution)/shard_map/ppermute | solution.py:466
  13.0 5.7 %collective-permute-start.8 = (f32[3,128,128]{2,1,0:T(8,128)S(1)}, f32[3,128,128]{2,1,0:T(8,128)S(1)}, u32[]{:S(2)}, u32[]{:S(2)}) collective-permute-start(f32[3,128,128]{2,1,0:T(8,128)S(1)} %shard_map.59.own), channel_id=1, source_target_pairs={{1,2},{2,1},{3,4},{4,3},{5,6},{6,5},{7,8},{8,7},{9,10},{10,9},{11,... | collective-permute-start | bytes 589832 | tf_op jit(solution)/shard_map/ppermute | solution.py:466
  13.0 2.5 %collective-permute-start.6 = (f32[2,128,128]{2,1,0:T(8,128)S(1)}, f32[2,128,128]{2,1,0:T(8,128)S(1)}, u32[]{:S(2)}, u32[]{:S(2)}) collective-permute-start(f32[2,128,128]{2,1,0:T(8,128)S(1)} %slice.32), channel_id=1, source_target_pairs={{0,1},{1,0},{2,3},{3,2},{4,5},{5,4},{6,7},{7,6},{8,9},{9,8},{10,11... | collective-permute-start | bytes 393224 | tf_op jit(solution)/shard_map/ppermute | solution.py:466
  13.9 1.7 %collective-permute-start.7 = (f32[1,128,128]{2,1,0:T(8,128)S(1)}, f32[1,128,128]{2,1,0:T(8,128)S(1)}, u32[]{:S(2)}, u32[]{:S(2)}) collective-permute-start(f32[1,128,128]{2,1,0:T(8,128)S(1)} %slice.33), channel_id=1, source_target_pairs={{0,1},{1,0},{2,3},{3,2},{4,5},{5,4},{6,7},{7,6},{8,9},{9,8},{10,11... | collective-permute-start | bytes 196616 | tf_op jit(solution)/shard_map/ppermute | solution.py:466
  18.7 5.9 %collective-permute-start.9 = (f32[2,128,128]{2,1,0:T(8,128)S(1)}, f32[2,128,128]{2,1,0:T(8,128)S(1)}, u32[]{:S(2)}, u32[]{:S(2)}) collective-permute-start(f32[2,128,128]{2,1,0:T(8,128)S(1)} %get-tuple-element.32), channel_id=1, source_target_pairs={{0,16},{1,17},{2,18},{3,19},{4,20},{5,21},{6,22},{7,23},{8,24},{9,... | collective-permute-start | bytes 393224 | tf_op jit(solution)/shard_map/ppermute | solution.py:466
  24.9 5.7 %collective-permute-start.12 = (f32[3,128,128]{2,1,0:T(8,128)S(1)}, f32[3,128,128]{2,1,0:T(8,128)S(1)}, u32[]{:S(2)}, u32[]{:S(2)}) collective-permute-start(f32[3,128,128]{2,1,0:T(8,128)S(1)} %shard_map.63.own.rest_0_), channel_id=1, source_target_pairs={{1,2},{2,1},{3,4},{4,3},{5,6},{6,5},{7,8},{8,7},{9,10},{10,9},{11,... | collective-permute-start | bytes 589832 | tf_op jit(solution)/shard_map/ppermute | solution.py:466
  25.9 3.3 %collective-permute-start.10 = (f32[2,128,128]{2,1,0:T(8,128)S(1)}, f32[2,128,128]{2,1,0:T(8,128)S(1)}, u32[]{:S(2)}, u32[]{:S(2)}) collective-permute-start(f32[2,128,128]{2,1,0:T(8,128)S(1)} %slice.34), channel_id=1, source_target_pairs={{0,1},{1,0},{2,3},{3,2},{4,5},{5,4},{6,7},{7,6},{8,9},{9,8},{10,11... | collective-permute-start | bytes 393224 | tf_op jit(solution)/shard_map/ppermute | solution.py:466
  27.9 1.3 %collective-permute-start.11 = (f32[1,128,128]{2,1,0:T(8,128)S(1)}, f32[1,128,128]{2,1,0:T(8,128)S(1)}, u32[]{:S(2)}, u32[]{:S(2)}) collective-permute-start(f32[1,128,128]{2,1,0:T(8,128)S(1)} %slice.35), channel_id=1, source_target_pairs={{0,1},{1,0},{2,3},{3,2},{4,5},{5,4},{6,7},{7,6},{8,9},{9,8},{10,11... | collective-permute-start | bytes 196616 | tf_op jit(solution)/shard_map/ppermute | solution.py:466
  29.9 1.1 %copy-start = (f32[1,1,3,128,128]{4,3,2,1,0:T(8,128)S(1)}, f32[1,1,3,128,128]{4,3,2,1,0:T(8,128)}, u32[]{:S(2)}) copy-start(f32[1,1,3,128,128]{4,3,2,1,0:T(8,128)} %param.5) | copy-start | bytes 589828
  30.9 6.1 %collective-permute-start.14 = (f32[2,128,128]{2,1,0:T(8,128)S(1)}, f32[2,128,128]{2,1,0:T(8,128)S(1)}, u32[]{:S(2)}, u32[]{:S(2)}) collective-permute-start(f32[2,128,128]{2,1,0:T(8,128)S(1)} %get-tuple-element.33), channel_id=1, source_target_pairs={{0,16},{1,17},{2,18},{3,19},{4,20},{5,21},{6,22},{7,23},{8,24},{9,... | collective-permute-start | bytes 393224 | tf_op jit(solution)/shard_map/ppermute | solution.py:466
  31.4 8.0 %collective-permute-start.17 = (f32[3,128,128]{2,1,0:T(8,128)S(1)}, f32[3,128,128]{2,1,0:T(8,128)S(1)}, u32[]{:S(2)}, u32[]{:S(2)}) collective-permute-start(f32[3,128,128]{2,1,0:T(8,128)S(1)} %shard_map.65.own), channel_id=1, source_target_pairs={{1,2},{2,1},{3,4},{4,3},{5,6},{6,5},{7,8},{8,7},{9,10},{10,9},{11,... | collective-permute-start | bytes 589832 | tf_op jit(solution)/shard_map/ppermute | solution.py:466
  33.9 3.6 %collective-permute-start.13 = (f32[3,128,128]{2,1,0:T(8,128)S(1)}, f32[3,128,128]{2,1,0:T(8,128)S(1)}, u32[]{:S(2)}, u32[]{:S(2)}) collective-permute-start(f32[3,128,128]{2,1,0:T(8,128)S(1)} %shard_map.65.own), channel_id=1, source_target_pairs={{0,1},{1,0},{2,3},{3,2},{4,5},{5,4},{6,7},{7,6},{8,9},{9,8},{10,11... | collective-permute-start | bytes 589832 | tf_op jit(solution)/shard_map/ppermute | solution.py:466
  33.9 5.0 %collective-permute-start.18 = (f32[264,128]{1,0:T(8,128)S(1)}, f32[264,128]{1,0:T(8,128)S(1)}, u32[]{:S(2)}, u32[]{:S(2)}) collective-permute-start(f32[264,128]{1,0:T(8,128)S(1)} %get-tuple-element.36), channel_id=1, source_target_pairs={{1,18},{2,17},{3,20},{4,19},{5,22},{6,21},{7,24},{8,23},{9,26},{10... | collective-permute-start | bytes 405512 | tf_op jit(solution)/shard_map/ppermute | solution.py:466
  37.0 1.3 %collective-permute-start.16 = (f32[1,128,128]{2,1,0:T(8,128)S(1)}, f32[1,128,128]{2,1,0:T(8,128)S(1)}, u32[]{:S(2)}, u32[]{:S(2)}) collective-permute-start(f32[1,128,128]{2,1,0:T(8,128)S(1)} %get-tuple-element.39), channel_id=1, source_target_pairs={{0,1},{1,0},{2,3},{3,2},{4,5},{5,4},{6,7},{7,6},{8,9},{9,8},{10,11... | collective-permute-start | bytes 196616 | tf_op jit(solution)/shard_map/ppermute | solution.py:466
  37.1 1.4 %collective-permute-start.15 = (f32[1,128,128]{2,1,0:T(8,128)S(1)}, f32[1,128,128]{2,1,0:T(8,128)S(1)}, u32[]{:S(2)}, u32[]{:S(2)}) collective-permute-start(f32[1,128,128]{2,1,0:T(8,128)S(1)} %get-tuple-element.40), channel_id=1, source_target_pairs={{0,1},{1,0},{2,3},{3,2},{4,5},{5,4},{6,7},{7,6},{8,9},{9,8},{10,11... | collective-permute-start | bytes 196616 | tf_op jit(solution)/shard_map/ppermute | solution.py:466
  39.7 5.7 %collective-permute-start.21 = (f32[3,128,128]{2,1,0:T(8,128)S(1)}, f32[3,128,128]{2,1,0:T(8,128)S(1)}, u32[]{:S(2)}, u32[]{:S(2)}) collective-permute-start(f32[3,128,128]{2,1,0:T(8,128)S(1)} %shard_map.69.own), channel_id=1, source_target_pairs={{1,2},{2,1},{3,4},{4,3},{5,6},{6,5},{7,8},{8,7},{9,10},{10,9},{11,... | collective-permute-start | bytes 589832 | tf_op jit(solution)/shard_map/ppermute | solution.py:466
  39.8 3.3 %collective-permute-start.19 = (f32[2,128,128]{2,1,0:T(8,128)S(1)}, f32[2,128,128]{2,1,0:T(8,128)S(1)}, u32[]{:S(2)}, u32[]{:S(2)}) collective-permute-start(f32[2,128,128]{2,1,0:T(8,128)S(1)} %slice.38), channel_id=1, source_target_pairs={{0,1},{1,0},{2,3},{3,2},{4,5},{5,4},{6,7},{7,6},{8,9},{9,8},{10,11... | collective-permute-start | bytes 393224 | tf_op jit(solution)/shard_map/ppermute | solution.py:466
  41.8 1.3 %collective-permute-start.20 = (f32[1,128,128]{2,1,0:T(8,128)S(1)}, f32[1,128,128]{2,1,0:T(8,128)S(1)}, u32[]{:S(2)}, u32[]{:S(2)}) collective-permute-start(f32[1,128,128]{2,1,0:T(8,128)S(1)} %slice.39), channel_id=1, source_target_pairs={{0,1},{1,0},{2,3},{3,2},{4,5},{5,4},{6,7},{7,6},{8,9},{9,8},{10,11... | collective-permute-start | bytes 196616 | tf_op jit(solution)/shard_map/ppermute | solution.py:466
  45.4 6.1 %collective-permute-start.22 = (f32[2,128,128]{2,1,0:T(8,128)S(1)}, f32[2,128,128]{2,1,0:T(8,128)S(1)}, u32[]{:S(2)}, u32[]{:S(2)}) collective-permute-start(f32[2,128,128]{2,1,0:T(8,128)S(1)} %get-tuple-element.38), channel_id=1, source_target_pairs={{0,16},{1,17},{2,18},{3,19},{4,20},{5,21},{6,22},{7,23},{8,24},{9,... | collective-permute-start | bytes 393224 | tf_op jit(solution)/shard_map/ppermute | solution.py:466
